TPU v7x, 256 devices: a whole 4x4x8 slice. The times are simulated.
256 devices in a mesh: dp: 32 (over x, z), tensor: 8 (over y, core).
Axes of the slice: x: 4, y: 4, z: 8, core: 2. Of those that a mesh axis runs over, the one named last changes fastest.
Arguments:
- cache_kv: bfloat16 [256, 2, 1024, 8, 128], P('dp', None, None, 'tensor'), may hold values from -6 to 6
- lengths: int32 [256], replicated, may hold values from 64 to 1024, as said below
- step_kv: bfloat16 [2, 256, 2, 8, 128], P(None, 'dp', None, 'tensor'), as said below
- queries: bfloat16 [2, 256, 64, 128], P(None, 'dp', 'tensor'), as said below
- parents: int32 [256], replicated, may hold values from 0 to 15, as said below
- finished: int32 [256], P('dp'), may hold values from 0 to 1, as said below
- reward_in: bfloat16 [8192, 4096], P('tensor', 'dp'), may hold values from -0.0625 to 0.0625
- reward_head: bfloat16 [4096], P('dp'), may hold values from -0.09375 to 0.09375
Outputs:
- first_out: bfloat16 [256, 8192], P('dp', 'tensor')
- second_out: bfloat16 [256, 8192], P('dp', 'tensor')
- scores: float32 [256], P('dp')
- new_cache: bfloat16 [256, 2, 1024, 8, 128], P('dp', None, None, 'tensor')
Inputs may be any that keep to these rules, and one draw needn't show every extreme that they name: `lengths`: multiples of 64; in every draw some beam has all 1024 positions valid. Beams b * 8 to b * 8 + 7 lie on one device; parents name beams of the same problem; on each device at most 4 slots name a parent of the other half of the problem, and in every draw some device has exactly 4. At most 4 finished beams among the 8 of one device; some device has exactly 4 in every draw. `step_kv`: new keys and values of order one. `queries`: queries of order one or larger.
All inputs are finite; a program needn't handle non-finite values.
Results may differ from a plain program's by a relative error of at most 0.0072.
Values may be sent and summed in bfloat16 or wider, within the bound.
No kernel may reach another device: no remote copies, remote signals or barrier semaphores. Data moves between devices by JAX's collectives and lax.ppermute only.
A program may use at most 128 MiB of HBM per device.

v0:
```python
import math

import jax
import jax.numpy as jnp
from jax import lax
from jax.sharding import PartitionSpec as P

D_GEN = 8192
FINISH_MOST = 4


def partner(array, axis, stride):
    return lax.ppermute(array, axis, [(i, i ^ 1 << stride) for i in range(lax.axis_size(axis))])


def attend(query_block, key_rows, value_rows, valid_length, extra_keys, extra_values):
    scaling = 1.0 / math.sqrt(query_block.shape[-1])
    logits = (
        jnp.einsum("bgrd,bcgd->bgrc", query_block, key_rows, preferred_element_type=jnp.float32)
        * scaling
    )
    places = lax.broadcasted_iota(jnp.int32, logits.shape, 3)
    logits = jnp.where(places < valid_length[:, None, None, None], logits, -1e30)
    extra_logits = (
        jnp.einsum("bgrd,begd->bgre", query_block, extra_keys, preferred_element_type=jnp.float32)
        * scaling
    )
    peak = jnp.maximum(
        jnp.max(logits, axis=3, keepdims=True), jnp.max(extra_logits, axis=3, keepdims=True)
    )
    cached = jnp.exp(logits - peak)
    fresh = jnp.exp(extra_logits - peak)
    total = jnp.sum(cached, axis=3, keepdims=True) + jnp.sum(fresh, axis=3, keepdims=True)
    weights = (cached / total).astype(jnp.bfloat16)
    extra_weights = (fresh / total).astype(jnp.bfloat16)
    mixed = jnp.einsum("bgrc,bcgd->bgrd", weights, value_rows, preferred_element_type=jnp.float32)
    mixed = mixed + jnp.einsum(
        "bgre,begd->bgrd", extra_weights, extra_values, preferred_element_type=jnp.float32
    )
    return mixed.astype(jnp.bfloat16).reshape(mixed.shape[0], -1)


def per_device(cache_kv, lengths, step_kv, queries, parents, finished, reward_in, reward_head):
    beam_count = cache_kv.shape[0]
    groups = cache_kv.shape[3]
    head_size = cache_kv.shape[4]
    per_group = queries.shape[2] // groups
    position = lax.axis_index("dp")
    own_half = position % 2
    start_row = position * beam_count
    own_lengths = lax.dynamic_slice_in_dim(lengths, start_row, beam_count)
    query_one = queries[0].reshape(beam_count, groups, per_group, head_size)
    query_two = queries[1].reshape(beam_count, groups, per_group, head_size)
    first_new = step_kv[0]
    first_out = attend(
        query_one,
        cache_kv[:, 0],
        cache_kv[:, 1],
        own_lengths,
        first_new[:, 0][:, None],
        first_new[:, 1][:, None],
    )
    my_parents = lax.dynamic_slice_in_dim(parents, start_row, beam_count)
    from_other = my_parents // beam_count != own_half
    local_index = my_parents % beam_count
    recv_cache, recv_new = partner((cache_kv, first_new), "dp", 0)
    source = jnp.where(from_other, beam_count + local_index, local_index)
    pooled_cache = jnp.concatenate([cache_kv, recv_cache], axis=0)[source]
    pooled_new = jnp.concatenate([first_new, recv_new], axis=0)[source]
    problem_start = position // 2 * (2 * beam_count)
    parent_lengths = lengths[problem_start + my_parents]
    second_new = step_kv[1]
    extra_keys = jnp.stack([pooled_new[:, 0], second_new[:, 0]], axis=1)
    extra_values = jnp.stack([pooled_new[:, 1], second_new[:, 1]], axis=1)
    second_out = attend(
        query_two, pooled_cache[:, 0], pooled_cache[:, 1], parent_lengths, extra_keys, extra_values
    )
    rows_wide = second_out.astype(jnp.float32)
    square_sums = lax.psum(jnp.sum(rows_wide * rows_wide, axis=1), "tensor")
    normed = (rows_wide * lax.rsqrt(square_sums / D_GEN + 1e-05)[:, None]).astype(jnp.bfloat16)
    finish_rank = jnp.cumsum(finished) - 1
    capacity = jnp.arange(FINISH_MOST, dtype=jnp.int32)
    packing = (finished[None, :] == 1) & (finish_rank[None, :] == capacity[:, None])
    packed = jnp.dot(
        packing.astype(jnp.bfloat16), normed, preferred_element_type=jnp.float32
    ).astype(jnp.bfloat16)
    partial_hidden = jnp.dot(
        lax.all_gather(packed, "dp", axis=0, tiled=True),
        reward_in,
        preferred_element_type=jnp.float32,
    )
    hidden = lax.psum(partial_hidden, "tensor")
    column_terms = jnp.sum(jax.nn.silu(hidden) * reward_head.astype(jnp.float32)[None, :], axis=1)
    slot_scores = lax.psum_scatter(column_terms, "dp", scatter_dimension=0, tiled=True)
    scores = jnp.sum(jnp.where(packing, slot_scores[:, None], 0.0), axis=0)
    return (first_out, second_out, scores, pooled_cache)


def solution(mesh):
    return jax.shard_map(
        per_device,
        mesh=mesh,
        in_specs=(
            P("dp", None, None, "tensor", None),
            P(),
            P(None, "dp", None, "tensor", None),
            P(None, "dp", "tensor", None),
            P(),
            P("dp"),
            P("tensor", "dp"),
            P("dp"),
        ),
        out_specs=(
            P("dp", "tensor"),
            P("dp", "tensor"),
            P("dp"),
            P("dp", None, None, "tensor", None),
        ),
        check_vma=False,
    )
```

profile of v0, /device:TPU:0, one launch (start us, length us, event | category | flops | bytes accessed | tf_op | source)
XLA Modules:
  0.0 328.7 jit_solution(2132949711843351735)
XLA Ops:
  7.5 0.7 slice_bitcast_fusion.14
  8.2 1.9 collective-permute-start.1
  10.1 0.8 reduce-window.8
  11.0 0.8 dynamic_slice.6
  11.7 0.8 compare_select_fusion.1
  12.5 0.8 fusion.38
  13.3 2.3 fusion.64
  15.9 0.7 broadcast_compare_fusion
  16.6 1.3 gather_fusion
  17.9 80.5 %collective-permute-done.1 = bf16[8,2,1,128]{3,1,0,2:T(2,128)(2,1)S(1)} collective-permute-done((bf16[8,2,1,128]{3,1,0,2:T(2,128)(2,1)S(1)}, bf16[8,2,1,128]{3,1,0,2:T(2,128)(2,1)S(1)}, u32[]{:S(2)}, u32[]{:S(2)}) %collective-permute-start.1) | collective-permute-done | bytes 4128 | tf_op jit(solution)/shard_map/ppermute | solution.py:13
  99.0 0.9 fusion.66
  99.9 7.4 %maximum_bitcast_fusion = bf16[16,2,1024,128]{3,2,1,0:T(8,128)(2,1)} fusion(bf16[8,2,1024,1,128]{4,2,1,0,3:T(8,128)(2,1)} %collective-permute-done, bf16[8,2,1024,1,128]{4,2,1,0,3:T(8,128)(2,1)} %bitcast.115), kind=kLoop, calls=%fused_computation.3 | loop fusion | flops 4194304 | bytes 16777216 | tf_op jit(solution)/shard_map/concatenate | solution.py:68
  107.3 6.5 %gather_fusion.1 = bf16[8,2,1024,128]{3,2,1,0:T(8,128)(2,1)} fusion(bf16[16,2,1024,128]{3,2,1,0:T(8,128)(2,1)} %maximum_bitcast_fusion, s32[1024]{0:T(1024)S(1)} %pad_clamp_fusion), kind=kCustom, calls=%fused_computation.1 | custom fusion | bytes 8388640 | tf_op jit(solution)/shard_map/gather | solution.py:68
  113.8 2.5 copy.57
  116.3 0.7 fusion.65
  117.5 0.7 copy-done.1
  118.8 14.2 %psum.14 = f32[8]{0:T(128)S(1)} all-reduce(f32[8]{0:T(128)S(1)} %get-tuple-element.40), channel_id=1, replica_groups=mesh['dp'=32,'tensor'=8] {'tensor'}, use_global_device_ids=true, to_apply=%region_8.9 | all-reduce | flops 8 | bytes 64 | tf_op jit(solution)/shard_map/psum | solution.py:79
  133.2 51.8 %all-gather = bf16[32,4,1024]{2,1,0:T(4,128)(2,1)S(1)} all-gather(bf16[1,4,1024]{2,1,0:T(4,128)(2,1)S(1)} %fusion.28), channel_id=1, replica_groups=mesh['dp'=32,'tensor'=8] {'dp'}, dimensions={0}, use_global_device_ids=true | all-gather | bytes 270336 | tf_op jit(solution)/shard_map/all_gather | solution.py:88
  185.1 0.8 fusion.67
  186.0 2.0 fusion.25
  189.9 4.6 %copy.47 = bf16[8,2,1024,1,128]{4,2,3,1,0:T(8,128)(2,1)} copy(bf16[8,2,1024,1,128]{4,2,0,3,1:T(8,128)(2,1)} %bitcast.113) | data formatting | bytes 8388608
  194.5 50.7 %all-reduce.3.cloned.1.call-done = f32[128,128]{1,0:T(8,128)} async-done(((f32[128,128]{1,0:T(8,128)}), f32[128,128]{1,0:T(8,128)}) %all-reduce.3.cloned.1.call-update) | async-done | bytes 65552 | tf_op jit(solution)/shard_map/psum | solution.py:92
  245.2 1.0 multiply_reduce_fusion
  246.1 75.1 %all-reduce = f32[128]{0:T(128)S(1)} all-reduce(f32[128]{0:T(128)S(1)} %multiply_reduce_fusion), channel_id=2, replica_groups=mesh['dp'=32,'tensor'=8] {'dp'}, use_global_device_ids=true, to_apply=%region_11.12.clone | all-reduce | flops 128 | bytes 1024
  (40 shorter events, 4.3 us)
Async XLA Ops:
  7.2 177.9 %copy-start = (bf16[1024,128]{1,0:T(8,128)(2,1)S(1)}, bf16[1024,128]{1,0:T(8,128)(2,1)}, u32[]{:S(2)}) copy-start(bf16[1024,128]{1,0:T(8,128)(2,1)} %param.14) | copy-start | bytes 786436
  7.2 238.0 %all-reduce.3.cloned.1.call-start = ((), (), s32[]{:S(2)}) async-start(), calls=%async_computation | async-start | bytes 131072 | tf_op jit(solution)/shard_map/psum | solution.py:92
  7.2 92.7 %collective-permute-start = (bf16[8,2,1024,1,128]{4,2,1,0,3:T(8,128)(2,1)}, bf16[8,2,1024,1,128]{4,2,1,0,3:T(8,128)(2,1)}, u32[]{:S(2)}, u32[]{:S(2)}) collective-permute-start(bf16[8,2,1024,1,128]{4,2,1,0,3:T(8,128)(2,1)} %bitcast.114), channel_id=1, source_target_pairs={{0,8},{8,0},{16,24},{24,16},{32,40},{40,32},{48,56},{56,48},{64,72... | collective-permute-start | bytes 12582920 | tf_op jit(solution)/shard_map/ppermute | solution.py:13
  8.2 90.2 %collective-permute-start.1 = (bf16[8,2,1,128]{3,1,0,2:T(2,128)(2,1)S(1)}, bf16[8,2,1,128]{3,1,0,2:T(2,128)(2,1)S(1)}, u32[]{:S(2)}, u32[]{:S(2)}) collective-permute-start(bf16[8,2,1,128]{3,1,0,2:T(2,128)(2,1)S(1)} %get-tuple-element.27), channel_id=1, source_target_pairs={{0,8},{8,0},{16,24},{24,16},{32,40},{40,32},{48,56},{56,48},{64,72... | collective-permute-start | bytes 12296 | tf_op jit(solution)/shard_map/ppermute | solution.py:13
  113.8 2.5 copy-start.3
  116.3 1.9 copy-start.1
  117.0 71.0 %copy-start.4 = (bf16[128]{0:T(256)(128)(2,1)S(1)}, bf16[128]{0:T(256)(128)(2,1)}, u32[]{:S(2)}) copy-start(bf16[128]{0:T(256)(128)(2,1)} %param.15) | copy-start | bytes 772
  117.1 71.6 %copy-start.5 = (u32[256]{0:T(256)S(1)}, u32[256]{0:T(256)}, u32[]{:S(2)}) copy-start(u32[256]{0:T(256)} %constant.94) | copy-start | bytes 3076
  118.8 75.7 %copy-start.2 = (bf16[1,8,8,128]{3,1,2,0:T(8,128)(2,1)}, bf16[1,8,8,128]{3,1,2,0:T(8,128)(2,1)S(1)}, u32[]{:S(2)}) copy-start(bf16[1,8,8,128]{3,1,2,0:T(8,128)(2,1)S(1)} %copy.58) | copy-start | bytes 49156
Sparse Core Ops, SparseCore 0:
  186.1 59.0 all-reduce.2
where the time goes:
time: 329 us
  blocking collectives  141 us (43%)
  waiting for transfers between devices  131 us (40%)
  local copies, waits for them, and re-layouts  19 us (6%)
  between operations  14.8 us (4%)
  other arithmetic  11.7 us (4%)
  matrix products  8.55 us (3%)
    ppermute x2, waiting for transfers between devices, partner(): lax.ppermute(array, axis, [(i, i ^ 1 << stride) for i in range(lax.axis_s...  80.5 us
    unnamed x1, blocking collectives  75.1 us
    all_gather x1, blocking collectives, per_device(): lax.all_gather(packed, 'dp', axis=0, tiled=True)  51.8 us
    psum x1, waiting for transfers between devices, per_device(): hidden = lax.psum(partial_hidden, 'tensor')  50.7 us
    psum x1, blocking collectives, per_device(): square_sums = lax.psum(jnp.sum(rows_wide * rows_wide, axis=1), 'tensor')  14.2 us
    gather x2, local copies, waits for them, and re-layouts, per_device(): pooled_cache = jnp.concatenate([cache_kv, recv_cache], axis=0)[source]  8.97 us
    concatenate x1, other arithmetic, per_device(): pooled_cache = jnp.concatenate([cache_kv, recv_cache], axis=0)[source]  7.41 us
    unnamed x18, local copies, waits for them, and re-layouts  6.7 us
  transfers between devices with their start and end apart: 3, of which 2 were waited for; matrix products, arithmetic and copies ran while one was open for 5% of the time, Pallas kernels for 0%

commit v1 on v0

v1 whole, which is shorter than its diff:
```python
import functools
import math

import jax
import jax.numpy as jnp
from jax import lax
from jax.experimental import pallas as pl
from jax.experimental.pallas import tpu as pltpu
from jax.sharding import PartitionSpec as P

D_GEN = 8192
MOST = 4
BD = 8
CACHE = 1024
HD = 128
GH = 8
F32 = jnp.float32
BF16 = jnp.bfloat16
VM = pltpu.VMEM
SM = pltpu.SMEM
HB = pltpu.HBM


def spec(space):
    return pl.BlockSpec(memory_space=space)


def needed(par_ref, slots_at, half):
    flags = []
    for b in range(BD):
        want = half * BD + b
        hit = par_ref[slots_at] == want
        for j in range(1, BD):
            hit = hit | (par_ref[slots_at + j] == want)
        flags.append(hit)
    return flags


def pack_kernel(par_ref, cache_ref, w_ref, head_ref, packed_ref, wext_ref, hscr, sems, wsem, hsem):
    me = lax.axis_index("dp")
    half = lax.rem(me, 2)
    start = (me - half) * BD + (1 - half) * BD
    flags = needed(par_ref, start, half)
    rank = jnp.int32(0)
    for b in range(BD):
        slot = jnp.minimum(rank, MOST - 1)

        @pl.when(flags[b] & (rank < MOST))
        def _():
            pltpu.make_async_copy(cache_ref.at[b], packed_ref.at[slot], sems.at[slot]).start()

        rank = rank + flags[b].astype(jnp.int32)
    rows = w_ref.shape[0]
    wcopy = pltpu.make_async_copy(w_ref, wext_ref.at[pl.ds(0, rows)], wsem)
    wcopy.start()
    hscr[...] = jnp.broadcast_to(head_ref[...].astype(F32), (16, HD)).astype(BF16)
    hcopy = pltpu.make_async_copy(hscr, wext_ref.at[pl.ds(rows, 16)], hsem)
    hcopy.start()
    hcopy.wait()
    wcopy.wait()
    for r in range(MOST):

        @pl.when(r < rank)
        def _():
            pltpu.make_async_copy(cache_ref.at[0], packed_ref.at[r], sems.at[r]).wait()


def attend_kernel(
    par_ref, len_ref, fino_ref, finr_ref, cache_ref, qo_ref, qr_ref, kvo_ref, kvr_ref,
    first_ref, own_ref, other_ref, rows_ref, newc_ref,
    buf, q1s, e1s, v1s, pcol, fscr, acc, rscr, pk, insem, outsem,
):
    me = lax.axis_index("dp")
    half = lax.rem(me, 2)
    pair = (me - half) * BD
    mine = pair + half * BD
    theirs = pair + (1 - half) * BD
    scaling = 1.0 / math.sqrt(HD)
    for b in range(BD):
        pltpu.make_async_copy(cache_ref.at[b], buf.at[b], insem.at[b]).start()
    own_local = []
    q1s[...] = jnp.zeros_like(q1s)
    for b in range(BD):
        q1s[b, 0:GH, :] = qo_ref[0, b]
    e1s[...] = jnp.full_like(e1s, -1e30)
    v1s[...] = jnp.zeros_like(v1s)
    for s in range(2 * BD):
        at = (mine if s < BD else theirs) + s % BD
        parent = par_ref[at]
        here = (parent >= half * BD) & (parent < half * BD + BD)
        local = jnp.where(here, parent - half * BD, -1)
        if s < BD:
            own_local.append(local)
        rows = pl.ds(s * GH, GH)
        pcol[rows, :] = jnp.full((GH, HD), local, jnp.int32)
        q = (qo_ref if s < BD else qr_ref)[1, s % BD].astype(F32)
        kv = kvo_ref if s < BD else kvr_ref
        k1 = kv[1, s % BD, 0:1, :].astype(F32)
        e1s[rows, :] = jnp.broadcast_to(jnp.sum(q * k1, axis=1, keepdims=True) * scaling, (GH, HD))
        v1s[rows, :] = jnp.broadcast_to(kv[1, s % BD, 1:2, :].astype(F32), (GH, HD))
    q2 = jnp.concatenate(
        [qo_ref[1].reshape(BD * GH, HD), qr_ref[1].reshape(BD * GH, HD)], axis=0
    )
    acc[...] = jnp.zeros_like(acc)
    for b in range(BD):
        pltpu.make_async_copy(cache_ref.at[b], buf.at[b], insem.at[b]).wait()
        for s in range(BD):

            @pl.when(own_local[s] == b)
            def _():
                pltpu.make_async_copy(buf.at[b], newc_ref.at[s], outsem.at[s]).start()

        length = len_ref[mine + b]
        q = jnp.concatenate([q2, q1s[b]], axis=0)
        logits = lax.dot_general(
            q, buf[b, 0], (((1,), (1,)), ((), ())), preferred_element_type=F32
        ) * scaling
        places = lax.broadcasted_iota(jnp.int32, logits.shape, 1)
        logits = jnp.where(places < length, logits, -1e30)
        k0 = kvo_ref[0, b, 0:1, :].astype(F32)
        v0 = kvo_ref[0, b, 1:2, :].astype(F32)
        e0 = jnp.sum(q.astype(F32) * k0, axis=1, keepdims=True) * scaling
        e1 = e1s[:, 0:1]
        peak = jnp.maximum(jnp.maximum(jnp.max(logits, axis=1, keepdims=True), e0), e1)
        p = jnp.exp(logits - peak)
        p0 = jnp.exp(e0 - peak)
        p1 = jnp.exp(e1 - peak)
        inv = 1.0 / (jnp.sum(p, axis=1, keepdims=True) + p0 + p1)
        mixed = jnp.dot((p * inv).astype(BF16), buf[b, 1], preferred_element_type=F32)
        mixed = mixed + (p0 * inv).astype(BF16).astype(F32) * v0
        mixed = mixed + (p1 * inv).astype(BF16).astype(F32) * v1s[...]
        fscr[b * GH : (b + 1) * GH, :] = mixed[2 * BD * GH : 2 * BD * GH + GH]
        acc[...] = jnp.where(pcol[...] == b, mixed[: 2 * BD * GH], acc[...])
    for h in range(GH):
        lanes = slice(h * HD, (h + 1) * HD)
        first_ref[:, lanes] = fscr[pl.ds(h, BD, stride=GH), :].astype(BF16)
        rscr[0:BD, lanes] = acc[pl.ds(h, BD, stride=GH), :].astype(BF16).astype(F32)
        rscr[BD : 2 * BD, lanes] = acc[pl.ds(BD * GH + h, BD, stride=GH), :].astype(BF16).astype(F32)
    own_ref[...] = rscr[0:BD, :].astype(BF16)
    other_ref[...] = rscr[BD : 2 * BD, :].astype(BF16)
    pk[...] = jnp.zeros_like(pk)
    rank = jnp.int32(0)
    for j in range(2 * BD):
        owned = half == j // BD
        flag = jnp.where(owned, fino_ref[j % BD], finr_ref[j % BD]) == 1
        source = jnp.where(owned, 0, BD) + j % BD

        @pl.when(flag)
        def _():
            pk[pl.ds(jnp.minimum(rank, BD - 1), 1), :] = rscr[pl.ds(source, 1), :]

        rank = rank + flag.astype(jnp.int32)
    packed = pk[...].astype(BF16)
    for k in range(rows_ref.shape[0]):
        rows_ref[k] = packed
    for s in range(BD):

        @pl.when(own_local[s] >= 0)
        def _():
            pltpu.make_async_copy(buf.at[0], newc_ref.at[s], outsem.at[s]).wait()


def place_kernel(par_ref, recv_ref, into_ref, newc_ref, sems):
    del into_ref
    me = lax.axis_index("dp")
    half = lax.rem(me, 2)
    mine = (me - half) * BD + half * BD
    flags = needed(par_ref, mine, 1 - half)
    ranks = []
    rank = jnp.int32(0)
    for b in range(BD):
        ranks.append(rank)
        rank = rank + flags[b].astype(jnp.int32)
    crossing = []
    for s in range(BD):
        parent = par_ref[mine + s]
        local = parent - (1 - half) * BD
        cross = (local >= 0) & (local < BD)
        slot = jnp.int32(0)
        for b in range(BD):
            slot = jnp.where(local == b, ranks[b], slot)
        slot = jnp.minimum(slot, MOST - 1)
        crossing.append(cross)

        @pl.when(cross)
        def _():
            pltpu.make_async_copy(recv_ref.at[slot], newc_ref.at[s], sems.at[s]).start()

    for s in range(BD):

        @pl.when(crossing[s])
        def _():
            pltpu.make_async_copy(recv_ref.at[0], newc_ref.at[s], sems.at[s]).wait()


def hidden_kernel(rows_ref, w0, w1, w2, w3, out_ref):
    depth = w0.shape[0] - 16
    rows = jnp.concatenate(
        [
            rows_ref[2 * p].astype(F32) + rows_ref[2 * p + 1].astype(F32)
            for p in range(rows_ref.shape[0] // 2)
        ],
        axis=0,
    )
    narrow = rows.astype(BF16)
    parts = [
        jnp.dot(narrow, w[0:depth, :], preferred_element_type=F32) for w in (w0, w1, w2, w3)
    ]
    squares = jnp.sum(rows * rows, axis=1, keepdims=True)
    parts.append(jnp.broadcast_to(squares, (rows.shape[0], HD)))
    for k in range(out_ref.shape[0]):
        for i, part in enumerate(parts):
            out_ref[k, :, i * HD : (i + 1) * HD] = part


def score_kernel(hid_ref, w0, w1, w2, w3, out_ref):
    depth = w0.shape[0] - 16
    total = hid_ref[0]
    for k in range(1, hid_ref.shape[0]):
        total = total + hid_ref[k]
    factor = lax.rsqrt(total[:, 4 * HD : 4 * HD + 1] / D_GEN + 1e-05)
    sums = jnp.zeros((total.shape[0], 1), F32)
    for i, w in enumerate((w0, w1, w2, w3)):
        head = w[depth : depth + 16, :].astype(F32)[0:1, :]
        v = total[:, i * HD : (i + 1) * HD] * factor
        sums = sums + jnp.sum(v / (1.0 + jnp.exp(-v)) * head, axis=1, keepdims=True)
    wide = jnp.broadcast_to(sums, (total.shape[0], HD))
    for z in range(out_ref.shape[0]):
        p = z // 2
        out_ref[z] = wide[p * BD : (p + 1) * BD]


def final_kernel(fino_ref, finr_ref, part_ref, out_ref, scr):
    me = lax.axis_index("dp")
    half = lax.rem(me, 2)
    total = part_ref[0]
    for k in range(1, part_ref.shape[0]):
        total = total + part_ref[k]
    scr[...] = total
    rank = jnp.int32(0)
    for j in range(BD):
        rank = rank + jnp.where(half == 1, (finr_ref[j] == 1).astype(jnp.int32), 0)
    for s in range(BD):
        flag = fino_ref[s] == 1
        value = scr[pl.ds(jnp.minimum(rank, BD - 1), 1), :][0, 0]
        out_ref[s] = jnp.where(flag, value, 0.0)
        rank = rank + flag.astype(jnp.int32)


def call(kernel, outs, ins, out_specs, scratch=(), aliases=None, cost=None, limit=None):
    return functools.partial(
        pl.pallas_call,
        kernel,
        out_shape=outs,
        in_specs=[spec(s) for s in ins],
        out_specs=[spec(s) for s in out_specs],
        scratch_shapes=list(scratch),
        input_output_aliases=aliases or {},
        compiler_params=pltpu.CompilerParams(vmem_limit_bytes=limit or 40 * 1024 * 1024),
        cost_estimate=pl.CostEstimate(flops=cost or 1000000, bytes_accessed=cost or 1000000, transcendentals=0),
    )()


def shape(dims, dtype):
    return jax.ShapeDtypeStruct(dims, dtype)


def swap(array):
    return lax.ppermute(array, "dp", [(i, i ^ 1) for i in range(lax.axis_size("dp"))])


def per_device(nx, nz, cache_kv, lengths, step_kv, queries, parents, finished, reward_in, reward_head):
    ndp = nx * nz
    zgroups = [[a * nz + b for b in range(nz)] for a in range(nx)]
    nt = lax.axis_size("tensor")
    cache = cache_kv.reshape(BD, 2, CACHE, HD)
    kv = step_kv.reshape(2, BD, 2, HD)
    depth = reward_in.shape[0]
    recv_q = swap(queries)
    recv_kv = swap(kv)
    recv_fin = swap(finished)
    packed, wext = call(
        pack_kernel,
        [shape((MOST, 2, CACHE, HD), BF16), shape((depth + 16, HD), BF16)],
        [SM, HB, HB, VM],
        [HB, HB],
        [VM((16, HD), BF16), pltpu.SemaphoreType.DMA((MOST,)), pltpu.SemaphoreType.DMA, pltpu.SemaphoreType.DMA],
    )(parents, cache, reward_in, reward_head.reshape(1, HD))
    recv_cache = swap(packed)
    others = [
        lax.ppermute(wext, "dp", [(i, (i + nz * k) % ndp) for i in range(ndp)]) for k in range(1, nx)
    ]
    first_out, own_out, other_out, rows, newc = call(
        attend_kernel,
        [
            shape((BD, GH * HD), BF16),
            shape((BD, GH * HD), BF16),
            shape((BD, GH * HD), BF16),
            shape((nz, BD, GH * HD), BF16),
            shape((BD, 2, CACHE, HD), BF16),
        ],
        [SM, SM, SM, SM, HB, VM, VM, VM, VM],
        [VM, VM, VM, VM, HB],
        [
            VM((BD, 2, CACHE, HD), BF16),
            VM((BD, 2 * GH, HD), BF16),
            VM((2 * BD * GH + 16, HD), F32),
            VM((2 * BD * GH + 16, HD), F32),
            VM((2 * BD * GH, HD), jnp.int32),
            VM((BD * GH, HD), F32),
            VM((2 * BD * GH, HD), F32),
            VM((2 * BD, GH * HD), F32),
            VM((BD, GH * HD), F32),
            pltpu.SemaphoreType.DMA((BD,)),
            pltpu.SemaphoreType.DMA((BD,)),
        ],
        cost=20000000,
    )(parents, lengths, finished, recv_fin, cache, queries, recv_q, kv, recv_kv)
    second_out = own_out + swap(other_out)
    gathered = lax.all_to_all(rows, "dp", 0, 0, axis_index_groups=zgroups, tiled=True)
    (partial,) = call(
        hidden_kernel, [shape((nt, nz // 2 * BD, 5 * HD), F32)], [VM] * 5, [VM]
    )(gathered, wext, *others)
    partials = lax.all_to_all(partial, "tensor", 0, 0, tiled=True)
    (sums,) = call(score_kernel, [shape((nz, BD, HD), F32)], [VM] * 5, [VM])(partials, wext, *others)
    sums = lax.all_to_all(sums, "dp", 0, 0, axis_index_groups=zgroups, tiled=True)
    (scores,) = call(
        final_kernel, [shape((BD,), F32)], [SM, SM, VM], [SM], [VM((BD, HD), F32)]
    )(finished, recv_fin, sums)
    (new_cache,) = call(
        place_kernel,
        [shape((BD, 2, CACHE, HD), BF16)],
        [SM, HB, HB],
        [HB],
        [pltpu.SemaphoreType.DMA((BD,))],
        aliases={2: 0},
    )(parents, recv_cache, newc)
    return (first_out, second_out, scores, new_cache.reshape(cache_kv.shape))


def solution(mesh):
    ndp = mesh.shape["dp"]
    nx = 4
    return jax.shard_map(
        functools.partial(per_device, nx, ndp // nx),
        mesh=mesh,
        in_specs=(
            P("dp", None, None, "tensor", None),
            P(),
            P(None, "dp", None, "tensor", None),
            P(None, "dp", "tensor", None),
            P(),
            P("dp"),
            P("tensor", "dp"),
            P("dp"),
        ),
        out_specs=(
            P("dp", "tensor"),
            P("dp", "tensor"),
            P("dp"),
            P("dp", None, None, "tensor", None),
        ),
        check_vma=False,
    )
```

time: 329 us -> 117 us (0.36)
  the two profiles are of different devices: /device:TPU:0 before, /device:TPU:2 now
where the time goes in v1:
time: 117 us; the launch traced here: 116 us
  waiting for transfers between devices  48.5 us (41%)
  blocking collectives  32.4 us (28%)
  starting transfers between devices  16.7 us (14%)
  Pallas kernels  12.9 us (11%)
  local copies, waits for them, and re-layouts  4.5 us (4%)
    ppermute x5, waiting for transfers between devices, swap(): lax.ppermute(array, 'dp', [(i, i ^ 1) for i in range(lax.axis_size('dp'))])  45.2 us
    all_to_all x1, blocking collectives, per_device(): lax.all_to_all(rows, 'dp', 0, 0, axis_index_groups=zgroups, tiled=True)  16.3 us
    all_to_all x1, blocking collectives, per_device(): partials = lax.all_to_all(partial, 'tensor', 0, 0, tiled=True)  16.1 us
    ppermute x5, starting transfers between devices, swap(): lax.ppermute(array, 'dp', [(i, i ^ 1) for i in range(lax.axis_size('dp'))])  8.61 us
    pallas_call x1, Pallas kernels, per_device(): call(attend_kernel, [shape((BD, GH * HD), BF16), shape((BD, GH * HD), BF1...  7.98 us
    ppermute x3, starting transfers between devices, per_device(): lax.ppermute(wext, 'dp', [(i, (i + nz * k) % ndp) for i in range(ndp)])  4.81 us
    unnamed x20, local copies, waits for them, and re-layouts  4.5 us
    all_to_all x1, starting transfers between devices, per_device(): lax.all_to_all(sums, 'dp', 0, 0, axis_index_groups=zgroups, tiled=True)  3.33 us
  transfers between devices with their start and end apart: 9, of which 4 were waited for; matrix products, arithmetic and copies ran while one was open for 1% of the time, Pallas kernels for 9%

profile of v1, /device:TPU:2, one launch (start us, length us, event | category | flops | bytes accessed | tf_op | source)
XLA Modules:
  0.0 116.4 jit_solution(2663666035171103463)
XLA Ops:
  0.7 2.2 %copy-done = bf16[8,2,1024,1,128]{4,2,3,1,0:T(8,128)(2,1)S(1)} copy-done((bf16[8,2,1024,1,128]{4,2,3,1,0:T(8,128)(2,1)S(1)}, bf16[8,2,1024,1,128]{4,2,3,1,0:T(8,128)(2,1)}, u32[]{:S(2)}) %copy-start) | copy-done | bytes 4194328
  2.9 0.9 copy-done.2
  3.8 0.7 copy-done.4
  4.5 0.7 copy-done.9
  5.1 0.7 shard_map.112
  5.9 2.9 %collective-permute-start.7 = (bf16[4,2,1024,128]{3,2,1,0:T(8,128)(2,1)}, bf16[4,2,1024,128]{3,2,1,0:T(8,128)(2,1)S(1)}, u32[]{:S(2)}, u32[]{:S(2)}) collective-permute-start(bf16[4,2,1024,128]{3,2,1,0:T(8,128)(2,1)} %get-tuple-element.16), channel_id=1, source_target_pairs={{0,8},{8,0},{16,24},{24,16},{32,40},{40,32},{48,56},{56,48},{64,72... | collective-permute-start | bytes 6291464 | tf_op jit(solution)/shard_map/ppermute | solution.py:269
  8.9 2.3 %collective-permute-start.6 = (bf16[1040,128]{1,0:T(8,128)(2,1)S(1)}, bf16[1040,128]{1,0:T(8,128)(2,1)S(1)}, u32[]{:S(2)}, u32[]{:S(2)}) collective-permute-start(bf16[1040,128]{1,0:T(8,128)(2,1)S(1)} %get-tuple-element.15.w0), channel_id=1, source_target_pairs={{0,192},{8,200},{16,208},{24,216},{32,224},{40,232},{48,240},{56,2... | collective-permute-start | bytes 798728 | tf_op jit(solution)/shard_map/ppermute | solution.py:291
  11.2 0.9 collective-permute-start.5
  12.0 1.9 %collective-permute-start = (s32[8]{0:T(128)S(1)}, s32[8]{0:T(128)S(1)}, u32[]{:S(2)}, u32[]{:S(2)}) collective-permute-start(s32[8]{0:T(128)S(1)} %copy-done.7), channel_id=1, source_target_pairs={{0,8},{8,0},{16,24},{24,16},{32,40},{40,32},{48,56},{56,48},{64,72... | collective-permute-start | bytes 104 | tf_op jit(solution)/shard_map/ppermute | solution.py:269
  14.0 40.9 %collective-permute-done.finr_ref = s32[8]{0:T(128)S(1)} collective-permute-done((s32[8]{0:T(128)S(1)}, s32[8]{0:T(128)S(1)}, u32[]{:S(2)}, u32[]{:S(2)}) %collective-permute-start) | collective-permute-done | bytes 64 | tf_op jit(solution)/shard_map/ppermute | solution.py:269
  54.9 1.7 %collective-permute-start.4 = (bf16[1040,128]{1,0:T(8,128)(2,1)S(1)}, bf16[1040,128]{1,0:T(8,128)(2,1)S(1)}, u32[]{:S(2)}, u32[]{:S(2)}) collective-permute-start(bf16[1040,128]{1,0:T(8,128)(2,1)S(1)} %get-tuple-element.15.w0), channel_id=1, source_target_pairs={{0,64},{8,72},{16,80},{24,88},{32,96},{40,104},{48,112},{56,120},{... | collective-permute-start | bytes 798728 | tf_op jit(solution)/shard_map/ppermute | solution.py:291
  56.5 1.7 %collective-permute-start.1 = (bf16[2,8,8,128]{3,2,1,0:T(8,128)(2,1)S(1)}, bf16[2,8,8,128]{3,2,1,0:T(8,128)(2,1)S(1)}, u32[]{:S(2)}, u32[]{:S(2)}) collective-permute-start(bf16[2,8,8,128]{3,2,1,0:T(8,128)(2,1)S(1)} %copy-done.3), channel_id=1, source_target_pairs={{0,8},{8,0},{16,24},{24,16},{32,40},{40,32},{48,56},{56,48},{64,72... | collective-permute-start | bytes 98312 | tf_op jit(solution)/shard_map/ppermute | solution.py:269
  58.3 2.2 %collective-permute-done.1.qr_ref = bf16[2,8,8,128]{3,2,1,0:T(8,128)(2,1)S(1)} collective-permute-done((bf16[2,8,8,128]{3,2,1,0:T(8,128)(2,1)S(1)}, bf16[2,8,8,128]{3,2,1,0:T(8,128)(2,1)S(1)}, u32[]{:S(2)}, u32[]{:S(2)}) %collective-permute-start.1) | collective-permute-done | bytes 32800 | tf_op jit(solution)/shard_map/ppermute | solution.py:269
  60.5 8.0 %shard_map.111 = (bf16[8,1024]{1,0:T(8,128)(2,1)}, bf16[8,1024]{1,0:T(8,128)(2,1)S(1)}, bf16[8,1024]{1,0:T(8,128)(2,1)S(1)}, bf16[8,8,1024]{2,1,0:T(8,128)(2,1)S(1)}, bf16[8,2,1024,128]{3,2,1,0:T(8,128)(2,1)}) custom-call(s32[256]{0:T(256)S(1)} %copy-done.4, s32[256]{0:T(256)S(1)} %copy-done.8, s32[8]{0:T(128)S(1)} %copy-done.7, ...), custom_call_target="tpu_custom_call" | custom-call | flops 20000000 | bytes 20000000 | tf_op jit(solution)/shard_map/pallas_call | solution.py:293
  68.5 16.3 %all_to_all.15.rows_ref = bf16[8,8,1024]{2,1,0:T(8,128)(2,1)S(1)} all-to-all(bf16[8,8,1024]{2,1,0:T(8,128)(2,1)S(1)} %get-tuple-element.14), channel_id=1, replica_groups={{0,8,16,24,32,40,48,56},{64,72,80,88,96,104,112,120},{128,136,144,152,1..., dimensions={0} | all-to-all | bytes 262144 | tf_op jit(solution)/shard_map/all_to_all | solution.py:320
  85.1 16.1 %all_to_all.16.hid_ref = f32[8,32,640]{2,1,0:T(8,128)S(1)} all-to-all(f32[8,32,640]{2,1,0:T(8,128)S(1)} %shard_map.113), channel_id=1, replica_groups=mesh['dp'=32,'tensor'=8] {'tensor'}, dimensions={0} | all-to-all | bytes 1310720 | tf_op jit(solution)/shard_map/all_to_all | solution.py:324
  101.2 0.8 shard_map.114
  102.0 3.3 %all-to-all-start.2 = ((f32[8,8,128]{2,1,0:T(8,128)}), f32[8,8,128]{2,1,0:T(8,128)S(1)}, u32[]{:S(2)}, u32[]{:S(2)}) async-start(f32[8,8,128]{2,1,0:T(8,128)} %shard_map.114), calls=%async_computation.2 | async-start | bytes 65536 | tf_op jit(solution)/shard_map/all_to_all | solution.py:326
  105.3 1.9 %collective-permute-start.3 = (bf16[8,1024]{1,0:T(8,128)(2,1)S(1)}, bf16[8,1024]{1,0:T(8,128)(2,1)S(1)}, u32[]{:S(2)}, u32[]{:S(2)}) collective-permute-start(bf16[8,1024]{1,0:T(8,128)(2,1)S(1)} %get-tuple-element.13), channel_id=1, source_target_pairs={{0,8},{8,0},{16,24},{24,16},{32,40},{40,32},{48,56},{56,48},{64,72... | collective-permute-start | bytes 49160 | tf_op jit(solution)/shard_map/ppermute | solution.py:269
  107.2 2.1 %collective-permute-done.3 = bf16[8,1024]{1,0:T(8,128)(2,1)S(1)} collective-permute-done((bf16[8,1024]{1,0:T(8,128)(2,1)S(1)}, bf16[8,1024]{1,0:T(8,128)(2,1)S(1)}, u32[]{:S(2)}, u32[]{:S(2)}) %collective-permute-start.3) | collective-permute-done | bytes 16416 | tf_op jit(solution)/shard_map/ppermute | solution.py:269
  109.3 0.6 add.3
  109.9 3.3 %all-to-all-done.2.part_ref = f32[8,8,128]{2,1,0:T(8,128)S(1)} async-done(((f32[8,8,128]{2,1,0:T(8,128)}), f32[8,8,128]{2,1,0:T(8,128)S(1)}, u32[]{:S(2)}, u32[]{:S(2)}) %all-to-all-start.2) | async-done | bytes 32800 | tf_op jit(solution)/shard_map/all_to_all | solution.py:326
  113.3 1.1 shard_map.115
  114.4 2.0 %shard_map.116 = bf16[8,2,1024,128]{3,2,1,0:T(8,128)(2,1)} custom-call(s32[256]{0:T(256)S(1)} %copy-done.5, bf16[4,2,1024,128]{3,2,1,0:T(8,128)(2,1)S(1)} %collective-permute-done.7.recv_ref, bf16[8,2,1024,128]{3,2,1,0:T(8,128)(2,1)} %get-tuple-element.17.into_ref), custom_call_target="tpu_custom_call", output_to_operand_aliasing={{}: (2, {})} | custom-call | flops 1000000 | bytes 1000000 | tf_op jit(solution)/shard_map/pallas_call | solution.py:330
  (23 shorter events, 0.4 us)
Async XLA Ops:
  0.6 11.4 %copy-start.7 = (s32[8]{0:T(128)S(1)}, s32[8]{0:T(128)}, u32[]{:S(2)}) copy-start(s32[8]{0:T(128)} %fino_ref.3) | copy-start | bytes 100
  0.6 59.8 %copy-start.8 = (s32[256]{0:T(256)S(1)}, s32[256]{0:T(256)}, u32[]{:S(2)}) copy-start(s32[256]{0:T(256)} %len_ref.1) | copy-start | bytes 3076
  0.7 2.2 %copy-start = (bf16[8,2,1024,1,128]{4,2,3,1,0:T(8,128)(2,1)S(1)}, bf16[8,2,1024,1,128]{4,2,3,1,0:T(8,128)(2,1)}, u32[]{:S(2)}) copy-start(bf16[8,2,1024,1,128]{4,2,3,1,0:T(8,128)(2,1)} %param.8) | copy-start | bytes 12582916
  2.9 0.9 copy-start.2
  3.8 0.7 copy-start.4
  4.5 0.7 copy-start.9
  5.1 3.6 %copy-start.6 = (bf16[2,8,2,1,128]{4,2,3,1,0:T(2,128)(2,1)S(1)}, bf16[2,8,2,1,128]{4,2,3,1,0:T(2,128)(2,1)}, u32[]{:S(2)}) copy-start(bf16[2,8,2,1,128]{4,2,3,1,0:T(2,128)(2,1)} %param.10) | copy-start | bytes 24580
  5.1 51.4 %copy-start.3 = (bf16[2,8,8,128]{3,2,1,0:T(8,128)(2,1)S(1)}, bf16[2,8,8,128]{3,2,1,0:T(8,128)(2,1)}, u32[]{:S(2)}) copy-start(bf16[2,8,8,128]{3,2,1,0:T(8,128)(2,1)} %qo_ref.1) | copy-start | bytes 98308
  5.1 55.3 %copy-start.1 = (bf16[8,2,1024,1,128]{4,2,3,1,0:T(8,128)(2,1)S(1)}, bf16[8,2,1024,1,128]{4,2,3,1,0:T(8,128)(2,1)}, u32[]{:S(2)}) copy-start(bf16[8,2,1024,1,128]{4,2,3,1,0:T(8,128)(2,1)} %param.8) | copy-start | bytes 12582916
  5.9 108.5 %collective-permute-start.7 = (bf16[4,2,1024,128]{3,2,1,0:T(8,128)(2,1)}, bf16[4,2,1024,128]{3,2,1,0:T(8,128)(2,1)S(1)}, u32[]{:S(2)}, u32[]{:S(2)}) collective-permute-start(bf16[4,2,1024,128]{3,2,1,0:T(8,128)(2,1)} %get-tuple-element.16), channel_id=1, source_target_pairs={{0,8},{8,0},{16,24},{24,16},{32,40},{40,32},{48,56},{56,48},{64,72... | collective-permute-start | bytes 6291464 | tf_op jit(solution)/shard_map/ppermute | solution.py:269
  8.8 47.8 %collective-permute-start.2 = (bf16[2,8,2,128]{3,2,1,0:T(2,128)(2,1)S(1)}, bf16[2,8,2,128]{3,2,1,0:T(2,128)(2,1)S(1)}, u32[]{:S(2)}, u32[]{:S(2)}) collective-permute-start(bf16[2,8,2,128]{3,2,1,0:T(2,128)(2,1)S(1)} %bitcast.8), channel_id=1, source_target_pairs={{0,8},{8,0},{16,24},{24,16},{32,40},{40,32},{48,56},{56,48},{64,72... | collective-permute-start | bytes 24584 | tf_op jit(solution)/shard_map/ppermute | solution.py:269
  8.9 105.5 %copy-start.5 = (s32[256]{0:T(256)S(1)}, s32[256]{0:T(256)}, u32[]{:S(2)}) copy-start(s32[256]{0:T(256)} %par_ref.5) | copy-start | bytes 3076
  8.9 75.9 %collective-permute-start.6 = (bf16[1040,128]{1,0:T(8,128)(2,1)S(1)}, bf16[1040,128]{1,0:T(8,128)(2,1)S(1)}, u32[]{:S(2)}, u32[]{:S(2)}) collective-permute-start(bf16[1040,128]{1,0:T(8,128)(2,1)S(1)} %get-tuple-element.15.w0), channel_id=1, source_target_pairs={{0,192},{8,200},{16,208},{24,216},{32,224},{40,232},{48,240},{56,2... | collective-permute-start | bytes 798728 | tf_op jit(solution)/shard_map/ppermute | solution.py:291
  11.2 73.6 %collective-permute-start.5 = (bf16[1040,128]{1,0:T(8,128)(2,1)S(1)}, bf16[1040,128]{1,0:T(8,128)(2,1)S(1)}, u32[]{:S(2)}, u32[]{:S(2)}) collective-permute-start(bf16[1040,128]{1,0:T(8,128)(2,1)S(1)} %get-tuple-element.15.w0), channel_id=1, source_target_pairs={{0,128},{8,136},{16,144},{24,152},{32,160},{40,168},{48,176},{56,1... | collective-permute-start | bytes 798728 | tf_op jit(solution)/shard_map/ppermute | solution.py:291
  12.0 42.8 %collective-permute-start = (s32[8]{0:T(128)S(1)}, s32[8]{0:T(128)S(1)}, u32[]{:S(2)}, u32[]{:S(2)}) collective-permute-start(s32[8]{0:T(128)S(1)} %copy-done.7), channel_id=1, source_target_pairs={{0,8},{8,0},{16,24},{24,16},{32,40},{40,32},{48,56},{56,48},{64,72... | collective-permute-start | bytes 104 | tf_op jit(solution)/shard_map/ppermute | solution.py:269
  54.9 29.9 %collective-permute-start.4 = (bf16[1040,128]{1,0:T(8,128)(2,1)S(1)}, bf16[1040,128]{1,0:T(8,128)(2,1)S(1)}, u32[]{:S(2)}, u32[]{:S(2)}) collective-permute-start(bf16[1040,128]{1,0:T(8,128)(2,1)S(1)} %get-tuple-element.15.w0), channel_id=1, source_target_pairs={{0,64},{8,72},{16,80},{24,88},{32,96},{40,104},{48,112},{56,120},{... | collective-permute-start | bytes 798728 | tf_op jit(solution)/shard_map/ppermute | solution.py:291
  56.5 3.9 %collective-permute-start.1 = (bf16[2,8,8,128]{3,2,1,0:T(8,128)(2,1)S(1)}, bf16[2,8,8,128]{3,2,1,0:T(8,128)(2,1)S(1)}, u32[]{:S(2)}, u32[]{:S(2)}) collective-permute-start(bf16[2,8,8,128]{3,2,1,0:T(8,128)(2,1)S(1)} %copy-done.3), channel_id=1, source_target_pairs={{0,8},{8,0},{16,24},{24,16},{32,40},{40,32},{48,56},{56,48},{64,72... | collective-permute-start | bytes 98312 | tf_op jit(solution)/shard_map/ppermute | solution.py:269
  102.0 11.3 %all-to-all-start.2 = ((f32[8,8,128]{2,1,0:T(8,128)}), f32[8,8,128]{2,1,0:T(8,128)S(1)}, u32[]{:S(2)}, u32[]{:S(2)}) async-start(f32[8,8,128]{2,1,0:T(8,128)} %shard_map.114), calls=%async_computation.2 | async-start | bytes 65536 | tf_op jit(solution)/shard_map/all_to_all | solution.py:326
  105.3 4.0 %collective-permute-start.3 = (bf16[8,1024]{1,0:T(8,128)(2,1)S(1)}, bf16[8,1024]{1,0:T(8,128)(2,1)S(1)}, u32[]{:S(2)}, u32[]{:S(2)}) collective-permute-start(bf16[8,1024]{1,0:T(8,128)(2,1)S(1)} %get-tuple-element.13), channel_id=1, source_target_pairs={{0,8},{8,0},{16,24},{24,16},{32,40},{40,32},{48,56},{56,48},{64,72... | collective-permute-start | bytes 49160 | tf_op jit(solution)/shard_map/ppermute | solution.py:269

commit v2 on v1

v2 whole, which is shorter than its diff:
```python
import functools
import math

import jax
import jax.numpy as jnp
from jax import lax
from jax.experimental import pallas as pl
from jax.experimental.pallas import tpu as pltpu
from jax.sharding import PartitionSpec as P

D_GEN = 8192
MOST = 4
BD = 8
CACHE = 1024
HD = 128
GH = 8
F32 = jnp.float32
BF16 = jnp.bfloat16
VM = pltpu.VMEM
SM = pltpu.SMEM
HB = pltpu.HBM


def spec(space):
    return pl.BlockSpec(memory_space=space)


def needed(par_ref, slots_at, half):
    flags = []
    for b in range(BD):
        want = half * BD + b
        hit = par_ref[slots_at] == want
        for j in range(1, BD):
            hit = hit | (par_ref[slots_at + j] == want)
        flags.append(hit)
    return flags


def ranked(flags):
    ranks = []
    rank = jnp.int32(0)
    for flag in flags:
        ranks.append(rank)
        rank = rank + flag.astype(jnp.int32)
    return ranks, rank


def message_kernel(fin_ref, q_ref, kv_ref, w_ref, head_ref, msg_ref, wext_ref, wsem):
    rows = w_ref.shape[0]
    wcopy = pltpu.make_async_copy(w_ref, wext_ref.at[pl.ds(0, rows)], wsem)
    wcopy.start()
    wext_ref[pl.ds(rows, 16), :] = jnp.broadcast_to(head_ref[...].astype(F32), (16, HD)).astype(BF16)
    for s in range(BD):
        step = kv_ref[1, s].astype(F32)
        flag = jnp.full((1, HD), fin_ref[s], jnp.int32).astype(F32)
        msg_ref[s] = jnp.concatenate(
            [q_ref[1, s].astype(F32), step, flag, jnp.zeros((5, HD), F32)], axis=0
        ).astype(BF16)
    wcopy.wait()


def pack_kernel(par_ref, cache_ref, after_ref, a_ref, sems):
    me = lax.axis_index("dp")
    half = lax.rem(me, 2)
    start = (me - half) * BD + (1 - half) * BD
    flags = needed(par_ref, start, half)
    ranks, total = ranked(flags)
    odd = lax.rem(lax.axis_index("tensor"), 2) == 1
    early = a_ref.shape[0]
    for b in range(BD):
        for r in range(min(b + 1, early)):

            @pl.when(flags[b] & (ranks[b] == r) & odd)
            def _():
                pltpu.make_async_copy(cache_ref.at[b], a_ref.at[r], sems.at[r]).start()

    for r in range(early):

        @pl.when((r < total) & odd)
        def _():
            pltpu.make_async_copy(cache_ref.at[0], a_ref.at[r], sems.at[r]).wait()


OWN = BD * GH
ALL = OWN + MOST * GH
ROWS = ALL + 2 * GH


def attend_kernel(
    par_ref, len_ref, fin_ref, cache_ref, q_ref, kv_ref, msg_ref,
    first_ref, own_ref, swap_ref, rows_ref, meta_ref, even_ref, odd_ref, newc_ref,
    buf, q2s, q1s, e1s, v1s, pcol, fscr, acc, rscr, crow, pk, insem, outsem, sendsem,
):
    me = lax.axis_index("dp")
    half = lax.rem(me, 2)
    pair = (me - half) * BD
    mine = pair + half * BD
    theirs = pair + (1 - half) * BD
    scaling = math.log2(math.e) / math.sqrt(HD)
    for b in range(BD):
        pltpu.make_async_copy(cache_ref.at[b], buf.at[b], insem.at[b]).start()
    q1s[...] = jnp.zeros_like(q1s)
    for b in range(BD):
        q1s[b, 0:GH, :] = q_ref[0, b]
    e1s[...] = jnp.full_like(e1s, -1e30)
    v1s[...] = jnp.zeros_like(v1s)
    own_local = []
    for s in range(BD):
        local = par_ref[mine + s] - half * BD
        local = jnp.where((local >= 0) & (local < BD), local, -1)
        own_local.append(local)
        rows = pl.ds(s * GH, GH)
        pcol[rows, :] = jnp.full((GH, HD), local, jnp.int32)
        q = q_ref[1, s].astype(F32)
        step = kv_ref[1, s].astype(F32)
        q2s[rows, :] = q
        e1s[rows, :] = jnp.broadcast_to(
            jnp.sum(q * step[0:1], axis=1, keepdims=True) * scaling, (GH, HD)
        )
        v1s[rows, :] = jnp.broadcast_to(step[1:2], (GH, HD))
    slots = [jnp.int32(0)] * MOST
    locals_ = [jnp.int32(-1)] * MOST
    count = jnp.int32(0)
    for s in range(BD):
        local = par_ref[theirs + s] - half * BD
        here = (local >= 0) & (local < BD)
        for j in range(min(s + 1, MOST)):
            take = here & (count == j)
            slots[j] = jnp.where(take, s, slots[j])
            locals_[j] = jnp.where(take, local, locals_[j])
        count = count + here.astype(jnp.int32)
    for j in range(MOST):
        rows = pl.ds(OWN + j * GH, GH)
        pcol[rows, :] = jnp.full((GH, HD), locals_[j], jnp.int32)
        block = msg_ref[slots[j]].astype(F32)
        q = block[0:GH]
        q2s[rows, :] = q
        e1s[rows, :] = jnp.broadcast_to(
            jnp.sum(q * block[GH : GH + 1], axis=1, keepdims=True) * scaling, (GH, HD)
        )
        v1s[rows, :] = jnp.broadcast_to(block[GH + 1 : GH + 2], (GH, HD))
    q2 = q2s[...].astype(BF16)
    acc[...] = jnp.zeros_like(acc)
    wanted = needed(par_ref, theirs, half)
    send_ranks, send_total = ranked(wanted)
    skip = MOST - odd_ref.shape[0]
    core = lax.rem(lax.axis_index("tensor"), 2)
    for b in range(BD):
        pltpu.make_async_copy(cache_ref.at[b], buf.at[b], insem.at[b]).wait()
        for r in range(min(b + 1, MOST)):

            @pl.when(wanted[b] & (send_ranks[b] == r) & (core == 0))
            def _():
                pltpu.make_async_copy(buf.at[b], even_ref.at[r], sendsem.at[r]).start()

            if r >= skip:

                @pl.when(wanted[b] & (send_ranks[b] == r) & (core == 1))
                def _():
                    pltpu.make_async_copy(buf.at[b], odd_ref.at[r - skip], sendsem.at[r]).start()

        for s in range(BD):

            @pl.when(own_local[s] == b)
            def _():
                pltpu.make_async_copy(buf.at[b], newc_ref.at[s], outsem.at[s]).start()

        length = len_ref[mine + b]
        q = jnp.concatenate([q2, q1s[b]], axis=0)
        logits = lax.dot_general(
            q, buf[b, 0], (((1,), (1,)), ((), ())), preferred_element_type=F32
        ) * scaling
        places = lax.broadcasted_iota(jnp.int32, logits.shape, 1)
        logits = jnp.where(places < length, logits, -1e30)
        step = kv_ref[0, b].astype(F32)
        e0 = jnp.sum(q.astype(F32) * step[0:1], axis=1, keepdims=True) * scaling
        e1 = e1s[:, 0:1]
        peak = jnp.maximum(jnp.maximum(jnp.max(logits, axis=1, keepdims=True), e0), e1)
        p = jnp.exp2(logits - peak)
        p0 = jnp.exp2(e0 - peak)
        p1 = jnp.exp2(e1 - peak)
        inv = 1.0 / (jnp.sum(p, axis=1, keepdims=True) + p0 + p1)
        mixed = jnp.dot((p * inv).astype(BF16), buf[b, 1], preferred_element_type=F32)
        mixed = mixed + (p0 * inv).astype(BF16).astype(F32) * step[1:2]
        mixed = mixed + (p1 * inv).astype(BF16).astype(F32) * v1s[...]
        fscr[b * GH : (b + 1) * GH, :] = mixed[ALL : ALL + GH]
        acc[...] = jnp.where(pcol[...] == b, mixed[:ALL], acc[...])
    rscr[...] = jnp.zeros_like(rscr)
    for h in range(GH):
        lanes = slice(h * HD, (h + 1) * HD)
        first_ref[:, lanes] = fscr[pl.ds(h, BD, stride=GH), :].astype(BF16)
        rscr[0:BD, lanes] = acc[pl.ds(h, BD, stride=GH), :].astype(BF16).astype(F32)
        crow[0:MOST, lanes] = acc[pl.ds(OWN + h, MOST, stride=GH), :].astype(BF16).astype(F32)
    for j in range(MOST):

        @pl.when(j < count)
        def _():
            rscr[pl.ds(BD + slots[j], 1), :] = crow[j : j + 1, :]

    own_ref[...] = rscr[0:BD, :].astype(BF16)
    pk[...] = jnp.zeros_like(pk)
    rank = jnp.int32(0)
    before = jnp.int32(0)
    for j in range(2 * BD):
        owned = half == j // BD
        theirs_flag = msg_ref[j % BD].astype(F32)[GH + 2 : GH + 3, :][0, 0] > 0.5
        flag = jnp.where(owned, (fin_ref[j % BD] == 1).astype(jnp.int32), theirs_flag.astype(jnp.int32))
        source = jnp.where(owned, 0, BD) + j % BD

        @pl.when(flag == 1)
        def _():
            pk[pl.ds(jnp.minimum(rank, BD - 1), 1), :] = rscr[pl.ds(source, 1), :]

        if j < BD:
            before = before + jnp.where(half == 1, flag, 0)
        rank = rank + flag
    packed = pk[...].astype(BF16)
    rows_ref[...] = packed
    swap_ref[...] = jnp.concatenate([rscr[BD : 2 * BD, :], pk[...]], axis=0).astype(BF16)
    ranks, _ = ranked(needed(par_ref, mine, 1 - half))
    for s in range(BD):
        local = par_ref[mine + s] - (1 - half) * BD
        slot = jnp.int32(-1)
        for b in range(BD):
            slot = jnp.where(local == b, ranks[b], slot)
        meta_ref[s : s + 1, :] = jnp.full((1, HD), slot, jnp.int32)
        flag = (fin_ref[s] == 1).astype(jnp.int32)
        place_at = jnp.where(flag == 1, jnp.minimum(before, BD - 1), -1)
        meta_ref[BD + s : BD + s + 1, :] = jnp.full((1, HD), place_at, jnp.int32)
        before = before + flag
    for r in range(MOST):

        @pl.when((r < send_total) & ((core == 0) | (r >= skip)))
        def _():
            pltpu.make_async_copy(buf.at[0], even_ref.at[0], sendsem.at[r]).wait()

    for s in range(BD):

        @pl.when(own_local[s] >= 0)
        def _():
            pltpu.make_async_copy(buf.at[0], newc_ref.at[s], outsem.at[s]).wait()


def place_start(first, parity, meta_ref, recv_ref, newc_ref, sems):
    crossing = []
    count = recv_ref.shape[0]
    core = lax.rem(lax.axis_index("tensor"), 2)
    for s in range(BD):
        slot = meta_ref[s : s + 1, :][0, 0] - first
        cross = (slot >= 0) & (slot < count) & (core == parity)
        slot = jnp.clip(slot, 0, count - 1)
        crossing.append(cross)

        @pl.when(cross)
        def _():
            pltpu.make_async_copy(recv_ref.at[slot], newc_ref.at[s], sems.at[s]).start()

    return crossing


def place_wait(crossing, recv_ref, newc_ref, sems):
    for s in range(BD):

        @pl.when(crossing[s])
        def _():
            pltpu.make_async_copy(recv_ref.at[0], newc_ref.at[s], sems.at[s]).wait()


def place_kernel(first, parity, meta_ref, recv_ref, *refs):
    newc_ref, sems = refs[-2:]
    waits = place_start(first, parity, meta_ref, recv_ref, newc_ref, sems)
    place_wait(waits, recv_ref, newc_ref, sems)


def gate_kernel(*refs):
    del refs


def join_kernel(parity, own_ref, rows_ref, swap_ref, meta_ref, recv_ref, *refs):
    second_ref, full_ref, _, newc_ref, sems = refs[-5:]
    waits = place_start(0, parity, meta_ref, recv_ref, newc_ref, sems)
    second_ref[...] = own_ref[...] + swap_ref[0:BD, :]
    full_ref[...] = rows_ref[...] + swap_ref[BD : 2 * BD, :]
    place_wait(waits, recv_ref, newc_ref, sems)


def hidden_kernel(own_ref, r1, r2, r3, w0, w1, w2, w3, out_ref):
    depth = w0.shape[0] - 16
    odd = lax.rem(lax.axis_index("dp"), 2) == 1
    near, far = r1[...].astype(F32), r2[...].astype(F32)
    rows = jnp.concatenate(
        [
            own_ref[...].astype(F32),
            jnp.where(odd, near, far),
            r3[...].astype(F32),
            jnp.where(odd, far, near),
        ],
        axis=0,
    )
    narrow = rows.astype(BF16)
    parts = [
        jnp.dot(narrow, w[0:depth, :], preferred_element_type=F32) for w in (w0, w1, w2, w3)
    ]
    squares = jnp.sum(rows * rows, axis=1, keepdims=True)
    parts.append(jnp.broadcast_to(squares, (rows.shape[0], HD)))
    for k in range(out_ref.shape[0]):
        for i, part in enumerate(parts):
            out_ref[k, :, i * HD : (i + 1) * HD] = part.astype(out_ref.dtype)


def score_kernel(hid_ref, w0, w1, w2, w3, wait_ref, gate_ref, out_ref, gated_ref):
    depth = w0.shape[0] - 16
    total = hid_ref[0].astype(F32)
    for k in range(1, hid_ref.shape[0]):
        total = total + hid_ref[k].astype(F32)
    factor = lax.rsqrt(total[:, 4 * HD : 4 * HD + 1] / D_GEN + 1e-05)
    sums = jnp.zeros((total.shape[0], 1), F32)
    for i, w in enumerate((w0, w1, w2, w3)):
        head = w[depth : depth + 16, :].astype(F32)[0:1, :]
        v = total[:, i * HD : (i + 1) * HD] * factor
        sums = sums + jnp.sum(v / (1.0 + jnp.exp(-v)) * head, axis=1, keepdims=True)
    wide = jnp.broadcast_to(sums, (total.shape[0], HD))
    pairs = out_ref.shape[0] // 2
    mine = lax.rem(lax.axis_index("dp") // 2, pairs)
    for q in range(pairs):
        target = lax.rem(mine + q, pairs)
        for half in range(2):
            out_ref[2 * target + half] = wide[q * BD : (q + 1) * BD]


def final_kernel(meta_ref, part_ref, hop_ref, out_ref, scr):
    total, other = part_ref[0], hop_ref[0]
    for k in range(1, part_ref.shape[0]):
        total = total + part_ref[k]
        other = other + hop_ref[k]
    odd = lax.rem(lax.axis_index("tensor"), 2) == 1
    scr[...] = jnp.where(odd, other, total)
    for s in range(BD):
        rank = meta_ref[BD + s : BD + s + 1, :][0, 0]
        value = scr[pl.ds(jnp.maximum(rank, 0), 1), :][0, 0]
        out_ref[s] = jnp.where(rank >= 0, value, 0.0)


def call(kernel, outs, ins, out_specs, scratch=(), aliases=None, cost=None, limit=60):
    return functools.partial(
        pl.pallas_call,
        kernel,
        out_shape=outs,
        in_specs=[spec(s) for s in ins],
        out_specs=[spec(s) for s in out_specs],
        scratch_shapes=list(scratch),
        input_output_aliases=aliases or {},
        compiler_params=pltpu.CompilerParams(vmem_limit_bytes=limit * 1024 * 1024),
        cost_estimate=pl.CostEstimate(flops=cost or 1000000, bytes_accessed=cost or 1000000, transcendentals=0),
    )()


def shape(dims, dtype):
    return jax.ShapeDtypeStruct(dims, dtype)


def swap(array):
    return lax.ppermute(array, "dp", [(i, i ^ 1) for i in range(lax.axis_size("dp"))])


def swap_half(array, parity):
    nd, nt = lax.axis_size("dp"), lax.axis_size("tensor")
    pairs = [(d * nt + t, (d ^ 1) * nt + t) for d in range(nd) for t in range(parity, nt, 2)]
    return lax.ppermute(array, ("dp", "tensor"), pairs)


def place(first, parity, meta, recv, newc):
    return call(
        functools.partial(place_kernel, first, parity),
        [shape(newc.shape, BF16)],
        [VM, VM, HB],
        [HB],
        [pltpu.SemaphoreType.DMA((BD,))],
        aliases={2: 0},
        limit=16,
    )(meta, recv, newc)[0]


def away(array, nz, k):
    nd = lax.axis_size("dp")
    pairs = []
    for d in range(nd):
        z = d % nz
        pairs.append((d, d - z + (z - k if z % 2 == 0 else z + k) % nz))
    return lax.ppermute(array, "dp", pairs)


def score_groups(nx, nz, nt):
    def index(x, z, t):
        return (x * nz + z) * nt + t

    groups = [[index(x, z, t) for z in range(nz)] for x in range(nx) for t in range(0, nt, 2)]
    across = 2 * nz // nt
    for z in range(nz):
        for x in range(0, nx, across):
            groups.append([index(x + i, z, t) for i in range(across) for t in range(1, nt, 2)])
    return groups


EARLY = 2


def per_device(nx, nz, cache_kv, lengths, step_kv, queries, parents, finished, reward_in, reward_head):
    ndp = nx * nz
    nt = lax.axis_size("tensor")
    cache = cache_kv.reshape(BD, 2, CACHE, HD)
    kv = step_kv.reshape(2, BD, 2, HD)
    depth = reward_in.shape[0]
    part_a = shape((EARLY, 2, CACHE, HD), BF16)
    part_b = shape((MOST - EARLY, 2, CACHE, HD), BF16)
    whole = shape((MOST, 2, CACHE, HD), BF16)
    msg, wext = call(
        message_kernel,
        [shape((BD, 16, HD), BF16), shape((depth + 16, HD), BF16)],
        [SM, VM, VM, HB, VM],
        [VM, VM],
        [pltpu.SemaphoreType.DMA],
        limit=60,
        cost=100000,
    )(finished, queries, kv, reward_in, reward_head.reshape(1, HD))
    recv_msg = swap(msg)
    (oa,) = call(
        pack_kernel,
        [part_a],
        [SM, HB, pl.ANY],
        [VM],
        [pltpu.SemaphoreType.DMA((EARLY,))],
        limit=59,
        cost=20000000,
    )(parents, cache, msg)
    (oa,) = call(
        gate_kernel, [part_a], [pl.ANY, pl.ANY], [pl.ANY], aliases={0: 0}, limit=16, cost=1000
    )(oa, recv_msg)
    recv_oa = swap_half(oa, 1)
    others = [
        lax.ppermute(wext, "dp", [(i, (i + nz * k) % ndp) for i in range(ndp)]) for k in range(1, nx)
    ]
    first_out, own_out, to_swap, rows, meta, to_even, to_odd, newc = call(
        attend_kernel,
        [
            shape((BD, GH * HD), BF16),
            shape((BD, GH * HD), BF16),
            shape((2 * BD, GH * HD), BF16),
            shape((BD, GH * HD), BF16),
            shape((2 * BD, HD), jnp.int32),
            whole,
            part_b,
            shape((BD, 2, CACHE, HD), BF16),
        ],
        [SM, SM, SM, HB, VM, VM, VM],
        [VM] * 7 + [HB],
        [
            VM((BD, 2, CACHE, HD), BF16),
            VM((ALL, HD), F32),
            VM((BD, 2 * GH, HD), BF16),
            VM((ROWS, HD), F32),
            VM((ROWS, HD), F32),
            VM((ALL, HD), jnp.int32),
            VM((OWN, HD), F32),
            VM((ALL, HD), F32),
            VM((2 * BD, GH * HD), F32),
            VM((BD, GH * HD), F32),
            VM((BD, GH * HD), F32),
            pltpu.SemaphoreType.DMA((BD,)),
            pltpu.SemaphoreType.DMA((BD,)),
            pltpu.SemaphoreType.DMA((MOST,)),
        ],
        cost=20000000,
        limit=32,
    )(parents, lengths, finished, cache, queries, kv, recv_msg)
    second_out, rows, to_even, newc = call(
        functools.partial(join_kernel, 1),
        [shape(own_out.shape, BF16), shape(rows.shape, BF16), whole, shape(newc.shape, BF16)],
        [VM] * 5 + [pl.ANY, HB, pl.ANY, pl.ANY, pl.ANY],
        [VM, VM, pl.ANY, HB],
        [pltpu.SemaphoreType.DMA((BD,))],
        aliases={5: 2, 6: 3},
        limit=16,
    )(own_out, rows, swap(to_swap), meta, recv_oa, to_even, newc, *others)
    recv_even = swap_half(to_even, 0)
    (partial,) = call(
        hidden_kernel, [shape((nt, nz // 2 * BD, 5 * HD), BF16)], [VM] * 8, [VM], limit=16
    )(rows, *[away(rows, nz, k) for k in (1, 2, 3)], wext, *others)
    partials = lax.all_to_all(partial, "tensor", 0, 0, tiled=True)
    sums, to_odd = call(
        score_kernel,
        [shape((nz, BD, HD), F32), part_b],
        [VM] * 5 + [pl.ANY, pl.ANY],
        [VM, pl.ANY],
        aliases={6: 1},
        limit=16,
    )(partials, wext, *others, recv_even, to_odd)
    recv_odd = swap_half(to_odd, 1)
    sums = lax.all_to_all(sums, ("dp", "tensor"), 0, 0, axis_index_groups=score_groups(nx, nz, nt), tiled=True)
    hop = lax.ppermute(sums, "tensor", [(t, t + 1) for t in range(0, nt, 2)])
    (scores,) = call(
        final_kernel, [shape((BD,), F32)], [VM, VM, VM], [SM], [VM((BD, HD), F32)], limit=16
    )(meta, sums, hop)
    newc = place(0, 0, meta, recv_even, newc)
    newc = place(EARLY, 1, meta, recv_odd, newc)
    return (first_out, second_out, scores, newc.reshape(cache_kv.shape))


def solution(mesh):
    ndp = mesh.shape["dp"]
    nx = 4
    return jax.shard_map(
        functools.partial(per_device, nx, ndp // nx),
        mesh=mesh,
        in_specs=(
            P("dp", None, None, "tensor", None),
            P(),
            P(None, "dp", None, "tensor", None),
            P(None, "dp", "tensor", None),
            P(),
            P("dp"),
            P("tensor", "dp"),
            P("dp"),
        ),
        out_specs=(
            P("dp", "tensor"),
            P("dp", "tensor"),
            P("dp"),
            P("dp", None, None, "tensor", None),
        ),
        check_vma=False,
    )
```

time: 117 us -> 79.4 us (0.68)
  the two profiles are of different devices: /device:TPU:2 before, /device:TPU:17 now
where the time goes in v2:
time: 79.4 us
  starting transfers between devices  23.4 us (29%)
  blocking collectives  20.2 us (25%)
  Pallas kernels  17.8 us (22%)
  waiting for transfers between devices  17 us (21%)
  between operations  0.84 us (1%)
    all_to_all x1, blocking collectives, per_device(): partials = lax.all_to_all(partial, 'tensor', 0, 0, tiled=True)  12.9 us
    ppermute x1, waiting for transfers between devices, per_device(): hop = lax.ppermute(sums, 'tensor', [(t, t + 1) for t in range(0, nt, 2)])  11.9 us
    ppermute x3, starting transfers between devices, away(): return lax.ppermute(array, 'dp', pairs)  9.67 us
    pallas_call x1, Pallas kernels, per_device(): call(attend_kernel, [shape((BD, GH * HD), BF16), shape((BD, GH * HD), BF1...  9.04 us
    all_to_all x1, blocking collectives, per_device(): lax.all_to_all(sums, ('dp', 'tensor'), 0, 0, axis_index_groups=score_grou...  7.35 us
    ppermute x3, starting transfers between devices, swap_half(): return lax.ppermute(array, ('dp', 'tensor'), pairs)  6.23 us
    ppermute x3, starting transfers between devices, per_device(): lax.ppermute(wext, 'dp', [(i, (i + nz * k) % ndp) for i in range(ndp)])  3.68 us
    pallas_call x1, Pallas kernels, per_device(): call(pack_kernel, [part_a], [SM, HB, pl.ANY], [VM], [pltpu.SemaphoreType....  2.95 us
  transfers between devices with their start and end apart: 12, of which 5 were waited for; matrix products, arithmetic and copies ran while one was open for 0% of the time, Pallas kernels for 17%

profile of v2, /device:TPU:17, one launch (start us, length us, event | category | flops | bytes accessed | tf_op | source)
XLA Modules:
  0.0 79.4 jit_solution(14819911795862037627)
XLA Ops:
  0.7 2.5 %shard_map.111 = (bf16[8,16,128]{2,1,0:T(8,128)(2,1)}, bf16[1040,128]{1,0:T(8,128)(2,1)}) custom-call(s32[8]{0:T(128)} %fin_ref.3, bf16[2,8,8,128]{3,2,1,0:T(8,128)(2,1)} %q_ref.3, bf16[2,8,2,128]{3,2,1,0:T(2,128)(2,1)} %bitcast.8, bf16[1024,128]{1,0:T(8,128)(2,1)} %w_ref.1, bf16[1,128]{1,0:T(2,128)(2,1)} %bitcast.11), custom_call_target="tpu_custom_call" | custom-call | flops 100000 | bytes 100000 | tf_op jit(solution)/shard_map/pallas_call | solution.py:417
  3.2 1.7 %collective-permute-start = (bf16[8,16,128]{2,1,0:T(8,128)(2,1)}, bf16[8,16,128]{2,1,0:T(8,128)(2,1)S(1)}, u32[]{:S(2)}, u32[]{:S(2)}) collective-permute-start(bf16[8,16,128]{2,1,0:T(8,128)(2,1)} %get-tuple-element.20.after_ref), channel_id=1, source_target_pairs={{0,8},{8,0},{16,24},{24,16},{32,40},{40,32},{48,56},{56,48},{64,72... | collective-permute-start | bytes 98312 | tf_op jit(solution)/shard_map/ppermute | solution.py:363
  4.9 2.9 %shard_map.113.refs_0_ = bf16[2,2,1024,128]{3,2,1,0:T(8,128)(2,1)} custom-call(s32[256]{0:T(256)} %par_ref.3, bf16[8,2,1024,128]{3,2,1,0:T(8,128)(2,1)} %bitcast.6, bf16[8,16,128]{2,1,0:T(8,128)(2,1)} %get-tuple-element.20.after_ref), custom_call_target="tpu_custom_call" | custom-call | flops 20000000 | bytes 20000000 | tf_op jit(solution)/shard_map/pallas_call | solution.py:427
  7.9 2.4 %collective-permute-start.2 = (bf16[2,2,1024,128]{3,2,1,0:T(8,128)(2,1)}, bf16[2,2,1024,128]{3,2,1,0:T(8,128)(2,1)S(1)}, u32[]{:S(2)}, u32[]{:S(2)}) collective-permute-start(bf16[2,2,1024,128]{3,2,1,0:T(8,128)(2,1)} %shard_map.114), channel_id=1, source_target_pairs={{1,9},{3,11},{5,13},{7,15},{9,1},{11,3},{13,5},{15,7},{17,25},{19,... | collective-permute-start | bytes 3145736 | tf_op jit(solution)/shard_map/ppermute | solution.py:369
  10.3 2.6 %collective-permute-start.5 = (bf16[1040,128]{1,0:T(8,128)(2,1)S(1)}, bf16[1040,128]{1,0:T(8,128)(2,1)S(1)}, u32[]{:S(2)}, u32[]{:S(2)}) collective-permute-start(bf16[1040,128]{1,0:T(8,128)(2,1)S(1)} %copy-done.1), channel_id=1, source_target_pairs={{0,192},{8,200},{16,208},{24,216},{32,224},{40,232},{48,240},{56,2... | collective-permute-start | bytes 798728 | tf_op jit(solution)/shard_map/ppermute | solution.py:441
  12.9 0.5 collective-permute-start.4
  13.4 0.6 collective-permute-start.3
  14.0 9.0 %shard_map.112 = (bf16[8,1024]{1,0:T(8,128)(2,1)}, bf16[8,1024]{1,0:T(8,128)(2,1)S(1)}, bf16[16,1024]{1,0:T(8,128)(2,1)S(1)}, bf16[8,1024]{1,0:T(8,128)(2,1)S(1)...) custom-call(s32[256]{0:T(256)S(1)} %copy-done.4, ...), custom_call_target="tpu_custom_call" | custom-call | flops 20000000 | bytes 20000000 | tf_op jit(solution)/shard_map/pallas_call | solution.py:443
  23.1 0.8 %collective-permute-start.1 = (bf16[16,1024]{1,0:T(8,128)(2,1)S(1)}, bf16[16,1024]{1,0:T(8,128)(2,1)S(1)}, u32[]{:S(2)}, u32[]{:S(2)}) collective-permute-start(bf16[16,1024]{1,0:T(8,128)(2,1)S(1)} %get-tuple-element.24), channel_id=1, source_target_pairs={{0,8},{8,0},{16,24},{24,16},{32,40},{40,32},{48,56},{56,48},{64,72... | collective-permute-start | bytes 98312 | tf_op jit(solution)/shard_map/ppermute | solution.py:363
  23.9 2.5 %collective-permute-done.1.swap_ref = bf16[16,1024]{1,0:T(8,128)(2,1)S(1)} collective-permute-done((bf16[16,1024]{1,0:T(8,128)(2,1)S(1)}, bf16[16,1024]{1,0:T(8,128)(2,1)S(1)}, u32[]{:S(2)}, u32[]{:S(2)}) %collective-permute-start.1) | collective-permute-done | bytes 32800 | tf_op jit(solution)/shard_map/ppermute | solution.py:363
  26.5 1.2 %collective-permute-done.3.refs_2_.w1 = bf16[1040,128]{1,0:T(8,128)(2,1)S(1)} collective-permute-done((bf16[1040,128]{1,0:T(8,128)(2,1)S(1)}, bf16[1040,128]{1,0:T(8,128)(2,1)S(1)}, u32[]{:S(2)}, u32[]{:S(2)}) %collective-permute-start.3) | collective-permute-done | bytes 266272 | tf_op jit(solution)/shard_map/ppermute | solution.py:441
  27.7 1.7 %shard_map.115 = (bf16[8,1024]{1,0:T(8,128)(2,1)}, bf16[8,1024]{1,0:T(8,128)(2,1)S(1)}, bf16[4,2,1024,128]{3,2,1,0:T(8,128)(2,1)S(1)}, bf16[8,2,1024,128]{3,2,1,0:T(8,128)(2,1)}) custom-call(bf16[8,1024]{1,0:T(8,128)(2,1)S(1)} %get-tuple-element.22.own_ref, ...), custom_call_target="tpu_custom_call", output_to_operand_aliasing={{2}: (5, {}), {3}: (6, {})} | custom-call | flops 1000000 | bytes 1000000 | tf_op jit(solution)/shard_map/pallas_call | solution.py:476
  29.4 0.8 %collective-permute-start.9 = (bf16[4,2,1024,128]{3,2,1,0:T(8,128)(2,1)S(1)}, bf16[4,2,1024,128]{3,2,1,0:T(8,128)(2,1)S(1)}, u32[]{:S(2)}, u32[]{:S(2)}) collective-permute-start(bf16[4,2,1024,128]{3,2,1,0:T(8,128)(2,1)S(1)} %get-tuple-element.31), channel_id=1, source_target_pairs={{0,8},{2,10},{4,12},{6,14},{8,0},{10,2},{12,4},{14,6},{16,24},{18,... | collective-permute-start | bytes 6291464 | tf_op jit(solution)/shard_map/ppermute | solution.py:369
  30.2 6.6 %collective-permute-start.8 = (bf16[8,1024]{1,0:T(8,128)(2,1)S(1)}, bf16[8,1024]{1,0:T(8,128)(2,1)S(1)}, u32[]{:S(2)}, u32[]{:S(2)}) collective-permute-start(bf16[8,1024]{1,0:T(8,128)(2,1)S(1)} %get-tuple-element.30.own_ref), channel_id=1, source_target_pairs={{0,40},{8,32},{16,56},{24,48},{32,8},{40,0},{48,24},{56,16},{64,10... | collective-permute-start | bytes 49160 | tf_op jit(solution)/shard_map/ppermute | solution.py:390
  37.0 2.9 %collective-permute-start.6 = (bf16[8,1024]{1,0:T(8,128)(2,1)S(1)}, bf16[8,1024]{1,0:T(8,128)(2,1)S(1)}, u32[]{:S(2)}, u32[]{:S(2)}) collective-permute-start(bf16[8,1024]{1,0:T(8,128)(2,1)S(1)} %get-tuple-element.30.own_ref), channel_id=1, source_target_pairs={{0,56},{8,16},{16,8},{24,32},{32,24},{40,48},{48,40},{56,0},{64,12... | collective-permute-start | bytes 49160 | tf_op jit(solution)/shard_map/ppermute | solution.py:390
  39.9 0.7 collective-permute-done.7.r2
  40.6 0.6 collective-permute-done.6.r1
  41.2 0.3 shard_map.116
  41.5 12.9 %all_to_all.10.hid_ref = bf16[8,32,640]{2,1,0:T(8,128)(2,1)S(1)} all-to-all(bf16[8,32,640]{2,1,0:T(8,128)(2,1)S(1)} %shard_map.116), channel_id=1, replica_groups=mesh['dp'=32,'tensor'=8] {'tensor'}, dimensions={0} | all-to-all | bytes 655360 | tf_op jit(solution)/shard_map/all_to_all | solution.py:489
  54.5 3.0 %collective-permute-start.11 = (bf16[2,2,1024,128]{3,2,1,0:T(8,128)(2,1)S(1)}, bf16[2,2,1024,128]{3,2,1,0:T(8,128)(2,1)S(1)}, u32[]{:S(2)}, u32[]{:S(2)}) collective-permute-start(bf16[2,2,1024,128]{3,2,1,0:T(8,128)(2,1)S(1)} %get-tuple-element.34), channel_id=1, source_target_pairs={{1,9},{3,11},{5,13},{7,15},{9,1},{11,3},{13,5},{15,7},{17,25},{19,... | collective-permute-start | bytes 3145736 | tf_op jit(solution)/shard_map/ppermute | solution.py:369
  57.6 7.4 %all_to_all.11.part_ref = f32[8,8,128]{2,1,0:T(8,128)S(1)} all-to-all(f32[8,8,128]{2,1,0:T(8,128)S(1)} %get-tuple-element.33), channel_id=1, replica_groups={{0,8,16,24,32,40,48,56},{2,10,18,26,34,42,50,58},{4,12,20,28,36,44,52,6..., dimensions={0} | all-to-all | bytes 65536 | tf_op jit(solution)/shard_map/all_to_all | solution.py:499
  64.9 1.3 %collective-permute-start.10 = (f32[8,8,128]{2,1,0:T(8,128)S(1)}, f32[8,8,128]{2,1,0:T(8,128)S(1)}, u32[]{:S(2)}, u32[]{:S(2)}) collective-permute-start(f32[8,8,128]{2,1,0:T(8,128)S(1)} %all_to_all.11.part_ref), channel_id=1, source_target_pairs={{0,1},{2,3},{4,5},{6,7},{8,9},{10,11},{12,13},{14,15},{16,17},{18,... | collective-permute-start | bytes 98312 | tf_op jit(solution)/shard_map/ppermute | solution.py:500
  66.4 11.9 %collective-permute-done.10.hop_ref = f32[8,8,128]{2,1,0:T(8,128)S(1)} collective-permute-done((f32[8,8,128]{2,1,0:T(8,128)S(1)}, f32[8,8,128]{2,1,0:T(8,128)S(1)}, u32[]{:S(2)}, u32[]{:S(2)}) %collective-permute-start.10) | collective-permute-done | bytes 32800 | tf_op jit(solution)/shard_map/ppermute | solution.py:500
  78.3 0.8 %shard_map.118 = f32[8]{0:T(128)} custom-call(s32[16,128]{1,0:T(8,128)S(1)} %get-tuple-element.25.meta_ref, f32[8,8,128]{2,1,0:T(8,128)S(1)} %all_to_all.11.part_ref, f32[8,8,128]{2,1,0:T(8,128)S(1)} %collective-permute-done.10.hop_ref), custom_call_target="tpu_custom_call" | custom-call | flops 1000000 | bytes 1000000 | tf_op jit(solution)/shard_map/pallas_call | solution.py:501
  (26 shorter events, 0.8 us)
Async XLA Ops:
  0.6 13.4 %copy-start.5 = (s32[8]{0:T(128)S(1)}, s32[8]{0:T(128)}, u32[]{:S(2)}) copy-start(s32[8]{0:T(128)} %fin_ref.3) | copy-start | bytes 100
  0.6 13.4 %copy-start.2 = (bf16[2,8,8,128]{3,2,1,0:T(8,128)(2,1)S(1)}, bf16[2,8,8,128]{3,2,1,0:T(8,128)(2,1)}, u32[]{:S(2)}) copy-start(bf16[2,8,8,128]{3,2,1,0:T(8,128)(2,1)} %q_ref.3) | copy-start | bytes 98308
  0.7 13.4 %copy-start.3 = (bf16[2,8,2,1,128]{4,2,3,1,0:T(2,128)(2,1)S(1)}, bf16[2,8,2,1,128]{4,2,3,1,0:T(2,128)(2,1)}, u32[]{:S(2)}) copy-start(bf16[2,8,2,1,128]{4,2,3,1,0:T(2,128)(2,1)} %param.10) | copy-start | bytes 24580
  0.7 13.4 %copy-start.4 = (s32[256]{0:T(256)S(1)}, s32[256]{0:T(256)}, u32[]{:S(2)}) copy-start(s32[256]{0:T(256)} %par_ref.3) | copy-start | bytes 3076
  0.7 13.4 %copy-start.6 = (s32[256]{0:T(256)S(1)}, s32[256]{0:T(256)}, u32[]{:S(2)}) copy-start(s32[256]{0:T(256)} %len_ref.1) | copy-start | bytes 3076
  3.2 7.1 %copy-start.1 = (bf16[1040,128]{1,0:T(8,128)(2,1)S(1)}, bf16[1040,128]{1,0:T(8,128)(2,1)}, u32[]{:S(2)}) copy-start(bf16[1040,128]{1,0:T(8,128)(2,1)} %get-tuple-element.28.w0) | copy-start | bytes 798724
  3.2 10.8 %copy-start = (bf16[8,2,1024,1,128]{4,2,3,1,0:T(8,128)(2,1)S(1)}, bf16[8,2,1024,1,128]{4,2,3,1,0:T(8,128)(2,1)}, u32[]{:S(2)}) copy-start(bf16[8,2,1024,1,128]{4,2,3,1,0:T(8,128)(2,1)} %param.8) | copy-start | bytes 12582916
  3.2 4.7 %collective-permute-start = (bf16[8,16,128]{2,1,0:T(8,128)(2,1)}, bf16[8,16,128]{2,1,0:T(8,128)(2,1)S(1)}, u32[]{:S(2)}, u32[]{:S(2)}) collective-permute-start(bf16[8,16,128]{2,1,0:T(8,128)(2,1)} %get-tuple-element.20.after_ref), channel_id=1, source_target_pairs={{0,8},{8,0},{16,24},{24,16},{32,40},{40,32},{48,56},{56,48},{64,72... | collective-permute-start | bytes 98312 | tf_op jit(solution)/shard_map/ppermute | solution.py:363
  7.9 19.8 %collective-permute-start.2 = (bf16[2,2,1024,128]{3,2,1,0:T(8,128)(2,1)}, bf16[2,2,1024,128]{3,2,1,0:T(8,128)(2,1)S(1)}, u32[]{:S(2)}, u32[]{:S(2)}) collective-permute-start(bf16[2,2,1024,128]{3,2,1,0:T(8,128)(2,1)} %shard_map.114), channel_id=1, source_target_pairs={{1,9},{3,11},{5,13},{7,15},{9,1},{11,3},{13,5},{15,7},{17,25},{19,... | collective-permute-start | bytes 3145736 | tf_op jit(solution)/shard_map/ppermute | solution.py:369
  10.3 16.1 %collective-permute-start.5 = (bf16[1040,128]{1,0:T(8,128)(2,1)S(1)}, bf16[1040,128]{1,0:T(8,128)(2,1)S(1)}, u32[]{:S(2)}, u32[]{:S(2)}) collective-permute-start(bf16[1040,128]{1,0:T(8,128)(2,1)S(1)} %copy-done.1), channel_id=1, source_target_pairs={{0,192},{8,200},{16,208},{24,216},{32,224},{40,232},{48,240},{56,2... | collective-permute-start | bytes 798728 | tf_op jit(solution)/shard_map/ppermute | solution.py:441
  12.9 13.6 %collective-permute-start.4 = (bf16[1040,128]{1,0:T(8,128)(2,1)S(1)}, bf16[1040,128]{1,0:T(8,128)(2,1)S(1)}, u32[]{:S(2)}, u32[]{:S(2)}) collective-permute-start(bf16[1040,128]{1,0:T(8,128)(2,1)S(1)} %copy-done.1), channel_id=1, source_target_pairs={{0,128},{8,136},{16,144},{24,152},{32,160},{40,168},{48,176},{56,1... | collective-permute-start | bytes 798728 | tf_op jit(solution)/shard_map/ppermute | solution.py:441
  13.4 14.3 %collective-permute-start.3 = (bf16[1040,128]{1,0:T(8,128)(2,1)S(1)}, bf16[1040,128]{1,0:T(8,128)(2,1)S(1)}, u32[]{:S(2)}, u32[]{:S(2)}) collective-permute-start(bf16[1040,128]{1,0:T(8,128)(2,1)S(1)} %copy-done.1), channel_id=1, source_target_pairs={{0,64},{8,72},{16,80},{24,88},{32,96},{40,104},{48,112},{56,120},{... | collective-permute-start | bytes 798728 | tf_op jit(solution)/shard_map/ppermute | solution.py:441
  23.1 3.4 %collective-permute-start.1 = (bf16[16,1024]{1,0:T(8,128)(2,1)S(1)}, bf16[16,1024]{1,0:T(8,128)(2,1)S(1)}, u32[]{:S(2)}, u32[]{:S(2)}) collective-permute-start(bf16[16,1024]{1,0:T(8,128)(2,1)S(1)} %get-tuple-element.24), channel_id=1, source_target_pairs={{0,8},{8,0},{16,24},{24,16},{32,40},{40,32},{48,56},{56,48},{64,72... | collective-permute-start | bytes 98312 | tf_op jit(solution)/shard_map/ppermute | solution.py:363
  29.4 24.9 %collective-permute-start.9 = (bf16[4,2,1024,128]{3,2,1,0:T(8,128)(2,1)S(1)}, bf16[4,2,1024,128]{3,2,1,0:T(8,128)(2,1)S(1)}, u32[]{:S(2)}, u32[]{:S(2)}) collective-permute-start(bf16[4,2,1024,128]{3,2,1,0:T(8,128)(2,1)S(1)} %get-tuple-element.31), channel_id=1, source_target_pairs={{0,8},{2,10},{4,12},{6,14},{8,0},{10,2},{12,4},{14,6},{16,24},{18,... | collective-permute-start | bytes 6291464 | tf_op jit(solution)/shard_map/ppermute | solution.py:369
  30.2 9.7 %collective-permute-start.8 = (bf16[8,1024]{1,0:T(8,128)(2,1)S(1)}, bf16[8,1024]{1,0:T(8,128)(2,1)S(1)}, u32[]{:S(2)}, u32[]{:S(2)}) collective-permute-start(bf16[8,1024]{1,0:T(8,128)(2,1)S(1)} %get-tuple-element.30.own_ref), channel_id=1, source_target_pairs={{0,40},{8,32},{16,56},{24,48},{32,8},{40,0},{48,24},{56,16},{64,10... | collective-permute-start | bytes 49160 | tf_op jit(solution)/shard_map/ppermute | solution.py:390
  36.8 3.8 %collective-permute-start.7 = (bf16[8,1024]{1,0:T(8,128)(2,1)S(1)}, bf16[8,1024]{1,0:T(8,128)(2,1)S(1)}, u32[]{:S(2)}, u32[]{:S(2)}) collective-permute-start(bf16[8,1024]{1,0:T(8,128)(2,1)S(1)} %get-tuple-element.30.own_ref), channel_id=1, source_target_pairs={{0,48},{8,24},{16,0},{24,40},{32,16},{40,56},{48,32},{56,8},{64,11... | collective-permute-start | bytes 49160 | tf_op jit(solution)/shard_map/ppermute | solution.py:390
  37.0 4.2 %collective-permute-start.6 = (bf16[8,1024]{1,0:T(8,128)(2,1)S(1)}, bf16[8,1024]{1,0:T(8,128)(2,1)S(1)}, u32[]{:S(2)}, u32[]{:S(2)}) collective-permute-start(bf16[8,1024]{1,0:T(8,128)(2,1)S(1)} %get-tuple-element.30.own_ref), channel_id=1, source_target_pairs={{0,56},{8,16},{16,8},{24,32},{32,24},{40,48},{48,40},{56,0},{64,12... | collective-permute-start | bytes 49160 | tf_op jit(solution)/shard_map/ppermute | solution.py:390
  54.5 24.6 %collective-permute-start.11 = (bf16[2,2,1024,128]{3,2,1,0:T(8,128)(2,1)S(1)}, bf16[2,2,1024,128]{3,2,1,0:T(8,128)(2,1)S(1)}, u32[]{:S(2)}, u32[]{:S(2)}) collective-permute-start(bf16[2,2,1024,128]{3,2,1,0:T(8,128)(2,1)S(1)} %get-tuple-element.34), channel_id=1, source_target_pairs={{1,9},{3,11},{5,13},{7,15},{9,1},{11,3},{13,5},{15,7},{17,25},{19,... | collective-permute-start | bytes 3145736 | tf_op jit(solution)/shard_map/ppermute | solution.py:369
  64.9 13.4 %collective-permute-start.10 = (f32[8,8,128]{2,1,0:T(8,128)S(1)}, f32[8,8,128]{2,1,0:T(8,128)S(1)}, u32[]{:S(2)}, u32[]{:S(2)}) collective-permute-start(f32[8,8,128]{2,1,0:T(8,128)S(1)} %all_to_all.11.part_ref), channel_id=1, source_target_pairs={{0,1},{2,3},{4,5},{6,7},{8,9},{10,11},{12,13},{14,15},{16,17},{18,... | collective-permute-start | bytes 98312 | tf_op jit(solution)/shard_map/ppermute | solution.py:500

commit v3 on v2

v3 whole, which is shorter than its diff:
```python
import functools
import math

import jax
import jax.numpy as jnp
from jax import lax
from jax.experimental import pallas as pl
from jax.experimental.pallas import tpu as pltpu
from jax.sharding import PartitionSpec as P

D_GEN = 8192
MOST = 4
BD = 8
CACHE = 1024
HD = 128
GH = 8
F32 = jnp.float32
BF16 = jnp.bfloat16
VM = pltpu.VMEM
SM = pltpu.SMEM
HB = pltpu.HBM


def spec(space):
    return pl.BlockSpec(memory_space=space)


def needed(par_ref, slots_at, half):
    flags = []
    for b in range(BD):
        want = half * BD + b
        hit = par_ref[slots_at] == want
        for j in range(1, BD):
            hit = hit | (par_ref[slots_at + j] == want)
        flags.append(hit)
    return flags


def ranked(flags):
    ranks = []
    rank = jnp.int32(0)
    for flag in flags:
        ranks.append(rank)
        rank = rank + flag.astype(jnp.int32)
    return ranks, rank


def message_kernel(fin_ref, q_ref, kv_ref, msg_ref):
    for s in range(BD):
        step = kv_ref[1, s].astype(F32)
        flag = jnp.full((1, HD), fin_ref[s], jnp.int32).astype(F32)
        msg_ref[s] = jnp.concatenate(
            [q_ref[1, s].astype(F32), step, flag, jnp.zeros((5, HD), F32)], axis=0
        ).astype(BF16)


def pack_kernel(par_ref, cache_ref, w_ref, head_ref, after_ref, a_ref, wext_ref, sems, wsem):
    me = lax.axis_index("dp")
    half = lax.rem(me, 2)
    start = (me - half) * BD + (1 - half) * BD
    flags = needed(par_ref, start, half)
    ranks, total = ranked(flags)
    early = a_ref.shape[0]
    for b in range(BD):
        for r in range(min(b + 1, early)):

            @pl.when(flags[b] & (ranks[b] == r))
            def _():
                pltpu.make_async_copy(cache_ref.at[b], a_ref.at[r], sems.at[r]).start()

    rows = w_ref.shape[0]
    wcopy = pltpu.make_async_copy(w_ref, wext_ref.at[pl.ds(0, rows)], wsem)
    wcopy.start()
    wext_ref[pl.ds(rows, 16), :] = jnp.broadcast_to(head_ref[...].astype(F32), (16, HD)).astype(BF16)
    wcopy.wait()
    for r in range(early):

        @pl.when(r < total)
        def _():
            pltpu.make_async_copy(cache_ref.at[0], a_ref.at[r], sems.at[r]).wait()


OWN = BD * GH
ALL = OWN + MOST * GH
ROWS = ALL + 2 * GH


def attend_kernel(
    par_ref, len_ref, fin_ref, cache_ref, q_ref, kv_ref, msg_ref,
    first_ref, own_ref, swap_ref, rows_ref, meta_ref, pick_ref, late_ref, newc_ref,
    q2s, q1s, e1s, v1s, pcol, fscr, acc, rscr, crow, outsem, sendsem,
):
    me = lax.axis_index("dp")
    half = lax.rem(me, 2)
    pair = (me - half) * BD
    mine = pair + half * BD
    theirs = pair + (1 - half) * BD
    scaling = math.log2(math.e) / math.sqrt(HD)
    wanted = needed(par_ref, theirs, half)
    send_ranks, send_total = ranked(wanted)
    skip = MOST - late_ref.shape[0]
    for b in range(BD):
        for r in range(skip, min(b + 1, MOST)):

            @pl.when(wanted[b] & (send_ranks[b] == r))
            def _():
                pltpu.make_async_copy(cache_ref.at[b], late_ref.at[r - skip], sendsem.at[r]).start()

    own_local = []
    for s in range(BD):
        local = par_ref[mine + s] - half * BD
        here = (local >= 0) & (local < BD)
        own_local.append(jnp.where(here, local, -1))

        @pl.when(here)
        def _():
            pltpu.make_async_copy(
                cache_ref.at[jnp.clip(local, 0, BD - 1)], newc_ref.at[s], outsem.at[s]
            ).start()

    slots = [jnp.int32(0)] * MOST
    locals_ = [jnp.int32(-1)] * MOST
    count = jnp.int32(0)
    for s in range(BD):
        local = par_ref[theirs + s] - half * BD
        here = (local >= 0) & (local < BD)
        for j in range(min(s + 1, MOST)):
            take = here & (count == j)
            slots[j] = jnp.where(take, s, slots[j])
            locals_[j] = jnp.where(take, local, locals_[j])
        count = count + here.astype(jnp.int32)
    q1s[...] = jnp.zeros_like(q1s)
    for b in range(BD):
        q1s[b, 0:GH, :] = q_ref[0, b]
    e1s[pl.ds(ALL, 2 * GH), :] = jnp.full((2 * GH, HD), -1e30, F32)
    v1s[pl.ds(ALL, 2 * GH), :] = jnp.zeros((2 * GH, HD), F32)
    for s in range(BD + MOST):
        rows = pl.ds(s * GH, GH)
        if s < BD:
            q = q_ref[1, s].astype(F32)
            step = kv_ref[1, s].astype(F32)
            parent = own_local[s]
        else:
            block = msg_ref[slots[s - BD]].astype(F32)
            q = block[0:GH]
            step = block[GH : GH + 2]
            parent = locals_[s - BD]
        pcol[rows, :] = jnp.full((GH, HD), parent, jnp.int32)
        q2s[rows, :] = q
        e1s[rows, :] = jnp.broadcast_to(
            jnp.sum(q * step[0:1], axis=1, keepdims=True) * scaling, (GH, HD)
        )
        v1s[rows, :] = jnp.broadcast_to(step[1:2], (GH, HD))
    q2 = q2s[...].astype(BF16)
    acc[...] = jnp.zeros_like(acc)
    places = lax.broadcasted_iota(jnp.int32, (1, CACHE), 1)
    for b in range(BD):
        bias = jnp.where(places < len_ref[mine + b], 0.0, -1e30)
        q = jnp.concatenate([q2, q1s[b]], axis=0)
        logits = lax.dot_general(
            q, cache_ref[b, 0], (((1,), (1,)), ((), ())), preferred_element_type=F32
        ) * scaling + bias
        step = kv_ref[0, b].astype(F32)
        e0 = jnp.sum(q.astype(F32) * step[0:1], axis=1, keepdims=True) * scaling
        e1 = e1s[:, 0:1]
        peak = jnp.maximum(jnp.maximum(jnp.max(logits, axis=1, keepdims=True), e0), e1)
        p = jnp.exp2(logits - peak)
        p0 = jnp.exp2(e0 - peak)
        p1 = jnp.exp2(e1 - peak)
        inv = 1.0 / (jnp.sum(p, axis=1, keepdims=True) + p0 + p1)
        mixed = jnp.dot((p * inv).astype(BF16), cache_ref[b, 1], preferred_element_type=F32)
        mixed = mixed + (p0 * inv).astype(BF16).astype(F32) * step[1:2]
        mixed = mixed + (p1 * inv).astype(BF16).astype(F32) * v1s[...]
        fscr[b * GH : (b + 1) * GH, :] = mixed[ALL : ALL + GH]
        acc[...] = jnp.where(pcol[...] == b, mixed[:ALL], acc[...])
    rscr[...] = jnp.zeros_like(rscr)
    at = pl.multiple_of(half * BD, BD)
    their = pl.multiple_of((1 - half) * BD, BD)
    for h in range(GH):
        lanes = slice(h * HD, (h + 1) * HD)
        first_ref[:, lanes] = fscr[pl.ds(h, BD, stride=GH), :].astype(BF16)
        rscr[pl.ds(at, BD), lanes] = acc[pl.ds(h, BD, stride=GH), :].astype(BF16).astype(F32)
        crow[0:MOST, lanes] = acc[pl.ds(OWN + h, MOST, stride=GH), :].astype(BF16).astype(F32)
    for j in range(MOST):

        @pl.when(j < count)
        def _():
            rscr[pl.ds(their + slots[j], 1), :] = crow[j : j + 1, :]

    lane = lax.broadcasted_iota(jnp.int32, (BD, HD), 1)
    flags = jnp.zeros((BD, HD), F32)
    for s in range(BD):
        theirs_flag = msg_ref[s].astype(F32)[GH + 2 : GH + 3, :]
        flags = jnp.where(lane == their + s, theirs_flag, flags)
        flags = jnp.where(lane == at + s, fin_ref[s].astype(F32), flags)
    before = flags
    for k in range(4):
        moved = pltpu.roll(before, 1 << k, 1)
        before = before + jnp.where(lane >= 1 << k, moved, 0.0)
    rank = lax.broadcasted_iota(jnp.int32, (BD, HD), 0).astype(F32)
    pick = jnp.where((flags > 0.5) & (before - 1.0 == rank), 1.0, 0.0)
    packed = jnp.dot(
        pick[:, 0 : 2 * BD].astype(BF16), rscr[...].astype(BF16), preferred_element_type=F32
    )
    pick_ref[...] = pltpu.roll(pick, jnp.where(half == 1, HD - BD, 0), 1)
    own_ref[...] = rscr[pl.ds(at, BD), :].astype(BF16)
    rows_ref[...] = packed.astype(BF16)
    swap_ref[...] = jnp.concatenate([rscr[pl.ds(their, BD), :], packed], axis=0).astype(BF16)
    ranks, _ = ranked(needed(par_ref, mine, 1 - half))
    for s in range(BD):
        local = par_ref[mine + s] - (1 - half) * BD
        slot = jnp.int32(-1)
        for b in range(BD):
            slot = jnp.where(local == b, ranks[b], slot)
        meta_ref[s : s + 1, :] = jnp.full((1, HD), slot, jnp.int32)
    for r in range(skip, MOST):

        @pl.when(r < send_total)
        def _():
            pltpu.make_async_copy(cache_ref.at[0], late_ref.at[0], sendsem.at[r]).wait()

    for s in range(BD):

        @pl.when(own_local[s] >= 0)
        def _():
            pltpu.make_async_copy(cache_ref.at[0], newc_ref.at[s], outsem.at[s]).wait()


def place_start(first, meta_ref, recv_ref, newc_ref, sems):
    crossing = []
    count = recv_ref.shape[0]
    for s in range(BD):
        slot = meta_ref[s : s + 1, :][0, 0] - first
        cross = (slot >= 0) & (slot < count)
        slot = jnp.clip(slot, 0, count - 1)
        crossing.append(cross)

        @pl.when(cross)
        def _():
            pltpu.make_async_copy(recv_ref.at[slot], newc_ref.at[s], sems.at[s]).start()

    return crossing


def place_wait(crossing, recv_ref, newc_ref, sems):
    for s in range(BD):

        @pl.when(crossing[s])
        def _():
            pltpu.make_async_copy(recv_ref.at[0], newc_ref.at[s], sems.at[s]).wait()


def place_kernel(first, meta_ref, recv_ref, *refs):
    newc_ref, sems = refs[-2:]
    waits = place_start(first, meta_ref, recv_ref, newc_ref, sems)
    place_wait(waits, recv_ref, newc_ref, sems)


def gate_kernel(*refs):
    del refs


def join_kernel(own_ref, rows_ref, swap_ref, meta_ref, recv_ref, *refs):
    second_ref, full_ref, _, newc_ref, sems = refs[-5:]
    waits = place_start(0, meta_ref, recv_ref, newc_ref, sems)
    second_ref[...] = own_ref[...] + swap_ref[0:BD, :]
    full_ref[...] = rows_ref[...] + swap_ref[BD : 2 * BD, :]
    place_wait(waits, recv_ref, newc_ref, sems)


def hidden_kernel(own_ref, r1, r2, r3, w0, w1, w2, w3, out_ref):
    depth = w0.shape[0] - 16
    odd = lax.rem(lax.axis_index("dp"), 2) == 1
    near, far = r1[...].astype(F32), r2[...].astype(F32)
    rows = jnp.concatenate(
        [
            own_ref[...].astype(F32),
            jnp.where(odd, near, far),
            r3[...].astype(F32),
            jnp.where(odd, far, near),
        ],
        axis=0,
    )
    narrow = rows.astype(BF16)
    parts = [
        jnp.dot(narrow, w[0:depth, :], preferred_element_type=F32) for w in (w0, w1, w2, w3)
    ]
    squares = jnp.sum(rows * rows, axis=1, keepdims=True)
    parts.append(jnp.broadcast_to(squares, (rows.shape[0], HD)))
    for k in range(out_ref.shape[0]):
        for i, part in enumerate(parts):
            out_ref[k, :, i * HD : (i + 1) * HD] = part.astype(out_ref.dtype)


def score_kernel(hid_ref, w0, w1, w2, w3, out_ref):
    depth = w0.shape[0] - 16
    total = hid_ref[0].astype(F32)
    for k in range(1, hid_ref.shape[0]):
        total = total + hid_ref[k].astype(F32)
    factor = lax.rsqrt(total[:, 4 * HD : 4 * HD + 1] / D_GEN + 1e-05)
    sums = jnp.zeros((total.shape[0], 1), F32)
    for i, w in enumerate((w0, w1, w2, w3)):
        head = w[depth : depth + 16, :].astype(F32)[0:1, :]
        v = total[:, i * HD : (i + 1) * HD] * factor
        sums = sums + jnp.sum(v / (1.0 + jnp.exp(-v)) * head, axis=1, keepdims=True)
    wide = jnp.broadcast_to(sums, (total.shape[0], HD))
    pairs = out_ref.shape[0]
    mine = lax.rem(lax.axis_index("dp") // 2, pairs)
    for q in range(pairs):
        out_ref[lax.rem(mine + q, pairs)] = wide[q * BD : (q + 1) * BD]


def add_kernel(a_ref, b_ref, out_ref):
    out_ref[...] = a_ref[...] + b_ref[...]


def final_kernel(pick_ref, a_ref, b_ref, out_ref):
    pair = lax.rem(lax.axis_index("dp") // 2, a_ref.shape[0])
    total = a_ref[pair] + b_ref[pair]
    sums = jnp.sum(pick_ref[...] * total, axis=0, keepdims=True)
    for s in range(BD):
        out_ref[s] = sums[0, s]


def call(kernel, outs, ins, out_specs, scratch=(), aliases=None, cost=None, limit=60):
    return functools.partial(
        pl.pallas_call,
        kernel,
        out_shape=outs,
        in_specs=[spec(s) for s in ins],
        out_specs=[spec(s) for s in out_specs],
        scratch_shapes=list(scratch),
        input_output_aliases=aliases or {},
        compiler_params=pltpu.CompilerParams(vmem_limit_bytes=limit * 1024 * 1024),
        cost_estimate=pl.CostEstimate(flops=cost or 1000000, bytes_accessed=cost or 1000000, transcendentals=0),
    )()


def shape(dims, dtype):
    return jax.ShapeDtypeStruct(dims, dtype)


def swap(array):
    return lax.ppermute(array, "dp", [(i, i ^ 1) for i in range(lax.axis_size("dp"))])


def place(first, meta, recv, newc):
    return call(
        functools.partial(place_kernel, first),
        [shape(newc.shape, BF16)],
        [VM, VM, HB],
        [HB],
        [pltpu.SemaphoreType.DMA((BD,))],
        aliases={2: 0},
        limit=16,
    )(meta, recv, newc)[0]


def away(array, nz, k):
    nd = lax.axis_size("dp")
    pairs = []
    for d in range(nd):
        z = d % nz
        pairs.append((d, d - z + (z - k if z % 2 == 0 else z + k) % nz))
    return lax.ppermute(array, "dp", pairs)


EARLY = 1


def per_device(nx, nz, cache_kv, lengths, step_kv, queries, parents, finished, reward_in, reward_head):
    ndp = nx * nz
    nt = lax.axis_size("tensor")
    cache = cache_kv.reshape(BD, 2, CACHE, HD)
    kv = step_kv.reshape(2, BD, 2, HD)
    depth = reward_in.shape[0]
    part_a = shape((EARLY, 2, CACHE, HD), BF16)
    part_b = shape((MOST - EARLY, 2, CACHE, HD), BF16)
    (msg,) = call(
        message_kernel, [shape((BD, 16, HD), BF16)], [SM, VM, VM], [VM], limit=60, cost=100000
    )(finished, queries, kv)
    recv_msg = swap(msg)
    early, wext = call(
        pack_kernel,
        [part_a, shape((depth + 16, HD), BF16)],
        [SM, HB, HB, VM, pl.ANY],
        [VM, VM],
        [pltpu.SemaphoreType.DMA((EARLY,)), pltpu.SemaphoreType.DMA],
        limit=58,
        cost=20000000,
    )(parents, cache, reward_in, reward_head.reshape(1, HD), msg)
    (early,) = call(
        gate_kernel, [part_a], [pl.ANY, pl.ANY], [pl.ANY], aliases={0: 0}, limit=16, cost=1000
    )(early, recv_msg)
    recv_early = swap(early)
    others = [
        lax.ppermute(wext, "dp", [(i, (i + nz * k) % ndp) for i in range(ndp)]) for k in range(1, nx)
    ]
    first_out, own_out, to_swap, rows, meta, pick, late, newc = call(
        attend_kernel,
        [
            shape((BD, GH * HD), BF16),
            shape((BD, GH * HD), BF16),
            shape((2 * BD, GH * HD), BF16),
            shape((BD, GH * HD), BF16),
            shape((BD, HD), jnp.int32),
            shape((BD, HD), F32),
            part_b,
            shape((BD, 2, CACHE, HD), BF16),
        ],
        [SM, SM, SM, VM, VM, VM, VM],
        [VM] * 7 + [HB],
        [
            VM((ALL, HD), F32),
            VM((BD, 2 * GH, HD), BF16),
            VM((ROWS, HD), F32),
            VM((ROWS, HD), F32),
            VM((ALL, HD), jnp.int32),
            VM((OWN, HD), F32),
            VM((ALL, HD), F32),
            VM((2 * BD, GH * HD), F32),
            VM((BD, GH * HD), F32),
            pltpu.SemaphoreType.DMA((BD,)),
            pltpu.SemaphoreType.DMA((MOST,)),
        ],
        cost=20000000,
        limit=32,
    )(parents, lengths, finished, cache, queries, kv, recv_msg)
    second_out, rows, late, newc = call(
        join_kernel,
        [shape(own_out.shape, BF16), shape(rows.shape, BF16), part_b, shape(newc.shape, BF16)],
        [VM] * 5 + [pl.ANY, HB, pl.ANY, pl.ANY, pl.ANY],
        [VM, VM, pl.ANY, HB],
        [pltpu.SemaphoreType.DMA((BD,))],
        aliases={5: 2, 6: 3},
        limit=16,
    )(own_out, rows, swap(to_swap), meta, recv_early, late, newc, *others)
    recv_late = swap(late)
    (partial,) = call(
        hidden_kernel, [shape((nt, nz // 2 * BD, 5 * HD), BF16)], [VM] * 8, [VM], limit=16
    )(rows, *[away(rows, nz, k) for k in (1, 2, 3)], wext, *others)
    partials = lax.all_to_all(partial, "tensor", 0, 0, tiled=True)
    (sums,) = call(
        score_kernel, [shape((nz // 2, BD, HD), F32)], [VM] * 5, [VM], limit=16
    )(partials, wext, *others)
    for k in (1, 2):
        (sums,) = call(add_kernel, [shape(sums.shape, F32)], [VM, VM], [VM], limit=16)(
            sums, away(sums, nz, k)
        )
    (scores,) = call(
        final_kernel, [shape((BD,), F32)], [VM, VM, VM], [SM], limit=16
    )(pick, sums, away(sums, nz, 3))
    newc = place(EARLY, meta, recv_late, newc)
    return (first_out, second_out, scores, newc.reshape(cache_kv.shape))


def solution(mesh):
    ndp = mesh.shape["dp"]
    nx = 4
    return jax.shard_map(
        functools.partial(per_device, nx, ndp // nx),
        mesh=mesh,
        in_specs=(
            P("dp", None, None, "tensor", None),
            P(),
            P(None, "dp", None, "tensor", None),
            P(None, "dp", "tensor", None),
            P(),
            P("dp"),
            P("tensor", "dp"),
            P("dp"),
        ),
        out_specs=(
            P("dp", "tensor"),
            P("dp", "tensor"),
            P("dp"),
            P("dp", None, None, "tensor", None),
        ),
        check_vma=False,
    )
```

time: 79.4 us -> 70.3 us (0.89)
  the two profiles are of different devices: /device:TPU:17 before, /device:TPU:32 now
where the time goes in v3:
time: 70.3 us; the launch traced here: 70 us
  starting transfers between devices  27.7 us (39%)
  Pallas kernels  15 us (21%)
  waiting for transfers between devices  14.1 us (20%)
  blocking collectives  12.5 us (18%)
  between operations  0.78 us (1%)
    ppermute x6, starting transfers between devices, away(): return lax.ppermute(array, 'dp', pairs)  18.7 us
    all_to_all x1, blocking collectives, per_device(): partials = lax.all_to_all(partial, 'tensor', 0, 0, tiled=True)  12.5 us
    ppermute x6, waiting for transfers between devices, away(): return lax.ppermute(array, 'dp', pairs)  9.94 us
    pallas_call x1, Pallas kernels, per_device(): call(attend_kernel, [shape((BD, GH * HD), BF16), shape((BD, GH * HD), BF1...  6.93 us
    ppermute x4, starting transfers between devices, swap(): lax.ppermute(array, 'dp', [(i, i ^ 1) for i in range(lax.axis_size('dp'))])  5.64 us
    ppermute x3, starting transfers between devices, per_device(): lax.ppermute(wext, 'dp', [(i, (i + nz * k) % ndp) for i in range(ndp)])  3.35 us
    pallas_call x1, Pallas kernels, per_device(): call(pack_kernel, [part_a, shape((depth + 16, HD), BF16)], [SM, HB, HB, V...  2.73 us
    ppermute x4, waiting for transfers between devices, swap(): lax.ppermute(array, 'dp', [(i, i ^ 1) for i in range(lax.axis_size('dp'))])  2.25 us
  transfers between devices with their start and end apart: 13, of which 6 were waited for; matrix products, arithmetic and copies ran while one was open for 0% of the time, Pallas kernels for 15%

profile of v3, /device:TPU:32, one launch (start us, length us, event | category | flops | bytes accessed | tf_op | source)
XLA Modules:
  0.0 70.0 jit_solution(11255176318070219373)
XLA Ops:
  0.7 1.4 %shard_map.111.after_ref = bf16[8,16,128]{2,1,0:T(8,128)(2,1)} custom-call(s32[8]{0:T(128)} %fin_ref.3, bf16[2,8,8,128]{3,2,1,0:T(8,128)(2,1)} %q_ref.3, bf16[2,8,2,128]{3,2,1,0:T(2,128)(2,1)} %bitcast.8), custom_call_target="tpu_custom_call" | custom-call | flops 100000 | bytes 100000 | tf_op jit(solution)/shard_map/pallas_call | solution.py:379
  2.1 1.8 %collective-permute-start = (bf16[8,16,128]{2,1,0:T(8,128)(2,1)}, bf16[8,16,128]{2,1,0:T(8,128)(2,1)S(1)}, u32[]{:S(2)}, u32[]{:S(2)}) collective-permute-start(bf16[8,16,128]{2,1,0:T(8,128)(2,1)} %shard_map.111.after_ref), channel_id=1, source_target_pairs={{0,8},{8,0},{16,24},{24,16},{32,40},{40,32},{48,56},{56,48},{64,72... | collective-permute-start | bytes 98312 | tf_op jit(solution)/shard_map/ppermute | solution.py:344
  4.0 2.7 %shard_map.113 = (bf16[1,2,1024,128]{3,2,1,0:T(8,128)(2,1)}, bf16[1040,128]{1,0:T(8,128)(2,1)}) custom-call(s32[256]{0:T(256)} %par_ref.3, bf16[8,2,1024,128]{3,2,1,0:T(8,128)(2,1)} %bitcast.6, bf16[1024,128]{1,0:T(8,128)(2,1)} %w_ref.1, bf16[1,128]{1,0:T(2,128)(2,1)} %bitcast.11, bf16[8,16,128]{2,1,0:T(8,128)(2,1)} %shard_map.111.after_ref), custom_call_target="tpu_custom_call" | custom-call | flops 20000000 | bytes 20000000 | tf_op jit(solution)/shard_map/pallas_call | solution.py:383
  6.7 1.4 %collective-permute-start.2 = (bf16[1,2,1024,128]{3,2,1,0:T(8,128)(2,1)}, bf16[1,2,1024,128]{3,2,1,0:T(8,128)(2,1)S(1)}, u32[]{:S(2)}, u32[]{:S(2)}) collective-permute-start(bf16[1,2,1024,128]{3,2,1,0:T(8,128)(2,1)} %shard_map.114), channel_id=1, source_target_pairs={{0,8},{8,0},{16,24},{24,16},{32,40},{40,32},{48,56},{56,48},{64,72... | collective-permute-start | bytes 1572872 | tf_op jit(solution)/shard_map/ppermute | solution.py:344
  8.1 1.5 %collective-permute-start.5 = (bf16[1040,128]{1,0:T(8,128)(2,1)}, bf16[1040,128]{1,0:T(8,128)(2,1)S(1)}, u32[]{:S(2)}, u32[]{:S(2)}) collective-permute-start(bf16[1040,128]{1,0:T(8,128)(2,1)} %get-tuple-element.26.w0), channel_id=1, source_target_pairs={{0,192},{8,200},{16,208},{24,216},{32,224},{40,232},{48,240},{56,2... | collective-permute-start | bytes 798728 | tf_op jit(solution)/shard_map/ppermute | solution.py:397
  9.6 0.8 %collective-permute-start.4 = (bf16[1040,128]{1,0:T(8,128)(2,1)}, bf16[1040,128]{1,0:T(8,128)(2,1)S(1)}, u32[]{:S(2)}, u32[]{:S(2)}) collective-permute-start(bf16[1040,128]{1,0:T(8,128)(2,1)} %get-tuple-element.26.w0), channel_id=1, source_target_pairs={{0,128},{8,136},{16,144},{24,152},{32,160},{40,168},{48,176},{56,1... | collective-permute-start | bytes 798728 | tf_op jit(solution)/shard_map/ppermute | solution.py:397
  10.4 1.1 %collective-permute-start.3 = (bf16[1040,128]{1,0:T(8,128)(2,1)}, bf16[1040,128]{1,0:T(8,128)(2,1)S(1)}, u32[]{:S(2)}, u32[]{:S(2)}) collective-permute-start(bf16[1040,128]{1,0:T(8,128)(2,1)} %get-tuple-element.26.w0), channel_id=1, source_target_pairs={{0,64},{8,72},{16,80},{24,88},{32,96},{40,104},{48,112},{56,120},{... | collective-permute-start | bytes 798728 | tf_op jit(solution)/shard_map/ppermute | solution.py:397
  11.5 6.9 %shard_map.112 = (bf16[8,1024]{1,0:T(8,128)(2,1)}, bf16[8,1024]{1,0:T(8,128)(2,1)S(1)}, bf16[16,1024]{1,0:T(8,128)(2,1)S(1)}, bf16[8,1024]{1,0:T(8,128)(2,1)S(1)...) custom-call(s32[256]{0:T(256)S(1)} %copy-done.4, ...), custom_call_target="tpu_custom_call" | custom-call | flops 20000000 | bytes 20000000 | tf_op jit(solution)/shard_map/pallas_call | solution.py:399
  18.4 1.8 %collective-permute-start.1 = (bf16[16,1024]{1,0:T(8,128)(2,1)S(1)}, bf16[16,1024]{1,0:T(8,128)(2,1)S(1)}, u32[]{:S(2)}, u32[]{:S(2)}) collective-permute-start(bf16[16,1024]{1,0:T(8,128)(2,1)S(1)} %get-tuple-element.21), channel_id=1, source_target_pairs={{0,8},{8,0},{16,24},{24,16},{32,40},{40,32},{48,56},{56,48},{64,72... | collective-permute-start | bytes 98312 | tf_op jit(solution)/shard_map/ppermute | solution.py:344
  20.2 2.2 %collective-permute-done.1.swap_ref = bf16[16,1024]{1,0:T(8,128)(2,1)S(1)} collective-permute-done((bf16[16,1024]{1,0:T(8,128)(2,1)S(1)}, bf16[16,1024]{1,0:T(8,128)(2,1)S(1)}, u32[]{:S(2)}, u32[]{:S(2)}) %collective-permute-start.1) | collective-permute-done | bytes 32800 | tf_op jit(solution)/shard_map/ppermute | solution.py:344
  22.4 1.9 %collective-permute-done.3.refs_2_.w1 = bf16[1040,128]{1,0:T(8,128)(2,1)S(1)} collective-permute-done((bf16[1040,128]{1,0:T(8,128)(2,1)}, bf16[1040,128]{1,0:T(8,128)(2,1)S(1)}, u32[]{:S(2)}, u32[]{:S(2)}) %collective-permute-start.3) | collective-permute-done | bytes 266272 | tf_op jit(solution)/shard_map/ppermute | solution.py:397
  24.3 1.7 %shard_map.115 = (bf16[8,1024]{1,0:T(8,128)(2,1)}, bf16[8,1024]{1,0:T(8,128)(2,1)S(1)}, bf16[3,2,1024,128]{3,2,1,0:T(8,128)(2,1)S(1)}, bf16[8,2,1024,128]{3,2,1,0:T(8,128)(2,1)}) custom-call(bf16[8,1024]{1,0:T(8,128)(2,1)S(1)} %get-tuple-element.19.own_ref, ...), custom_call_target="tpu_custom_call", output_to_operand_aliasing={{2}: (5, {}), {3}: (6, {})} | custom-call | flops 1000000 | bytes 1000000 | tf_op jit(solution)/shard_map/pallas_call | solution.py:429
  26.6 5.8 %collective-permute-start.8 = (bf16[8,1024]{1,0:T(8,128)(2,1)S(1)}, bf16[8,1024]{1,0:T(8,128)(2,1)S(1)}, u32[]{:S(2)}, u32[]{:S(2)}) collective-permute-start(bf16[8,1024]{1,0:T(8,128)(2,1)S(1)} %get-tuple-element.29.own_ref), channel_id=1, source_target_pairs={{0,40},{8,32},{16,56},{24,48},{32,8},{40,0},{48,24},{56,16},{64,10... | collective-permute-start | bytes 49160 | tf_op jit(solution)/shard_map/ppermute | solution.py:365
  32.5 1.5 %collective-permute-start.7 = (bf16[8,1024]{1,0:T(8,128)(2,1)S(1)}, bf16[8,1024]{1,0:T(8,128)(2,1)S(1)}, u32[]{:S(2)}, u32[]{:S(2)}) collective-permute-start(bf16[8,1024]{1,0:T(8,128)(2,1)S(1)} %get-tuple-element.29.own_ref), channel_id=1, source_target_pairs={{0,48},{8,24},{16,0},{24,40},{32,16},{40,56},{48,32},{56,8},{64,11... | collective-permute-start | bytes 49160 | tf_op jit(solution)/shard_map/ppermute | solution.py:365
  34.0 1.7 %collective-permute-start.6 = (bf16[8,1024]{1,0:T(8,128)(2,1)S(1)}, bf16[8,1024]{1,0:T(8,128)(2,1)S(1)}, u32[]{:S(2)}, u32[]{:S(2)}) collective-permute-start(bf16[8,1024]{1,0:T(8,128)(2,1)S(1)} %get-tuple-element.29.own_ref), channel_id=1, source_target_pairs={{0,56},{8,16},{16,8},{24,32},{32,24},{40,48},{48,40},{56,0},{64,12... | collective-permute-start | bytes 49160 | tf_op jit(solution)/shard_map/ppermute | solution.py:365
  35.7 2.7 %collective-permute-done.7.r2 = bf16[8,1024]{1,0:T(8,128)(2,1)S(1)} collective-permute-done((bf16[8,1024]{1,0:T(8,128)(2,1)S(1)}, bf16[8,1024]{1,0:T(8,128)(2,1)S(1)}, u32[]{:S(2)}, u32[]{:S(2)}) %collective-permute-start.7) | collective-permute-done | bytes 16416 | tf_op jit(solution)/shard_map/ppermute | solution.py:365
  38.7 12.5 %all_to_all.5.hid_ref = bf16[8,32,640]{2,1,0:T(8,128)(2,1)S(1)} all-to-all(bf16[8,32,640]{2,1,0:T(8,128)(2,1)S(1)} %shard_map.116), channel_id=1, replica_groups=mesh['dp'=32,'tensor'=8] {'tensor'}, dimensions={0} | all-to-all | bytes 655360 | tf_op jit(solution)/shard_map/all_to_all | solution.py:442
  51.4 2.0 %collective-permute-start.9 = (f32[4,8,128]{2,1,0:T(8,128)S(1)}, f32[4,8,128]{2,1,0:T(8,128)S(1)}, u32[]{:S(2)}, u32[]{:S(2)}) collective-permute-start(f32[4,8,128]{2,1,0:T(8,128)S(1)} %shard_map.117.a_ref), channel_id=1, source_target_pairs={{0,56},{8,16},{16,8},{24,32},{32,24},{40,48},{48,40},{56,0},{64,12... | collective-permute-start | bytes 49160 | tf_op jit(solution)/shard_map/ppermute | solution.py:365
  53.5 1.8 %collective-permute-done.9.b_ref = f32[4,8,128]{2,1,0:T(8,128)S(1)} collective-permute-done((f32[4,8,128]{2,1,0:T(8,128)S(1)}, f32[4,8,128]{2,1,0:T(8,128)S(1)}, u32[]{:S(2)}, u32[]{:S(2)}) %collective-permute-start.9) | collective-permute-done | bytes 16416 | tf_op jit(solution)/shard_map/ppermute | solution.py:365
  55.3 3.2 %collective-permute-start.10 = (f32[4,8,128]{2,1,0:T(8,128)S(1)}, f32[4,8,128]{2,1,0:T(8,128)S(1)}, u32[]{:S(2)}, u32[]{:S(2)}) collective-permute-start(f32[4,8,128]{2,1,0:T(8,128)S(1)} %shard_map.118.a_ref), channel_id=1, source_target_pairs={{0,48},{8,24},{16,0},{24,40},{32,16},{40,56},{48,32},{56,8},{64,11... | collective-permute-start | bytes 49160 | tf_op jit(solution)/shard_map/ppermute | solution.py:365
  58.5 3.0 %collective-permute-done.10.b_ref = f32[4,8,128]{2,1,0:T(8,128)S(1)} collective-permute-done((f32[4,8,128]{2,1,0:T(8,128)S(1)}, f32[4,8,128]{2,1,0:T(8,128)S(1)}, u32[]{:S(2)}, u32[]{:S(2)}) %collective-permute-start.10) | collective-permute-done | bytes 16416 | tf_op jit(solution)/shard_map/ppermute | solution.py:365
  61.5 4.3 %collective-permute-start.11 = (f32[4,8,128]{2,1,0:T(8,128)S(1)}, f32[4,8,128]{2,1,0:T(8,128)S(1)}, u32[]{:S(2)}, u32[]{:S(2)}) collective-permute-start(f32[4,8,128]{2,1,0:T(8,128)S(1)} %shard_map.119.a_ref), channel_id=1, source_target_pairs={{0,40},{8,32},{16,56},{24,48},{32,8},{40,0},{48,24},{56,16},{64,10... | collective-permute-start | bytes 49160 | tf_op jit(solution)/shard_map/ppermute | solution.py:365
  65.9 2.4 %collective-permute-done.11.b_ref = f32[4,8,128]{2,1,0:T(8,128)S(1)} collective-permute-done((f32[4,8,128]{2,1,0:T(8,128)S(1)}, f32[4,8,128]{2,1,0:T(8,128)S(1)}, u32[]{:S(2)}, u32[]{:S(2)}) %collective-permute-start.11) | collective-permute-done | bytes 16416 | tf_op jit(solution)/shard_map/ppermute | solution.py:365
  68.9 1.1 %shard_map.121 = bf16[8,2,1024,128]{3,2,1,0:T(8,128)(2,1)} custom-call(s32[8,128]{1,0:T(8,128)S(1)} %get-tuple-element.22.meta_ref, bf16[3,2,1024,128]{3,2,1,0:T(8,128)(2,1)S(1)} %collective-permute-done.12.recv_ref, bf16[8,2,1024,128]{3,2,1,0:T(8,128)(2,1)} %get-tuple-element.31.refs_0_), custom_call_target="tpu_custom_call", output_to_operand_aliasing={{}: (2, {})} | custom-call | flops 1000000 | bytes 1000000 | tf_op jit(solution)/shard_map/pallas_call | solution.py:348
  (28 shorter events, 1.9 us)
Async XLA Ops:
  0.6 10.8 %copy-start.5 = (s32[8]{0:T(128)S(1)}, s32[8]{0:T(128)}, u32[]{:S(2)}) copy-start(s32[8]{0:T(128)} %fin_ref.3) | copy-start | bytes 100
  0.6 10.8 %copy-start.2 = (bf16[2,8,8,128]{3,2,1,0:T(8,128)(2,1)S(1)}, bf16[2,8,8,128]{3,2,1,0:T(8,128)(2,1)}, u32[]{:S(2)}) copy-start(bf16[2,8,8,128]{3,2,1,0:T(8,128)(2,1)} %q_ref.3) | copy-start | bytes 98308
  0.7 10.8 %copy-start.3 = (bf16[2,8,2,1,128]{4,2,3,1,0:T(2,128)(2,1)S(1)}, bf16[2,8,2,1,128]{4,2,3,1,0:T(2,128)(2,1)}, u32[]{:S(2)}) copy-start(bf16[2,8,2,1,128]{4,2,3,1,0:T(2,128)(2,1)} %param.10) | copy-start | bytes 24580
  0.7 10.8 %copy-start.4 = (s32[256]{0:T(256)S(1)}, s32[256]{0:T(256)}, u32[]{:S(2)}) copy-start(s32[256]{0:T(256)} %par_ref.3) | copy-start | bytes 3076
  0.7 10.8 %copy-start.6 = (s32[256]{0:T(256)S(1)}, s32[256]{0:T(256)}, u32[]{:S(2)}) copy-start(s32[256]{0:T(256)} %len_ref.1) | copy-start | bytes 3076
  2.1 9.3 %copy-start = (bf16[8,2,1024,1,128]{4,2,3,1,0:T(8,128)(2,1)S(1)}, bf16[8,2,1024,1,128]{4,2,3,1,0:T(8,128)(2,1)}, u32[]{:S(2)}) copy-start(bf16[8,2,1024,1,128]{4,2,3,1,0:T(8,128)(2,1)} %param.8) | copy-start | bytes 12582916
  2.1 4.6 %collective-permute-start = (bf16[8,16,128]{2,1,0:T(8,128)(2,1)}, bf16[8,16,128]{2,1,0:T(8,128)(2,1)S(1)}, u32[]{:S(2)}, u32[]{:S(2)}) collective-permute-start(bf16[8,16,128]{2,1,0:T(8,128)(2,1)} %shard_map.111.after_ref), channel_id=1, source_target_pairs={{0,8},{8,0},{16,24},{24,16},{32,40},{40,32},{48,56},{56,48},{64,72... | collective-permute-start | bytes 98312 | tf_op jit(solution)/shard_map/ppermute | solution.py:344
  6.7 17.6 %collective-permute-start.2 = (bf16[1,2,1024,128]{3,2,1,0:T(8,128)(2,1)}, bf16[1,2,1024,128]{3,2,1,0:T(8,128)(2,1)S(1)}, u32[]{:S(2)}, u32[]{:S(2)}) collective-permute-start(bf16[1,2,1024,128]{3,2,1,0:T(8,128)(2,1)} %shard_map.114), channel_id=1, source_target_pairs={{0,8},{8,0},{16,24},{24,16},{32,40},{40,32},{48,56},{56,48},{64,72... | collective-permute-start | bytes 1572872 | tf_op jit(solution)/shard_map/ppermute | solution.py:344
  8.1 14.3 %collective-permute-start.5 = (bf16[1040,128]{1,0:T(8,128)(2,1)}, bf16[1040,128]{1,0:T(8,128)(2,1)S(1)}, u32[]{:S(2)}, u32[]{:S(2)}) collective-permute-start(bf16[1040,128]{1,0:T(8,128)(2,1)} %get-tuple-element.26.w0), channel_id=1, source_target_pairs={{0,192},{8,200},{16,208},{24,216},{32,224},{40,232},{48,240},{56,2... | collective-permute-start | bytes 798728 | tf_op jit(solution)/shard_map/ppermute | solution.py:397
  9.6 12.9 %collective-permute-start.4 = (bf16[1040,128]{1,0:T(8,128)(2,1)}, bf16[1040,128]{1,0:T(8,128)(2,1)S(1)}, u32[]{:S(2)}, u32[]{:S(2)}) collective-permute-start(bf16[1040,128]{1,0:T(8,128)(2,1)} %get-tuple-element.26.w0), channel_id=1, source_target_pairs={{0,128},{8,136},{16,144},{24,152},{32,160},{40,168},{48,176},{56,1... | collective-permute-start | bytes 798728 | tf_op jit(solution)/shard_map/ppermute | solution.py:397
  10.4 13.9 %collective-permute-start.3 = (bf16[1040,128]{1,0:T(8,128)(2,1)}, bf16[1040,128]{1,0:T(8,128)(2,1)S(1)}, u32[]{:S(2)}, u32[]{:S(2)}) collective-permute-start(bf16[1040,128]{1,0:T(8,128)(2,1)} %get-tuple-element.26.w0), channel_id=1, source_target_pairs={{0,64},{8,72},{16,80},{24,88},{32,96},{40,104},{48,112},{56,120},{... | collective-permute-start | bytes 798728 | tf_op jit(solution)/shard_map/ppermute | solution.py:397
  18.4 20.0 %copy-start.1 = (bf16[1040,128]{1,0:T(8,128)(2,1)S(1)}, bf16[1040,128]{1,0:T(8,128)(2,1)}, u32[]{:S(2)}) copy-start(bf16[1040,128]{1,0:T(8,128)(2,1)} %get-tuple-element.26.w0) | copy-start | bytes 798724
  18.4 4.0 %collective-permute-start.1 = (bf16[16,1024]{1,0:T(8,128)(2,1)S(1)}, bf16[16,1024]{1,0:T(8,128)(2,1)S(1)}, u32[]{:S(2)}, u32[]{:S(2)}) collective-permute-start(bf16[16,1024]{1,0:T(8,128)(2,1)S(1)} %get-tuple-element.21), channel_id=1, source_target_pairs={{0,8},{8,0},{16,24},{24,16},{32,40},{40,32},{48,56},{56,48},{64,72... | collective-permute-start | bytes 98312 | tf_op jit(solution)/shard_map/ppermute | solution.py:344
  26.0 43.0 %collective-permute-start.12 = (bf16[3,2,1024,128]{3,2,1,0:T(8,128)(2,1)S(1)}, bf16[3,2,1024,128]{3,2,1,0:T(8,128)(2,1)S(1)}, u32[]{:S(2)}, u32[]{:S(2)}) collective-permute-start(bf16[3,2,1024,128]{3,2,1,0:T(8,128)(2,1)S(1)} %get-tuple-element.30), channel_id=1, source_target_pairs={{0,8},{8,0},{16,24},{24,16},{32,40},{40,32},{48,56},{56,48},{64,72... | collective-permute-start | bytes 4718600 | tf_op jit(solution)/shard_map/ppermute | solution.py:344
  26.6 9.1 %collective-permute-start.8 = (bf16[8,1024]{1,0:T(8,128)(2,1)S(1)}, bf16[8,1024]{1,0:T(8,128)(2,1)S(1)}, u32[]{:S(2)}, u32[]{:S(2)}) collective-permute-start(bf16[8,1024]{1,0:T(8,128)(2,1)S(1)} %get-tuple-element.29.own_ref), channel_id=1, source_target_pairs={{0,40},{8,32},{16,56},{24,48},{32,8},{40,0},{48,24},{56,16},{64,10... | collective-permute-start | bytes 49160 | tf_op jit(solution)/shard_map/ppermute | solution.py:365
  32.5 6.0 %collective-permute-start.7 = (bf16[8,1024]{1,0:T(8,128)(2,1)S(1)}, bf16[8,1024]{1,0:T(8,128)(2,1)S(1)}, u32[]{:S(2)}, u32[]{:S(2)}) collective-permute-start(bf16[8,1024]{1,0:T(8,128)(2,1)S(1)} %get-tuple-element.29.own_ref), channel_id=1, source_target_pairs={{0,48},{8,24},{16,0},{24,40},{32,16},{40,56},{48,32},{56,8},{64,11... | collective-permute-start | bytes 49160 | tf_op jit(solution)/shard_map/ppermute | solution.py:365
  34.0 4.5 %collective-permute-start.6 = (bf16[8,1024]{1,0:T(8,128)(2,1)S(1)}, bf16[8,1024]{1,0:T(8,128)(2,1)S(1)}, u32[]{:S(2)}, u32[]{:S(2)}) collective-permute-start(bf16[8,1024]{1,0:T(8,128)(2,1)S(1)} %get-tuple-element.29.own_ref), channel_id=1, source_target_pairs={{0,56},{8,16},{16,8},{24,32},{32,24},{40,48},{48,40},{56,0},{64,12... | collective-permute-start | bytes 49160 | tf_op jit(solution)/shard_map/ppermute | solution.py:365
  51.4 3.8 %collective-permute-start.9 = (f32[4,8,128]{2,1,0:T(8,128)S(1)}, f32[4,8,128]{2,1,0:T(8,128)S(1)}, u32[]{:S(2)}, u32[]{:S(2)}) collective-permute-start(f32[4,8,128]{2,1,0:T(8,128)S(1)} %shard_map.117.a_ref), channel_id=1, source_target_pairs={{0,56},{8,16},{16,8},{24,32},{32,24},{40,48},{48,40},{56,0},{64,12... | collective-permute-start | bytes 49160 | tf_op jit(solution)/shard_map/ppermute | solution.py:365
  55.3 6.3 %collective-permute-start.10 = (f32[4,8,128]{2,1,0:T(8,128)S(1)}, f32[4,8,128]{2,1,0:T(8,128)S(1)}, u32[]{:S(2)}, u32[]{:S(2)}) collective-permute-start(f32[4,8,128]{2,1,0:T(8,128)S(1)} %shard_map.118.a_ref), channel_id=1, source_target_pairs={{0,48},{8,24},{16,0},{24,40},{32,16},{40,56},{48,32},{56,8},{64,11... | collective-permute-start | bytes 49160 | tf_op jit(solution)/shard_map/ppermute | solution.py:365
  61.5 6.7 %collective-permute-start.11 = (f32[4,8,128]{2,1,0:T(8,128)S(1)}, f32[4,8,128]{2,1,0:T(8,128)S(1)}, u32[]{:S(2)}, u32[]{:S(2)}) collective-permute-start(f32[4,8,128]{2,1,0:T(8,128)S(1)} %shard_map.119.a_ref), channel_id=1, source_target_pairs={{0,40},{8,32},{16,56},{24,48},{32,8},{40,0},{48,24},{56,16},{64,10... | collective-permute-start | bytes 49160 | tf_op jit(solution)/shard_map/ppermute | solution.py:365

commit v4 on v3

--- a/solution.py
+++ b/solution.py
@@ -25,24 +25,27 @@
     return pl.BlockSpec(memory_space=space)
 
 
-def needed(par_ref, slots_at, half):
-    flags = []
+def locals_of(par_ref, slots_at, half):
+    found = []
+    for j in range(BD):
+        local = par_ref[slots_at + j] - half * BD
+        found.append(jnp.where((local >= 0) & (local < BD), local, -1))
+    return found
+
+
+def needed(found):
+    mask = jnp.int32(0)
+    for local in found:
+        mask = mask | jnp.where(local >= 0, jnp.int32(1) << jnp.maximum(local, 0), 0)
+    ranks, beams = [], [jnp.int32(0)] * MOST
+    total = jnp.int32(0)
     for b in range(BD):
-        want = half * BD + b
-        hit = par_ref[slots_at] == want
-        for j in range(1, BD):
-            hit = hit | (par_ref[slots_at + j] == want)
-        flags.append(hit)
-    return flags
-
-
-def ranked(flags):
-    ranks = []
-    rank = jnp.int32(0)
-    for flag in flags:
-        ranks.append(rank)
-        rank = rank + flag.astype(jnp.int32)
-    return ranks, rank
+        bit = (mask >> b) & 1
+        ranks.append(total)
+        for r in range(min(b + 1, MOST)):
+            beams[r] = jnp.where((bit == 1) & (total == r), b, beams[r])
+        total = total + bit
+    return ranks, beams, total
 
 
 def message_kernel(fin_ref, q_ref, kv_ref, msg_ref):
@@ -58,26 +61,24 @@
     me = lax.axis_index("dp")
     half = lax.rem(me, 2)
     start = (me - half) * BD + (1 - half) * BD
-    flags = needed(par_ref, start, half)
-    ranks, total = ranked(flags)
+    _, beams, total = needed(locals_of(par_ref, start, half))
     early = a_ref.shape[0]
-    for b in range(BD):
-        for r in range(min(b + 1, early)):
-
-            @pl.when(flags[b] & (ranks[b] == r))
-            def _():
-                pltpu.make_async_copy(cache_ref.at[b], a_ref.at[r], sems.at[r]).start()
+    for u in range(early):
+
+        @pl.when(u // 2 < total)
+        def _():
+            pltpu.make_async_copy(cache_ref.at[beams[u // 2], u % 2], a_ref.at[u], sems.at[u]).start()
 
     rows = w_ref.shape[0]
     wcopy = pltpu.make_async_copy(w_ref, wext_ref.at[pl.ds(0, rows)], wsem)
     wcopy.start()
     wext_ref[pl.ds(rows, 16), :] = jnp.broadcast_to(head_ref[...].astype(F32), (16, HD)).astype(BF16)
     wcopy.wait()
-    for r in range(early):
-
-        @pl.when(r < total)
-        def _():
-            pltpu.make_async_copy(cache_ref.at[0], a_ref.at[r], sems.at[r]).wait()
+    for u in range(early):
+
+        @pl.when(u // 2 < total)
+        def _():
+            pltpu.make_async_copy(cache_ref.at[0, 0], a_ref.at[u], sems.at[u]).wait()
 
 
 OWN = BD * GH
@@ -96,38 +97,35 @@
     mine = pair + half * BD
     theirs = pair + (1 - half) * BD
     scaling = math.log2(math.e) / math.sqrt(HD)
-    wanted = needed(par_ref, theirs, half)
-    send_ranks, send_total = ranked(wanted)
-    skip = MOST - late_ref.shape[0]
-    for b in range(BD):
-        for r in range(skip, min(b + 1, MOST)):
-
-            @pl.when(wanted[b] & (send_ranks[b] == r))
-            def _():
-                pltpu.make_async_copy(cache_ref.at[b], late_ref.at[r - skip], sendsem.at[r]).start()
-
-    own_local = []
-    for s in range(BD):
-        local = par_ref[mine + s] - half * BD
-        here = (local >= 0) & (local < BD)
-        own_local.append(jnp.where(here, local, -1))
-
-        @pl.when(here)
+    their_local = locals_of(par_ref, theirs, half)
+    _, beams, send_total = needed(their_local)
+    skip = 2 * MOST - late_ref.shape[0]
+    for u in range(skip, 2 * MOST):
+
+        @pl.when(u // 2 < send_total)
         def _():
             pltpu.make_async_copy(
-                cache_ref.at[jnp.clip(local, 0, BD - 1)], newc_ref.at[s], outsem.at[s]
+                cache_ref.at[beams[u // 2], u % 2], late_ref.at[u - skip], sendsem.at[u]
+            ).start()
+
+    own_local = locals_of(par_ref, mine, half)
+    for s in range(BD):
+
+        @pl.when(own_local[s] >= 0)
+        def _():
+            pltpu.make_async_copy(
+                cache_ref.at[jnp.maximum(own_local[s], 0)], newc_ref.at[s], outsem.at[s]
             ).start()
 
     slots = [jnp.int32(0)] * MOST
     locals_ = [jnp.int32(-1)] * MOST
     count = jnp.int32(0)
     for s in range(BD):
-        local = par_ref[theirs + s] - half * BD
-        here = (local >= 0) & (local < BD)
+        here = their_local[s] >= 0
         for j in range(min(s + 1, MOST)):
             take = here & (count == j)
             slots[j] = jnp.where(take, s, slots[j])
-            locals_[j] = jnp.where(take, local, locals_[j])
+            locals_[j] = jnp.where(take, their_local[s], locals_[j])
         count = count + here.astype(jnp.int32)
     q1s[...] = jnp.zeros_like(q1s)
     for b in range(BD):
@@ -168,9 +166,8 @@
         p0 = jnp.exp2(e0 - peak)
         p1 = jnp.exp2(e1 - peak)
         inv = 1.0 / (jnp.sum(p, axis=1, keepdims=True) + p0 + p1)
-        mixed = jnp.dot((p * inv).astype(BF16), cache_ref[b, 1], preferred_element_type=F32)
-        mixed = mixed + (p0 * inv).astype(BF16).astype(F32) * step[1:2]
-        mixed = mixed + (p1 * inv).astype(BF16).astype(F32) * v1s[...]
+        mixed = jnp.dot(p.astype(BF16), cache_ref[b, 1], preferred_element_type=F32)
+        mixed = (mixed + p0 * step[1:2] + p1 * v1s[...]) * inv
         fscr[b * GH : (b + 1) * GH, :] = mixed[ALL : ALL + GH]
         acc[...] = jnp.where(pcol[...] == b, mixed[:ALL], acc[...])
     rscr[...] = jnp.zeros_like(rscr)
@@ -206,18 +203,18 @@
     own_ref[...] = rscr[pl.ds(at, BD), :].astype(BF16)
     rows_ref[...] = packed.astype(BF16)
     swap_ref[...] = jnp.concatenate([rscr[pl.ds(their, BD), :], packed], axis=0).astype(BF16)
-    ranks, _ = ranked(needed(par_ref, mine, 1 - half))
-    for s in range(BD):
-        local = par_ref[mine + s] - (1 - half) * BD
+    cross_local = locals_of(par_ref, mine, 1 - half)
+    ranks, _, _ = needed(cross_local)
+    for s in range(BD):
         slot = jnp.int32(-1)
         for b in range(BD):
-            slot = jnp.where(local == b, ranks[b], slot)
+            slot = jnp.where(cross_local[s] == b, ranks[b], slot)
         meta_ref[s : s + 1, :] = jnp.full((1, HD), slot, jnp.int32)
-    for r in range(skip, MOST):
-
-        @pl.when(r < send_total)
-        def _():
-            pltpu.make_async_copy(cache_ref.at[0], late_ref.at[0], sendsem.at[r]).wait()
+    for u in range(skip, 2 * MOST):
+
+        @pl.when(u // 2 < send_total)
+        def _():
+            pltpu.make_async_copy(cache_ref.at[0, 0], late_ref.at[0], sendsem.at[u]).wait()
 
     for s in range(BD):
 
@@ -226,46 +223,40 @@
             pltpu.make_async_copy(cache_ref.at[0], newc_ref.at[s], outsem.at[s]).wait()
 
 
-def place_start(first, meta_ref, recv_ref, newc_ref, sems):
-    crossing = []
+def place_kernel(first, meta_ref, recv_ref, pick_ref, *refs):
+    token_ref, newc_ref, sems = refs[-3:]
+    token_ref[...] = pick_ref[...]
     count = recv_ref.shape[0]
-    for s in range(BD):
-        slot = meta_ref[s : s + 1, :][0, 0] - first
-        cross = (slot >= 0) & (slot < count)
-        slot = jnp.clip(slot, 0, count - 1)
-        crossing.append(cross)
-
-        @pl.when(cross)
-        def _():
-            pltpu.make_async_copy(recv_ref.at[slot], newc_ref.at[s], sems.at[s]).start()
-
-    return crossing
-
-
-def place_wait(crossing, recv_ref, newc_ref, sems):
-    for s in range(BD):
-
-        @pl.when(crossing[s])
-        def _():
-            pltpu.make_async_copy(recv_ref.at[0], newc_ref.at[s], sems.at[s]).wait()
-
-
-def place_kernel(first, meta_ref, recv_ref, *refs):
-    newc_ref, sems = refs[-2:]
-    waits = place_start(first, meta_ref, recv_ref, newc_ref, sems)
-    place_wait(waits, recv_ref, newc_ref, sems)
+    waits = []
+    for s in range(BD):
+        slot = meta_ref[s : s + 1, :][0, 0]
+        for half in range(2):
+            unit = 2 * slot + half - first
+            fits = (slot >= 0) & (unit >= 0) & (unit < count)
+            waits.append(fits)
+
+            @pl.when(fits)
+            def _():
+                pltpu.make_async_copy(
+                    recv_ref.at[jnp.clip(unit, 0, count - 1)], newc_ref.at[s, half], sems.at[s, half]
+                ).start()
+
+    for s in range(BD):
+        for half in range(2):
+
+            @pl.when(waits[2 * s + half])
+            def _():
+                pltpu.make_async_copy(recv_ref.at[0], newc_ref.at[s, half], sems.at[s, half]).wait()
 
 
 def gate_kernel(*refs):
     del refs
 
 
-def join_kernel(own_ref, rows_ref, swap_ref, meta_ref, recv_ref, *refs):
-    second_ref, full_ref, _, newc_ref, sems = refs[-5:]
-    waits = place_start(0, meta_ref, recv_ref, newc_ref, sems)
+def join_kernel(own_ref, rows_ref, swap_ref, *refs):
+    second_ref, full_ref = refs[-3:-1]
     second_ref[...] = own_ref[...] + swap_ref[0:BD, :]
     full_ref[...] = rows_ref[...] + swap_ref[BD : 2 * BD, :]
-    place_wait(waits, recv_ref, newc_ref, sems)
 
 
 def hidden_kernel(own_ref, r1, r2, r3, w0, w1, w2, w3, out_ref):
@@ -310,13 +301,14 @@
         out_ref[lax.rem(mine + q, pairs)] = wide[q * BD : (q + 1) * BD]
 
 
-def add_kernel(a_ref, b_ref, out_ref):
-    out_ref[...] = a_ref[...] + b_ref[...]
-
-
-def final_kernel(pick_ref, a_ref, b_ref, out_ref):
-    pair = lax.rem(lax.axis_index("dp") // 2, a_ref.shape[0])
-    total = a_ref[pair] + b_ref[pair]
+def spread_kernel(own_ref, near_ref, far_ref, two_ref, three_ref):
+    two_ref[...] = near_ref[...] + far_ref[...]
+    three_ref[...] = own_ref[...] + two_ref[...]
+
+
+def final_kernel(pick_ref, own_ref, two_ref, three_ref, out_ref):
+    pair = lax.rem(lax.axis_index("dp") // 2, own_ref.shape[0])
+    total = own_ref[pair] + two_ref[pair] + three_ref[pair]
     sums = jnp.sum(pick_ref[...] * total, axis=0, keepdims=True)
     for s in range(BD):
         out_ref[s] = sums[0, s]
@@ -344,16 +336,16 @@
     return lax.ppermute(array, "dp", [(i, i ^ 1) for i in range(lax.axis_size("dp"))])
 
 
-def place(first, meta, recv, newc):
+def place(first, meta, recv, pick, newc):
     return call(
         functools.partial(place_kernel, first),
-        [shape(newc.shape, BF16)],
-        [VM, VM, HB],
-        [HB],
-        [pltpu.SemaphoreType.DMA((BD,))],
-        aliases={2: 0},
+        [shape(pick.shape, F32), shape(newc.shape, BF16)],
+        [VM, VM, VM, HB],
+        [VM, HB],
+        [pltpu.SemaphoreType.DMA((BD, 2))],
+        aliases={3: 1},
         limit=16,
-    )(meta, recv, newc)[0]
+    )(meta, recv, pick, newc)
 
 
 def away(array, nz, k):
@@ -374,10 +366,10 @@
     cache = cache_kv.reshape(BD, 2, CACHE, HD)
     kv = step_kv.reshape(2, BD, 2, HD)
     depth = reward_in.shape[0]
-    part_a = shape((EARLY, 2, CACHE, HD), BF16)
-    part_b = shape((MOST - EARLY, 2, CACHE, HD), BF16)
+    part_a = shape((EARLY, CACHE, HD), BF16)
+    part_b = shape((2 * MOST - EARLY, CACHE, HD), BF16)
     (msg,) = call(
-        message_kernel, [shape((BD, 16, HD), BF16)], [SM, VM, VM], [VM], limit=60, cost=100000
+        message_kernel, [shape((BD, 16, HD), BF16)], [SM, VM, VM], [VM], limit=57, cost=100000
     )(finished, queries, kv)
     recv_msg = swap(msg)
     early, wext = call(
@@ -386,7 +378,7 @@
         [SM, HB, HB, VM, pl.ANY],
         [VM, VM],
         [pltpu.SemaphoreType.DMA((EARLY,)), pltpu.SemaphoreType.DMA],
-        limit=58,
+        limit=57,
         cost=20000000,
     )(parents, cache, reward_in, reward_head.reshape(1, HD), msg)
     (early,) = call(
@@ -421,20 +413,19 @@
             VM((2 * BD, GH * HD), F32),
             VM((BD, GH * HD), F32),
             pltpu.SemaphoreType.DMA((BD,)),
-            pltpu.SemaphoreType.DMA((MOST,)),
+            pltpu.SemaphoreType.DMA((2 * MOST,)),
         ],
         cost=20000000,
         limit=32,
     )(parents, lengths, finished, cache, queries, kv, recv_msg)
-    second_out, rows, late, newc = call(
+    second_out, rows, late = call(
         join_kernel,
-        [shape(own_out.shape, BF16), shape(rows.shape, BF16), part_b, shape(newc.shape, BF16)],
-        [VM] * 5 + [pl.ANY, HB, pl.ANY, pl.ANY, pl.ANY],
-        [VM, VM, pl.ANY, HB],
-        [pltpu.SemaphoreType.DMA((BD,))],
-        aliases={5: 2, 6: 3},
+        [shape(own_out.shape, BF16), shape(rows.shape, BF16), part_b],
+        [VM] * 3 + [pl.ANY] * 4,
+        [VM, VM, pl.ANY],
+        aliases={3: 2},
         limit=16,
-    )(own_out, rows, swap(to_swap), meta, recv_early, late, newc, *others)
+    )(own_out, rows, swap(to_swap), late, recv_early, others[0], others[2])
     recv_late = swap(late)
     (partial,) = call(
         hidden_kernel, [shape((nt, nz // 2 * BD, 5 * HD), BF16)], [VM] * 8, [VM], limit=16
@@ -443,14 +434,14 @@
     (sums,) = call(
         score_kernel, [shape((nz // 2, BD, HD), F32)], [VM] * 5, [VM], limit=16
     )(partials, wext, *others)
-    for k in (1, 2):
-        (sums,) = call(add_kernel, [shape(sums.shape, F32)], [VM, VM], [VM], limit=16)(
-            sums, away(sums, nz, k)
-        )
+    two, three = call(
+        spread_kernel, [shape(sums.shape, F32)] * 2, [VM] * 3, [VM] * 2, limit=16
+    )(sums, away(sums, nz, 1), away(sums, nz, 2))
+    pick, newc = place(0, meta, recv_early, pick, newc)
+    pick, newc = place(EARLY, meta, recv_late, pick, newc)
     (scores,) = call(
-        final_kernel, [shape((BD,), F32)], [VM, VM, VM], [SM], limit=16
-    )(pick, sums, away(sums, nz, 3))
-    newc = place(EARLY, meta, recv_late, newc)
+        final_kernel, [shape((BD,), F32)], [VM] * 4, [SM], limit=16
+    )(pick, three, away(two, nz, 2), away(three, nz, 3))
     return (first_out, second_out, scores, newc.reshape(cache_kv.shape))
 
 

time: 70.3 us -> 65.3 us (0.929)
  the two profiles are of different devices: /device:TPU:32 before, /device:TPU:2 now
where the time goes in v4:
time: 65.3 us; the launch traced here: 65 us
  starting transfers between devices  24.5 us (38%)
  Pallas kernels  13.8 us (21%)
  waiting for transfers between devices  13.3 us (20%)
  blocking collectives  12.5 us (19%)
  between operations  0.79 us (1%)
    ppermute x7, starting transfers between devices, away(): return lax.ppermute(array, 'dp', pairs)  14.6 us
    all_to_all x1, blocking collectives, per_device(): partials = lax.all_to_all(partial, 'tensor', 0, 0, tiled=True)  12.5 us
    ppermute x7, waiting for transfers between devices, away(): return lax.ppermute(array, 'dp', pairs)  11.3 us
    ppermute x4, starting transfers between devices, swap(): lax.ppermute(array, 'dp', [(i, i ^ 1) for i in range(lax.axis_size('dp'))])  6.3 us
    pallas_call x1, Pallas kernels, per_device(): call(attend_kernel, [shape((BD, GH * HD), BF16), shape((BD, GH * HD), BF1...  6.04 us
    ppermute x3, starting transfers between devices, per_device(): lax.ppermute(wext, 'dp', [(i, (i + nz * k) % ndp) for i in range(ndp)])  3.59 us
    pallas_call x1, Pallas kernels, per_device(): call(pack_kernel, [part_a, shape((depth + 16, HD), BF16)], [SM, HB, HB, V...  2.47 us
    pallas_call x2, Pallas kernels, place(): call(functools.partial(place_kernel, first), [shape(pick.shape, F32), sha...  2.05 us
  transfers between devices with their start and end apart: 14, of which 6 were waited for; matrix products, arithmetic and copies ran while one was open for 0% of the time, Pallas kernels for 17%

profile of v4, /device:TPU:2, one launch (start us, length us, event | category | flops | bytes accessed | tf_op | source)
XLA Modules:
  0.0 65.0 jit_solution(1451835182588417423)
XLA Ops:
  0.7 1.5 %shard_map.111.after_ref = bf16[8,16,128]{2,1,0:T(8,128)(2,1)} custom-call(s32[8]{0:T(128)} %fin_ref.3, bf16[2,8,8,128]{3,2,1,0:T(8,128)(2,1)} %q_ref.3, bf16[2,8,2,128]{3,2,1,0:T(2,128)(2,1)} %bitcast.8), custom_call_target="tpu_custom_call" | custom-call | flops 100000 | bytes 100000 | tf_op jit(solution)/shard_map/pallas_call | solution.py:371
  2.2 1.9 %collective-permute-start = (bf16[8,16,128]{2,1,0:T(8,128)(2,1)}, bf16[8,16,128]{2,1,0:T(8,128)(2,1)S(1)}, u32[]{:S(2)}, u32[]{:S(2)}) collective-permute-start(bf16[8,16,128]{2,1,0:T(8,128)(2,1)} %shard_map.111.after_ref), channel_id=1, source_target_pairs={{0,8},{8,0},{16,24},{24,16},{32,40},{40,32},{48,56},{56,48},{64,72... | collective-permute-start | bytes 98312 | tf_op jit(solution)/shard_map/ppermute | solution.py:336
  4.2 2.5 %shard_map.113 = (bf16[1,1024,128]{2,1,0:T(8,128)(2,1)}, bf16[1040,128]{1,0:T(8,128)(2,1)}) custom-call(s32[256]{0:T(256)} %par_ref.3, bf16[8,2,1024,128]{3,2,1,0:T(8,128)(2,1)} %bitcast.6, bf16[1024,128]{1,0:T(8,128)(2,1)} %w_ref.1, bf16[1,128]{1,0:T(2,128)(2,1)} %bitcast.11, bf16[8,16,128]{2,1,0:T(8,128)(2,1)} %shard_map.111.after_ref), custom_call_target="tpu_custom_call" | custom-call | flops 20000000 | bytes 20000000 | tf_op jit(solution)/shard_map/pallas_call | solution.py:375
  6.6 1.7 %collective-permute-start.3 = (bf16[1040,128]{1,0:T(8,128)(2,1)}, bf16[1040,128]{1,0:T(8,128)(2,1)S(1)}, u32[]{:S(2)}, u32[]{:S(2)}) collective-permute-start(bf16[1040,128]{1,0:T(8,128)(2,1)} %get-tuple-element.29.w0), channel_id=1, source_target_pairs={{0,64},{8,72},{16,80},{24,88},{32,96},{40,104},{48,112},{56,120},{... | collective-permute-start | bytes 798728 | tf_op jit(solution)/shard_map/ppermute | solution.py:389
  9.3 6.0 %shard_map.112 = (bf16[8,1024]{1,0:T(8,128)(2,1)}, bf16[8,1024]{1,0:T(8,128)(2,1)S(1)}, bf16[16,1024]{1,0:T(8,128)(2,1)S(1)}, bf16[8,1024]{1,0:T(8,128)(2,1)S(1)...) custom-call(s32[256]{0:T(256)S(1)} %copy-done.4, ...), custom_call_target="tpu_custom_call" | custom-call | flops 20000000 | bytes 20000000 | tf_op jit(solution)/shard_map/pallas_call | solution.py:391
  15.4 2.0 %collective-permute-start.1 = (bf16[16,1024]{1,0:T(8,128)(2,1)S(1)}, bf16[16,1024]{1,0:T(8,128)(2,1)S(1)}, u32[]{:S(2)}, u32[]{:S(2)}) collective-permute-start(bf16[16,1024]{1,0:T(8,128)(2,1)S(1)} %get-tuple-element.26), channel_id=1, source_target_pairs={{0,8},{8,0},{16,24},{24,16},{32,40},{40,32},{48,56},{56,48},{64,72... | collective-permute-start | bytes 98312 | tf_op jit(solution)/shard_map/ppermute | solution.py:336
  17.3 2.0 %collective-permute-done.1.swap_ref = bf16[16,1024]{1,0:T(8,128)(2,1)S(1)} collective-permute-done((bf16[16,1024]{1,0:T(8,128)(2,1)S(1)}, bf16[16,1024]{1,0:T(8,128)(2,1)S(1)}, u32[]{:S(2)}, u32[]{:S(2)}) %collective-permute-start.1) | collective-permute-done | bytes 32800 | tf_op jit(solution)/shard_map/ppermute | solution.py:336
  19.4 0.6 shard_map.115
  20.0 1.9 %collective-permute-start.5 = (bf16[7,1024,128]{2,1,0:T(8,128)(2,1)S(1)}, bf16[7,1024,128]{2,1,0:T(8,128)(2,1)S(1)}, u32[]{:S(2)}, u32[]{:S(2)}) collective-permute-start(bf16[7,1024,128]{2,1,0:T(8,128)(2,1)S(1)} %get-tuple-element.32), channel_id=1, source_target_pairs={{0,8},{8,0},{16,24},{24,16},{32,40},{40,32},{48,56},{56,48},{64,72... | collective-permute-start | bytes 5505032 | tf_op jit(solution)/shard_map/ppermute | solution.py:336
  21.9 1.5 %collective-permute-start.9 = (bf16[1040,128]{1,0:T(8,128)(2,1)S(1)}, bf16[1040,128]{1,0:T(8,128)(2,1)S(1)}, u32[]{:S(2)}, u32[]{:S(2)}) collective-permute-start(bf16[1040,128]{1,0:T(8,128)(2,1)S(1)} %copy-done.1), channel_id=1, source_target_pairs={{0,128},{8,136},{16,144},{24,152},{32,160},{40,168},{48,176},{56,1... | collective-permute-start | bytes 798728 | tf_op jit(solution)/shard_map/ppermute | solution.py:389
  23.4 5.3 %collective-permute-start.6 = (bf16[8,1024]{1,0:T(8,128)(2,1)S(1)}, bf16[8,1024]{1,0:T(8,128)(2,1)S(1)}, u32[]{:S(2)}, u32[]{:S(2)}) collective-permute-start(bf16[8,1024]{1,0:T(8,128)(2,1)S(1)} %get-tuple-element.38.own_ref), channel_id=1, source_target_pairs={{0,56},{8,16},{16,8},{24,32},{32,24},{40,48},{48,40},{56,0},{64,12... | collective-permute-start | bytes 49160 | tf_op jit(solution)/shard_map/ppermute | solution.py:357
  28.7 1.1 %collective-permute-start.7 = (bf16[8,1024]{1,0:T(8,128)(2,1)S(1)}, bf16[8,1024]{1,0:T(8,128)(2,1)S(1)}, u32[]{:S(2)}, u32[]{:S(2)}) collective-permute-start(bf16[8,1024]{1,0:T(8,128)(2,1)S(1)} %get-tuple-element.38.own_ref), channel_id=1, source_target_pairs={{0,48},{8,24},{16,0},{24,40},{32,16},{40,56},{48,32},{56,8},{64,11... | collective-permute-start | bytes 49160 | tf_op jit(solution)/shard_map/ppermute | solution.py:357
  29.8 1.2 %collective-permute-start.8 = (bf16[8,1024]{1,0:T(8,128)(2,1)S(1)}, bf16[8,1024]{1,0:T(8,128)(2,1)S(1)}, u32[]{:S(2)}, u32[]{:S(2)}) collective-permute-start(bf16[8,1024]{1,0:T(8,128)(2,1)S(1)} %get-tuple-element.38.own_ref), channel_id=1, source_target_pairs={{0,40},{8,32},{16,56},{24,48},{32,8},{40,0},{48,24},{56,16},{64,10... | collective-permute-start | bytes 49160 | tf_op jit(solution)/shard_map/ppermute | solution.py:357
  31.1 2.4 %collective-permute-done.7.r2 = bf16[8,1024]{1,0:T(8,128)(2,1)S(1)} collective-permute-done((bf16[8,1024]{1,0:T(8,128)(2,1)S(1)}, bf16[8,1024]{1,0:T(8,128)(2,1)S(1)}, u32[]{:S(2)}, u32[]{:S(2)}) %collective-permute-start.7) | collective-permute-done | bytes 16416 | tf_op jit(solution)/shard_map/ppermute | solution.py:357
  33.4 3.3 %collective-permute-done.8.r3 = bf16[8,1024]{1,0:T(8,128)(2,1)S(1)} collective-permute-done((bf16[8,1024]{1,0:T(8,128)(2,1)S(1)}, bf16[8,1024]{1,0:T(8,128)(2,1)S(1)}, u32[]{:S(2)}, u32[]{:S(2)}) %collective-permute-start.8) | collective-permute-done | bytes 16416 | tf_op jit(solution)/shard_map/ppermute | solution.py:357
  37.0 12.5 %all_to_all.5.hid_ref = bf16[8,32,640]{2,1,0:T(8,128)(2,1)S(1)} all-to-all(bf16[8,32,640]{2,1,0:T(8,128)(2,1)S(1)} %shard_map.118), channel_id=1, replica_groups=mesh['dp'=32,'tensor'=8] {'tensor'}, dimensions={0} | all-to-all | bytes 655360 | tf_op jit(solution)/shard_map/all_to_all | solution.py:433
  50.3 1.3 %collective-permute-start.11 = (f32[4,8,128]{2,1,0:T(8,128)S(1)}, f32[4,8,128]{2,1,0:T(8,128)S(1)}, u32[]{:S(2)}, u32[]{:S(2)}) collective-permute-start(f32[4,8,128]{2,1,0:T(8,128)S(1)} %shard_map.119.own_ref), channel_id=1, source_target_pairs={{0,48},{8,24},{16,0},{24,40},{32,16},{40,56},{48,32},{56,8},{64,11... | collective-permute-start | bytes 49160 | tf_op jit(solution)/shard_map/ppermute | solution.py:357
  51.6 3.2 %collective-permute-done.10.near_ref = f32[4,8,128]{2,1,0:T(8,128)S(1)} collective-permute-done((f32[4,8,128]{2,1,0:T(8,128)S(1)}, f32[4,8,128]{2,1,0:T(8,128)S(1)}, u32[]{:S(2)}, u32[]{:S(2)}) %collective-permute-start.10) | collective-permute-done | bytes 16416 | tf_op jit(solution)/shard_map/ppermute | solution.py:357
  55.1 2.5 %collective-permute-start.12 = (f32[4,8,128]{2,1,0:T(8,128)S(1)}, f32[4,8,128]{2,1,0:T(8,128)S(1)}, u32[]{:S(2)}, u32[]{:S(2)}) collective-permute-start(f32[4,8,128]{2,1,0:T(8,128)S(1)} %get-tuple-element.40), channel_id=1, source_target_pairs={{0,48},{8,24},{16,0},{24,40},{32,16},{40,56},{48,32},{56,8},{64,11... | collective-permute-start | bytes 49160 | tf_op jit(solution)/shard_map/ppermute | solution.py:357
  57.5 2.7 %collective-permute-start.13 = (f32[4,8,128]{2,1,0:T(8,128)S(1)}, f32[4,8,128]{2,1,0:T(8,128)S(1)}, u32[]{:S(2)}, u32[]{:S(2)}) collective-permute-start(f32[4,8,128]{2,1,0:T(8,128)S(1)} %get-tuple-element.39.own_ref), channel_id=1, source_target_pairs={{0,40},{8,32},{16,56},{24,48},{32,8},{40,0},{48,24},{56,16},{64,10... | collective-permute-start | bytes 49160 | tf_op jit(solution)/shard_map/ppermute | solution.py:357
  60.2 0.9 %shard_map.116 = (f32[8,128]{1,0:T(8,128)S(1)}, bf16[8,2,1024,128]{3,2,1,0:T(8,128)(2,1)}) custom-call(s32[8,128]{1,0:T(8,128)S(1)} %get-tuple-element.31.meta_ref, bf16[1,1024,128]{2,1,0:T(8,128)(2,1)S(1)} %collective-permute-done.2.refs_1_.recv_ref, f32[8,128]{1,0:T(8,128)S(1)} %get-tuple-element.33.pick_ref, ...), custom_call_target="tpu_custom_call", output_to_operand_aliasing={{1}: (3, {})} | custom-call | flops 1000000 | bytes 1000000 | tf_op jit(solution)/shard_map/pallas_call | solution.py:340
  61.1 1.1 %shard_map.117 = (f32[8,128]{1,0:T(8,128)S(1)}, bf16[8,2,1024,128]{3,2,1,0:T(8,128)(2,1)}) custom-call(s32[8,128]{1,0:T(8,128)S(1)} %get-tuple-element.31.meta_ref, bf16[7,1024,128]{2,1,0:T(8,128)(2,1)S(1)} %collective-permute-done.5.recv_ref, f32[8,128]{1,0:T(8,128)S(1)} %get-tuple-element.35.pick_ref, ...), custom_call_target="tpu_custom_call", output_to_operand_aliasing={{1}: (3, {})} | custom-call | flops 1000000 | bytes 1000000 | tf_op jit(solution)/shard_map/pallas_call | solution.py:340
  62.3 2.1 %collective-permute-done.13.three_ref = f32[4,8,128]{2,1,0:T(8,128)S(1)} collective-permute-done((f32[4,8,128]{2,1,0:T(8,128)S(1)}, f32[4,8,128]{2,1,0:T(8,128)S(1)}, u32[]{:S(2)}, u32[]{:S(2)}) %collective-permute-start.13) | collective-permute-done | bytes 16416 | tf_op jit(solution)/shard_map/ppermute | solution.py:357
  64.4 0.6 shard_map.121
  (30 shorter events, 2.3 us)
Async XLA Ops:
  0.6 8.7 %copy-start.3 = (bf16[2,8,2,1,128]{4,2,3,1,0:T(2,128)(2,1)S(1)}, bf16[2,8,2,1,128]{4,2,3,1,0:T(2,128)(2,1)}, u32[]{:S(2)}) copy-start(bf16[2,8,2,1,128]{4,2,3,1,0:T(2,128)(2,1)} %param.10) | copy-start | bytes 24580
  0.6 8.7 %copy-start.2 = (bf16[2,8,8,128]{3,2,1,0:T(8,128)(2,1)S(1)}, bf16[2,8,8,128]{3,2,1,0:T(8,128)(2,1)}, u32[]{:S(2)}) copy-start(bf16[2,8,8,128]{3,2,1,0:T(8,128)(2,1)} %q_ref.3) | copy-start | bytes 98308
  0.7 8.6 %copy-start.5 = (s32[8]{0:T(128)S(1)}, s32[8]{0:T(128)}, u32[]{:S(2)}) copy-start(s32[8]{0:T(128)} %fin_ref.3) | copy-start | bytes 100
  0.7 8.6 %copy-start = (bf16[8,2,1024,1,128]{4,2,3,1,0:T(8,128)(2,1)S(1)}, bf16[8,2,1024,1,128]{4,2,3,1,0:T(8,128)(2,1)}, u32[]{:S(2)}) copy-start(bf16[8,2,1024,1,128]{4,2,3,1,0:T(8,128)(2,1)} %param.8) | copy-start | bytes 12582916
  0.7 8.6 %copy-start.4 = (s32[256]{0:T(256)S(1)}, s32[256]{0:T(256)}, u32[]{:S(2)}) copy-start(s32[256]{0:T(256)} %par_ref.3) | copy-start | bytes 3076
  0.7 8.6 %copy-start.6 = (s32[256]{0:T(256)S(1)}, s32[256]{0:T(256)}, u32[]{:S(2)}) copy-start(s32[256]{0:T(256)} %len_ref.1) | copy-start | bytes 3076
  2.2 6.5 %collective-permute-start = (bf16[8,16,128]{2,1,0:T(8,128)(2,1)}, bf16[8,16,128]{2,1,0:T(8,128)(2,1)S(1)}, u32[]{:S(2)}, u32[]{:S(2)}) collective-permute-start(bf16[8,16,128]{2,1,0:T(8,128)(2,1)} %shard_map.111.after_ref), channel_id=1, source_target_pairs={{0,8},{8,0},{16,24},{24,16},{32,40},{40,32},{48,56},{56,48},{64,72... | collective-permute-start | bytes 98312 | tf_op jit(solution)/shard_map/ppermute | solution.py:336
  6.6 15.2 %copy-start.1 = (bf16[1040,128]{1,0:T(8,128)(2,1)S(1)}, bf16[1040,128]{1,0:T(8,128)(2,1)}, u32[]{:S(2)}) copy-start(bf16[1040,128]{1,0:T(8,128)(2,1)} %get-tuple-element.29.w0) | copy-start | bytes 798724
  6.6 12.7 %collective-permute-start.3 = (bf16[1040,128]{1,0:T(8,128)(2,1)}, bf16[1040,128]{1,0:T(8,128)(2,1)S(1)}, u32[]{:S(2)}, u32[]{:S(2)}) collective-permute-start(bf16[1040,128]{1,0:T(8,128)(2,1)} %get-tuple-element.29.w0), channel_id=1, source_target_pairs={{0,64},{8,72},{16,80},{24,88},{32,96},{40,104},{48,112},{56,120},{... | collective-permute-start | bytes 798728 | tf_op jit(solution)/shard_map/ppermute | solution.py:389
  8.3 11.1 %collective-permute-start.4 = (bf16[1040,128]{1,0:T(8,128)(2,1)}, bf16[1040,128]{1,0:T(8,128)(2,1)S(1)}, u32[]{:S(2)}, u32[]{:S(2)}) collective-permute-start(bf16[1040,128]{1,0:T(8,128)(2,1)} %get-tuple-element.29.w0), channel_id=1, source_target_pairs={{0,192},{8,200},{16,208},{24,216},{32,224},{40,232},{48,240},{56,2... | collective-permute-start | bytes 798728 | tf_op jit(solution)/shard_map/ppermute | solution.py:389
  8.8 10.6 %collective-permute-start.2 = (bf16[1,1024,128]{2,1,0:T(8,128)(2,1)}, bf16[1,1024,128]{2,1,0:T(8,128)(2,1)S(1)}, u32[]{:S(2)}, u32[]{:S(2)}) collective-permute-start(bf16[1,1024,128]{2,1,0:T(8,128)(2,1)} %shard_map.114), channel_id=1, source_target_pairs={{0,8},{8,0},{16,24},{24,16},{32,40},{40,32},{48,56},{56,48},{64,72... | collective-permute-start | bytes 786440 | tf_op jit(solution)/shard_map/ppermute | solution.py:336
  15.4 4.0 %collective-permute-start.1 = (bf16[16,1024]{1,0:T(8,128)(2,1)S(1)}, bf16[16,1024]{1,0:T(8,128)(2,1)S(1)}, u32[]{:S(2)}, u32[]{:S(2)}) collective-permute-start(bf16[16,1024]{1,0:T(8,128)(2,1)S(1)} %get-tuple-element.26), channel_id=1, source_target_pairs={{0,8},{8,0},{16,24},{24,16},{32,40},{40,32},{48,56},{56,48},{64,72... | collective-permute-start | bytes 98312 | tf_op jit(solution)/shard_map/ppermute | solution.py:336
  20.0 41.1 %collective-permute-start.5 = (bf16[7,1024,128]{2,1,0:T(8,128)(2,1)S(1)}, bf16[7,1024,128]{2,1,0:T(8,128)(2,1)S(1)}, u32[]{:S(2)}, u32[]{:S(2)}) collective-permute-start(bf16[7,1024,128]{2,1,0:T(8,128)(2,1)S(1)} %get-tuple-element.32), channel_id=1, source_target_pairs={{0,8},{8,0},{16,24},{24,16},{32,40},{40,32},{48,56},{56,48},{64,72... | collective-permute-start | bytes 5505032 | tf_op jit(solution)/shard_map/ppermute | solution.py:336
  21.9 9.2 %collective-permute-start.9 = (bf16[1040,128]{1,0:T(8,128)(2,1)S(1)}, bf16[1040,128]{1,0:T(8,128)(2,1)S(1)}, u32[]{:S(2)}, u32[]{:S(2)}) collective-permute-start(bf16[1040,128]{1,0:T(8,128)(2,1)S(1)} %copy-done.1), channel_id=1, source_target_pairs={{0,128},{8,136},{16,144},{24,152},{32,160},{40,168},{48,176},{56,1... | collective-permute-start | bytes 798728 | tf_op jit(solution)/shard_map/ppermute | solution.py:389
  23.4 7.7 %collective-permute-start.6 = (bf16[8,1024]{1,0:T(8,128)(2,1)S(1)}, bf16[8,1024]{1,0:T(8,128)(2,1)S(1)}, u32[]{:S(2)}, u32[]{:S(2)}) collective-permute-start(bf16[8,1024]{1,0:T(8,128)(2,1)S(1)} %get-tuple-element.38.own_ref), channel_id=1, source_target_pairs={{0,56},{8,16},{16,8},{24,32},{32,24},{40,48},{48,40},{56,0},{64,12... | collective-permute-start | bytes 49160 | tf_op jit(solution)/shard_map/ppermute | solution.py:357
  28.7 4.7 %collective-permute-start.7 = (bf16[8,1024]{1,0:T(8,128)(2,1)S(1)}, bf16[8,1024]{1,0:T(8,128)(2,1)S(1)}, u32[]{:S(2)}, u32[]{:S(2)}) collective-permute-start(bf16[8,1024]{1,0:T(8,128)(2,1)S(1)} %get-tuple-element.38.own_ref), channel_id=1, source_target_pairs={{0,48},{8,24},{16,0},{24,40},{32,16},{40,56},{48,32},{56,8},{64,11... | collective-permute-start | bytes 49160 | tf_op jit(solution)/shard_map/ppermute | solution.py:357
  29.8 6.9 %collective-permute-start.8 = (bf16[8,1024]{1,0:T(8,128)(2,1)S(1)}, bf16[8,1024]{1,0:T(8,128)(2,1)S(1)}, u32[]{:S(2)}, u32[]{:S(2)}) collective-permute-start(bf16[8,1024]{1,0:T(8,128)(2,1)S(1)} %get-tuple-element.38.own_ref), channel_id=1, source_target_pairs={{0,40},{8,32},{16,56},{24,48},{32,8},{40,0},{48,24},{56,16},{64,10... | collective-permute-start | bytes 49160 | tf_op jit(solution)/shard_map/ppermute | solution.py:357
  49.8 5.0 %collective-permute-start.10 = (f32[4,8,128]{2,1,0:T(8,128)S(1)}, f32[4,8,128]{2,1,0:T(8,128)S(1)}, u32[]{:S(2)}, u32[]{:S(2)}) collective-permute-start(f32[4,8,128]{2,1,0:T(8,128)S(1)} %shard_map.119.own_ref), channel_id=1, source_target_pairs={{0,56},{8,16},{16,8},{24,32},{32,24},{40,48},{48,40},{56,0},{64,12... | collective-permute-start | bytes 49160 | tf_op jit(solution)/shard_map/ppermute | solution.py:357
  50.3 4.7 %collective-permute-start.11 = (f32[4,8,128]{2,1,0:T(8,128)S(1)}, f32[4,8,128]{2,1,0:T(8,128)S(1)}, u32[]{:S(2)}, u32[]{:S(2)}) collective-permute-start(f32[4,8,128]{2,1,0:T(8,128)S(1)} %shard_map.119.own_ref), channel_id=1, source_target_pairs={{0,48},{8,24},{16,0},{24,40},{32,16},{40,56},{48,32},{56,8},{64,11... | collective-permute-start | bytes 49160 | tf_op jit(solution)/shard_map/ppermute | solution.py:357
  55.1 7.2 %collective-permute-start.12 = (f32[4,8,128]{2,1,0:T(8,128)S(1)}, f32[4,8,128]{2,1,0:T(8,128)S(1)}, u32[]{:S(2)}, u32[]{:S(2)}) collective-permute-start(f32[4,8,128]{2,1,0:T(8,128)S(1)} %get-tuple-element.40), channel_id=1, source_target_pairs={{0,48},{8,24},{16,0},{24,40},{32,16},{40,56},{48,32},{56,8},{64,11... | collective-permute-start | bytes 49160 | tf_op jit(solution)/shard_map/ppermute | solution.py:357
  57.5 6.9 %collective-permute-start.13 = (f32[4,8,128]{2,1,0:T(8,128)S(1)}, f32[4,8,128]{2,1,0:T(8,128)S(1)}, u32[]{:S(2)}, u32[]{:S(2)}) collective-permute-start(f32[4,8,128]{2,1,0:T(8,128)S(1)} %get-tuple-element.39.own_ref), channel_id=1, source_target_pairs={{0,40},{8,32},{16,56},{24,48},{32,8},{40,0},{48,24},{56,16},{64,10... | collective-permute-start | bytes 49160 | tf_op jit(solution)/shard_map/ppermute | solution.py:357

commit v5 on v4

--- a/solution.py
+++ b/solution.py
@@ -152,12 +152,15 @@
     q2 = q2s[...].astype(BF16)
     acc[...] = jnp.zeros_like(acc)
     places = lax.broadcasted_iota(jnp.int32, (1, CACHE), 1)
-    for b in range(BD):
+    def match(b):
+        q = jnp.concatenate([q2, q1s[b]], axis=0)
+        return q, lax.dot_general(
+            q, cache_ref[b, 0], (((1,), (1,)), ((), ())), preferred_element_type=F32
+        )
+
+    def weigh(b, q, logits):
         bias = jnp.where(places < len_ref[mine + b], 0.0, -1e30)
-        q = jnp.concatenate([q2, q1s[b]], axis=0)
-        logits = lax.dot_general(
-            q, cache_ref[b, 0], (((1,), (1,)), ((), ())), preferred_element_type=F32
-        ) * scaling + bias
+        logits = logits * scaling + bias
         step = kv_ref[0, b].astype(F32)
         e0 = jnp.sum(q.astype(F32) * step[0:1], axis=1, keepdims=True) * scaling
         e1 = e1s[:, 0:1]
@@ -166,10 +169,23 @@
         p0 = jnp.exp2(e0 - peak)
         p1 = jnp.exp2(e1 - peak)
         inv = 1.0 / (jnp.sum(p, axis=1, keepdims=True) + p0 + p1)
-        mixed = jnp.dot(p.astype(BF16), cache_ref[b, 1], preferred_element_type=F32)
-        mixed = (mixed + p0 * step[1:2] + p1 * v1s[...]) * inv
+        return p, p0, p1, inv, step
+
+    def mix(b, p, p0, p1, inv, step):
+        mixed = jnp.dot((p * inv).astype(BF16), cache_ref[b, 1], preferred_element_type=F32)
+        mixed = mixed + (p0 * inv).astype(BF16).astype(F32) * step[1:2]
+        mixed = mixed + (p1 * inv).astype(BF16).astype(F32) * v1s[...]
         fscr[b * GH : (b + 1) * GH, :] = mixed[ALL : ALL + GH]
         acc[...] = jnp.where(pcol[...] == b, mixed[:ALL], acc[...])
+
+    first = match(0)
+    second = match(1)
+    held = weigh(0, *first)
+    for b in range(BD):
+        third = match(b + 2) if b + 2 < BD else None
+        ahead = weigh(b + 1, *second) if b + 1 < BD else None
+        mix(b, *held)
+        held, second = ahead, third
     rscr[...] = jnp.zeros_like(rscr)
     at = pl.multiple_of(half * BD, BD)
     their = pl.multiple_of((1 - half) * BD, BD)

time: 65.3 us -> 64.2 us (0.983)
  Pallas kernels: 13.8 us -> 12.8 us
    pallas_call x1, Pallas kernels: 6.04 us -> 4.8 us  [per_device(): call(attend_kernel, [shape((BD, GH * HD), BF16), shape((BD, GH * HD), BF1...]
    ppermute x3, starting transfers between devices: 3.59 us -> 4.51 us  [per_device(): lax.ppermute(wext, 'dp', [(i, (i + nz * k) % ndp) for i in range(ndp)])]
    ppermute x7, starting transfers between devices: 14.6 us -> 13.8 us  [away(): return lax.ppermute(array, 'dp', pairs)]
    ppermute x4, starting transfers between devices: 6.3 us -> 5.54 us  [swap(): lax.ppermute(array, 'dp', [(i, i ^ 1) for i in range(lax.axis_size('dp'))])]
  transfers between devices with their start and end apart: 14 -> 14, of which waited for: 6 -> 5; matrix products, arithmetic and copies ran while one was open for 0% -> 0% of each run, Pallas kernels for 17% -> 16%
where the time goes in v5:
time: 64.2 us; the launch traced here: 63.7 us
  starting transfers between devices  23.9 us (37%)
  waiting for transfers between devices  13.6 us (21%)
  Pallas kernels  12.8 us (20%)
  blocking collectives  12.5 us (19%)
  between operations  0.79 us (1%)
    ppermute x7, starting transfers between devices, away(): return lax.ppermute(array, 'dp', pairs)  13.8 us
    all_to_all x1, blocking collectives, per_device(): partials = lax.all_to_all(partial, 'tensor', 0, 0, tiled=True)  12.5 us
    ppermute x7, waiting for transfers between devices, away(): return lax.ppermute(array, 'dp', pairs)  11.3 us
    ppermute x4, starting transfers between devices, swap(): lax.ppermute(array, 'dp', [(i, i ^ 1) for i in range(lax.axis_size('dp'))])  5.54 us
    pallas_call x1, Pallas kernels, per_device(): call(attend_kernel, [shape((BD, GH * HD), BF16), shape((BD, GH * HD), BF1...  4.8 us
    ppermute x3, starting transfers between devices, per_device(): lax.ppermute(wext, 'dp', [(i, (i + nz * k) % ndp) for i in range(ndp)])  4.51 us
    pallas_call x1, Pallas kernels, per_device(): call(pack_kernel, [part_a, shape((depth + 16, HD), BF16)], [SM, HB, HB, V...  2.56 us
    ppermute x4, waiting for transfers between devices, swap(): lax.ppermute(array, 'dp', [(i, i ^ 1) for i in range(lax.axis_size('dp'))])  2.33 us
  transfers between devices with their start and end apart: 14, of which 5 were waited for; matrix products, arithmetic and copies ran while one was open for 0% of the time, Pallas kernels for 16%

profile of v5, /device:TPU:2, one launch (start us, length us, event | category | flops | bytes accessed | tf_op | source)
XLA Modules:
  0.0 63.7 jit_solution(1367907864317496664)
XLA Ops:
  0.7 1.5 %shard_map.111.after_ref = bf16[8,16,128]{2,1,0:T(8,128)(2,1)} custom-call(s32[8]{0:T(128)} %fin_ref.3, bf16[2,8,8,128]{3,2,1,0:T(8,128)(2,1)} %q_ref.3, bf16[2,8,2,128]{3,2,1,0:T(2,128)(2,1)} %bitcast.8), custom_call_target="tpu_custom_call" | custom-call | flops 100000 | bytes 100000 | tf_op jit(solution)/shard_map/pallas_call | solution.py:387
  2.2 1.9 %collective-permute-start = (bf16[8,16,128]{2,1,0:T(8,128)(2,1)}, bf16[8,16,128]{2,1,0:T(8,128)(2,1)S(1)}, u32[]{:S(2)}, u32[]{:S(2)}) collective-permute-start(bf16[8,16,128]{2,1,0:T(8,128)(2,1)} %shard_map.111.after_ref), channel_id=1, source_target_pairs={{0,8},{8,0},{16,24},{24,16},{32,40},{40,32},{48,56},{56,48},{64,72... | collective-permute-start | bytes 98312 | tf_op jit(solution)/shard_map/ppermute | solution.py:352
  4.2 2.6 %shard_map.113 = (bf16[1,1024,128]{2,1,0:T(8,128)(2,1)}, bf16[1040,128]{1,0:T(8,128)(2,1)}) custom-call(s32[256]{0:T(256)} %par_ref.3, bf16[8,2,1024,128]{3,2,1,0:T(8,128)(2,1)} %bitcast.6, bf16[1024,128]{1,0:T(8,128)(2,1)} %w_ref.1, bf16[1,128]{1,0:T(2,128)(2,1)} %bitcast.11, bf16[8,16,128]{2,1,0:T(8,128)(2,1)} %shard_map.111.after_ref), custom_call_target="tpu_custom_call" | custom-call | flops 20000000 | bytes 20000000 | tf_op jit(solution)/shard_map/pallas_call | solution.py:391
  6.7 1.6 %collective-permute-start.3 = (bf16[1040,128]{1,0:T(8,128)(2,1)}, bf16[1040,128]{1,0:T(8,128)(2,1)S(1)}, u32[]{:S(2)}, u32[]{:S(2)}) collective-permute-start(bf16[1040,128]{1,0:T(8,128)(2,1)} %get-tuple-element.29.w0), channel_id=1, source_target_pairs={{0,64},{8,72},{16,80},{24,88},{32,96},{40,104},{48,112},{56,120},{... | collective-permute-start | bytes 798728 | tf_op jit(solution)/shard_map/ppermute | solution.py:405
  9.2 4.8 %shard_map.112 = (bf16[8,1024]{1,0:T(8,128)(2,1)}, bf16[8,1024]{1,0:T(8,128)(2,1)S(1)}, bf16[16,1024]{1,0:T(8,128)(2,1)S(1)}, bf16[8,1024]{1,0:T(8,128)(2,1)S(1)...) custom-call(s32[256]{0:T(256)S(1)} %copy-done.4, ...), custom_call_target="tpu_custom_call" | custom-call | flops 20000000 | bytes 20000000 | tf_op jit(solution)/shard_map/pallas_call | solution.py:407
  14.0 1.7 %collective-permute-start.1 = (bf16[16,1024]{1,0:T(8,128)(2,1)S(1)}, bf16[16,1024]{1,0:T(8,128)(2,1)S(1)}, u32[]{:S(2)}, u32[]{:S(2)}) collective-permute-start(bf16[16,1024]{1,0:T(8,128)(2,1)S(1)} %get-tuple-element.26), channel_id=1, source_target_pairs={{0,8},{8,0},{16,24},{24,16},{32,40},{40,32},{48,56},{56,48},{64,72... | collective-permute-start | bytes 98312 | tf_op jit(solution)/shard_map/ppermute | solution.py:352
  15.7 2.3 %collective-permute-done.1.swap_ref = bf16[16,1024]{1,0:T(8,128)(2,1)S(1)} collective-permute-done((bf16[16,1024]{1,0:T(8,128)(2,1)S(1)}, bf16[16,1024]{1,0:T(8,128)(2,1)S(1)}, u32[]{:S(2)}, u32[]{:S(2)}) %collective-permute-start.1) | collective-permute-done | bytes 32800 | tf_op jit(solution)/shard_map/ppermute | solution.py:352
  18.1 0.6 shard_map.115
  18.7 1.6 %collective-permute-start.5 = (bf16[7,1024,128]{2,1,0:T(8,128)(2,1)S(1)}, bf16[7,1024,128]{2,1,0:T(8,128)(2,1)S(1)}, u32[]{:S(2)}, u32[]{:S(2)}) collective-permute-start(bf16[7,1024,128]{2,1,0:T(8,128)(2,1)S(1)} %get-tuple-element.32), channel_id=1, source_target_pairs={{0,8},{8,0},{16,24},{24,16},{32,40},{40,32},{48,56},{56,48},{64,72... | collective-permute-start | bytes 5505032 | tf_op jit(solution)/shard_map/ppermute | solution.py:352
  20.3 2.4 %collective-permute-start.9 = (bf16[1040,128]{1,0:T(8,128)(2,1)S(1)}, bf16[1040,128]{1,0:T(8,128)(2,1)S(1)}, u32[]{:S(2)}, u32[]{:S(2)}) collective-permute-start(bf16[1040,128]{1,0:T(8,128)(2,1)S(1)} %copy-done.1), channel_id=1, source_target_pairs={{0,128},{8,136},{16,144},{24,152},{32,160},{40,168},{48,176},{56,1... | collective-permute-start | bytes 798728 | tf_op jit(solution)/shard_map/ppermute | solution.py:405
  22.7 4.7 %collective-permute-start.6 = (bf16[8,1024]{1,0:T(8,128)(2,1)S(1)}, bf16[8,1024]{1,0:T(8,128)(2,1)S(1)}, u32[]{:S(2)}, u32[]{:S(2)}) collective-permute-start(bf16[8,1024]{1,0:T(8,128)(2,1)S(1)} %get-tuple-element.38.own_ref), channel_id=1, source_target_pairs={{0,56},{8,16},{16,8},{24,32},{32,24},{40,48},{48,40},{56,0},{64,12... | collective-permute-start | bytes 49160 | tf_op jit(solution)/shard_map/ppermute | solution.py:373
  27.4 1.6 %collective-permute-start.7 = (bf16[8,1024]{1,0:T(8,128)(2,1)S(1)}, bf16[8,1024]{1,0:T(8,128)(2,1)S(1)}, u32[]{:S(2)}, u32[]{:S(2)}) collective-permute-start(bf16[8,1024]{1,0:T(8,128)(2,1)S(1)} %get-tuple-element.38.own_ref), channel_id=1, source_target_pairs={{0,48},{8,24},{16,0},{24,40},{32,16},{40,56},{48,32},{56,8},{64,11... | collective-permute-start | bytes 49160 | tf_op jit(solution)/shard_map/ppermute | solution.py:373
  29.0 0.7 %collective-permute-start.8 = (bf16[8,1024]{1,0:T(8,128)(2,1)S(1)}, bf16[8,1024]{1,0:T(8,128)(2,1)S(1)}, u32[]{:S(2)}, u32[]{:S(2)}) collective-permute-start(bf16[8,1024]{1,0:T(8,128)(2,1)S(1)} %get-tuple-element.38.own_ref), channel_id=1, source_target_pairs={{0,40},{8,32},{16,56},{24,48},{32,8},{40,0},{48,24},{56,16},{64,10... | collective-permute-start | bytes 49160 | tf_op jit(solution)/shard_map/ppermute | solution.py:373
  29.7 2.4 %collective-permute-done.7.r2 = bf16[8,1024]{1,0:T(8,128)(2,1)S(1)} collective-permute-done((bf16[8,1024]{1,0:T(8,128)(2,1)S(1)}, bf16[8,1024]{1,0:T(8,128)(2,1)S(1)}, u32[]{:S(2)}, u32[]{:S(2)}) %collective-permute-start.7) | collective-permute-done | bytes 16416 | tf_op jit(solution)/shard_map/ppermute | solution.py:373
  32.1 3.7 %collective-permute-done.8.r3 = bf16[8,1024]{1,0:T(8,128)(2,1)S(1)} collective-permute-done((bf16[8,1024]{1,0:T(8,128)(2,1)S(1)}, bf16[8,1024]{1,0:T(8,128)(2,1)S(1)}, u32[]{:S(2)}, u32[]{:S(2)}) %collective-permute-start.8) | collective-permute-done | bytes 16416 | tf_op jit(solution)/shard_map/ppermute | solution.py:373
  36.1 12.5 %all_to_all.5.hid_ref = bf16[8,32,640]{2,1,0:T(8,128)(2,1)S(1)} all-to-all(bf16[8,32,640]{2,1,0:T(8,128)(2,1)S(1)} %shard_map.118), channel_id=1, replica_groups=mesh['dp'=32,'tensor'=8] {'tensor'}, dimensions={0} | all-to-all | bytes 655360 | tf_op jit(solution)/shard_map/all_to_all | solution.py:449
  49.1 1.1 %collective-permute-start.11 = (f32[4,8,128]{2,1,0:T(8,128)S(1)}, f32[4,8,128]{2,1,0:T(8,128)S(1)}, u32[]{:S(2)}, u32[]{:S(2)}) collective-permute-start(f32[4,8,128]{2,1,0:T(8,128)S(1)} %shard_map.119.own_ref), channel_id=1, source_target_pairs={{0,48},{8,24},{16,0},{24,40},{32,16},{40,56},{48,32},{56,8},{64,11... | collective-permute-start | bytes 49160 | tf_op jit(solution)/shard_map/ppermute | solution.py:373
  50.2 3.6 %collective-permute-done.10.near_ref = f32[4,8,128]{2,1,0:T(8,128)S(1)} collective-permute-done((f32[4,8,128]{2,1,0:T(8,128)S(1)}, f32[4,8,128]{2,1,0:T(8,128)S(1)}, u32[]{:S(2)}, u32[]{:S(2)}) %collective-permute-start.10) | collective-permute-done | bytes 16416 | tf_op jit(solution)/shard_map/ppermute | solution.py:373
  53.9 2.3 %collective-permute-start.12 = (f32[4,8,128]{2,1,0:T(8,128)S(1)}, f32[4,8,128]{2,1,0:T(8,128)S(1)}, u32[]{:S(2)}, u32[]{:S(2)}) collective-permute-start(f32[4,8,128]{2,1,0:T(8,128)S(1)} %get-tuple-element.40), channel_id=1, source_target_pairs={{0,48},{8,24},{16,0},{24,40},{32,16},{40,56},{48,32},{56,8},{64,11... | collective-permute-start | bytes 49160 | tf_op jit(solution)/shard_map/ppermute | solution.py:373
  56.2 3.1 %collective-permute-start.13 = (f32[4,8,128]{2,1,0:T(8,128)S(1)}, f32[4,8,128]{2,1,0:T(8,128)S(1)}, u32[]{:S(2)}, u32[]{:S(2)}) collective-permute-start(f32[4,8,128]{2,1,0:T(8,128)S(1)} %get-tuple-element.39.own_ref), channel_id=1, source_target_pairs={{0,40},{8,32},{16,56},{24,48},{32,8},{40,0},{48,24},{56,16},{64,10... | collective-permute-start | bytes 49160 | tf_op jit(solution)/shard_map/ppermute | solution.py:373
  59.3 0.9 %shard_map.116 = (f32[8,128]{1,0:T(8,128)S(1)}, bf16[8,2,1024,128]{3,2,1,0:T(8,128)(2,1)}) custom-call(s32[8,128]{1,0:T(8,128)S(1)} %get-tuple-element.31.meta_ref, bf16[1,1024,128]{2,1,0:T(8,128)(2,1)S(1)} %collective-permute-done.2.refs_1_.recv_ref, f32[8,128]{1,0:T(8,128)S(1)} %get-tuple-element.33.pick_ref, ...), custom_call_target="tpu_custom_call", output_to_operand_aliasing={{1}: (3, {})} | custom-call | flops 1000000 | bytes 1000000 | tf_op jit(solution)/shard_map/pallas_call | solution.py:356
  60.2 1.3 %shard_map.117 = (f32[8,128]{1,0:T(8,128)S(1)}, bf16[8,2,1024,128]{3,2,1,0:T(8,128)(2,1)}) custom-call(s32[8,128]{1,0:T(8,128)S(1)} %get-tuple-element.31.meta_ref, bf16[7,1024,128]{2,1,0:T(8,128)(2,1)S(1)} %collective-permute-done.5.recv_ref, f32[8,128]{1,0:T(8,128)S(1)} %get-tuple-element.35.pick_ref, ...), custom_call_target="tpu_custom_call", output_to_operand_aliasing={{1}: (3, {})} | custom-call | flops 1000000 | bytes 1000000 | tf_op jit(solution)/shard_map/pallas_call | solution.py:356
  61.5 1.5 %collective-permute-done.13.three_ref = f32[4,8,128]{2,1,0:T(8,128)S(1)} collective-permute-done((f32[4,8,128]{2,1,0:T(8,128)S(1)}, f32[4,8,128]{2,1,0:T(8,128)S(1)}, u32[]{:S(2)}, u32[]{:S(2)}) %collective-permute-start.13) | collective-permute-done | bytes 16416 | tf_op jit(solution)/shard_map/ppermute | solution.py:373
  63.0 0.6 shard_map.121
  (30 shorter events, 1.7 us)
Async XLA Ops:
  0.6 8.6 %copy-start.3 = (bf16[2,8,2,1,128]{4,2,3,1,0:T(2,128)(2,1)S(1)}, bf16[2,8,2,1,128]{4,2,3,1,0:T(2,128)(2,1)}, u32[]{:S(2)}) copy-start(bf16[2,8,2,1,128]{4,2,3,1,0:T(2,128)(2,1)} %param.10) | copy-start | bytes 24580
  0.6 8.6 %copy-start.2 = (bf16[2,8,8,128]{3,2,1,0:T(8,128)(2,1)S(1)}, bf16[2,8,8,128]{3,2,1,0:T(8,128)(2,1)}, u32[]{:S(2)}) copy-start(bf16[2,8,8,128]{3,2,1,0:T(8,128)(2,1)} %q_ref.3) | copy-start | bytes 98308
  0.7 8.6 %copy-start.5 = (s32[8]{0:T(128)S(1)}, s32[8]{0:T(128)}, u32[]{:S(2)}) copy-start(s32[8]{0:T(128)} %fin_ref.3) | copy-start | bytes 100
  0.7 8.5 %copy-start = (bf16[8,2,1024,1,128]{4,2,3,1,0:T(8,128)(2,1)S(1)}, bf16[8,2,1024,1,128]{4,2,3,1,0:T(8,128)(2,1)}, u32[]{:S(2)}) copy-start(bf16[8,2,1024,1,128]{4,2,3,1,0:T(8,128)(2,1)} %param.8) | copy-start | bytes 12582916
  0.7 8.5 %copy-start.4 = (s32[256]{0:T(256)S(1)}, s32[256]{0:T(256)}, u32[]{:S(2)}) copy-start(s32[256]{0:T(256)} %par_ref.3) | copy-start | bytes 3076
  0.7 8.5 %copy-start.6 = (s32[256]{0:T(256)S(1)}, s32[256]{0:T(256)}, u32[]{:S(2)}) copy-start(s32[256]{0:T(256)} %len_ref.1) | copy-start | bytes 3076
  2.2 6.6 %collective-permute-start = (bf16[8,16,128]{2,1,0:T(8,128)(2,1)}, bf16[8,16,128]{2,1,0:T(8,128)(2,1)S(1)}, u32[]{:S(2)}, u32[]{:S(2)}) collective-permute-start(bf16[8,16,128]{2,1,0:T(8,128)(2,1)} %shard_map.111.after_ref), channel_id=1, source_target_pairs={{0,8},{8,0},{16,24},{24,16},{32,40},{40,32},{48,56},{56,48},{64,72... | collective-permute-start | bytes 98312 | tf_op jit(solution)/shard_map/ppermute | solution.py:352
  6.7 13.5 %copy-start.1 = (bf16[1040,128]{1,0:T(8,128)(2,1)S(1)}, bf16[1040,128]{1,0:T(8,128)(2,1)}, u32[]{:S(2)}) copy-start(bf16[1040,128]{1,0:T(8,128)(2,1)} %get-tuple-element.29.w0) | copy-start | bytes 798724
  6.7 11.3 %collective-permute-start.3 = (bf16[1040,128]{1,0:T(8,128)(2,1)}, bf16[1040,128]{1,0:T(8,128)(2,1)S(1)}, u32[]{:S(2)}, u32[]{:S(2)}) collective-permute-start(bf16[1040,128]{1,0:T(8,128)(2,1)} %get-tuple-element.29.w0), channel_id=1, source_target_pairs={{0,64},{8,72},{16,80},{24,88},{32,96},{40,104},{48,112},{56,120},{... | collective-permute-start | bytes 798728 | tf_op jit(solution)/shard_map/ppermute | solution.py:405
  8.3 9.7 %collective-permute-start.4 = (bf16[1040,128]{1,0:T(8,128)(2,1)}, bf16[1040,128]{1,0:T(8,128)(2,1)S(1)}, u32[]{:S(2)}, u32[]{:S(2)}) collective-permute-start(bf16[1040,128]{1,0:T(8,128)(2,1)} %get-tuple-element.29.w0), channel_id=1, source_target_pairs={{0,192},{8,200},{16,208},{24,216},{32,224},{40,232},{48,240},{56,2... | collective-permute-start | bytes 798728 | tf_op jit(solution)/shard_map/ppermute | solution.py:405
  8.8 9.2 %collective-permute-start.2 = (bf16[1,1024,128]{2,1,0:T(8,128)(2,1)}, bf16[1,1024,128]{2,1,0:T(8,128)(2,1)S(1)}, u32[]{:S(2)}, u32[]{:S(2)}) collective-permute-start(bf16[1,1024,128]{2,1,0:T(8,128)(2,1)} %shard_map.114), channel_id=1, source_target_pairs={{0,8},{8,0},{16,24},{24,16},{32,40},{40,32},{48,56},{56,48},{64,72... | collective-permute-start | bytes 786440 | tf_op jit(solution)/shard_map/ppermute | solution.py:352
  14.0 4.0 %collective-permute-start.1 = (bf16[16,1024]{1,0:T(8,128)(2,1)S(1)}, bf16[16,1024]{1,0:T(8,128)(2,1)S(1)}, u32[]{:S(2)}, u32[]{:S(2)}) collective-permute-start(bf16[16,1024]{1,0:T(8,128)(2,1)S(1)} %get-tuple-element.26), channel_id=1, source_target_pairs={{0,8},{8,0},{16,24},{24,16},{32,40},{40,32},{48,56},{56,48},{64,72... | collective-permute-start | bytes 98312 | tf_op jit(solution)/shard_map/ppermute | solution.py:352
  18.7 41.5 %collective-permute-start.5 = (bf16[7,1024,128]{2,1,0:T(8,128)(2,1)S(1)}, bf16[7,1024,128]{2,1,0:T(8,128)(2,1)S(1)}, u32[]{:S(2)}, u32[]{:S(2)}) collective-permute-start(bf16[7,1024,128]{2,1,0:T(8,128)(2,1)S(1)} %get-tuple-element.32), channel_id=1, source_target_pairs={{0,8},{8,0},{16,24},{24,16},{32,40},{40,32},{48,56},{56,48},{64,72... | collective-permute-start | bytes 5505032 | tf_op jit(solution)/shard_map/ppermute | solution.py:352
  20.3 9.5 %collective-permute-start.9 = (bf16[1040,128]{1,0:T(8,128)(2,1)S(1)}, bf16[1040,128]{1,0:T(8,128)(2,1)S(1)}, u32[]{:S(2)}, u32[]{:S(2)}) collective-permute-start(bf16[1040,128]{1,0:T(8,128)(2,1)S(1)} %copy-done.1), channel_id=1, source_target_pairs={{0,128},{8,136},{16,144},{24,152},{32,160},{40,168},{48,176},{56,1... | collective-permute-start | bytes 798728 | tf_op jit(solution)/shard_map/ppermute | solution.py:405
  22.7 7.1 %collective-permute-start.6 = (bf16[8,1024]{1,0:T(8,128)(2,1)S(1)}, bf16[8,1024]{1,0:T(8,128)(2,1)S(1)}, u32[]{:S(2)}, u32[]{:S(2)}) collective-permute-start(bf16[8,1024]{1,0:T(8,128)(2,1)S(1)} %get-tuple-element.38.own_ref), channel_id=1, source_target_pairs={{0,56},{8,16},{16,8},{24,32},{32,24},{40,48},{48,40},{56,0},{64,12... | collective-permute-start | bytes 49160 | tf_op jit(solution)/shard_map/ppermute | solution.py:373
  27.4 4.7 %collective-permute-start.7 = (bf16[8,1024]{1,0:T(8,128)(2,1)S(1)}, bf16[8,1024]{1,0:T(8,128)(2,1)S(1)}, u32[]{:S(2)}, u32[]{:S(2)}) collective-permute-start(bf16[8,1024]{1,0:T(8,128)(2,1)S(1)} %get-tuple-element.38.own_ref), channel_id=1, source_target_pairs={{0,48},{8,24},{16,0},{24,40},{32,16},{40,56},{48,32},{56,8},{64,11... | collective-permute-start | bytes 49160 | tf_op jit(solution)/shard_map/ppermute | solution.py:373
  29.0 6.9 %collective-permute-start.8 = (bf16[8,1024]{1,0:T(8,128)(2,1)S(1)}, bf16[8,1024]{1,0:T(8,128)(2,1)S(1)}, u32[]{:S(2)}, u32[]{:S(2)}) collective-permute-start(bf16[8,1024]{1,0:T(8,128)(2,1)S(1)} %get-tuple-element.38.own_ref), channel_id=1, source_target_pairs={{0,40},{8,32},{16,56},{24,48},{32,8},{40,0},{48,24},{56,16},{64,10... | collective-permute-start | bytes 49160 | tf_op jit(solution)/shard_map/ppermute | solution.py:373
  48.8 5.0 %collective-permute-start.10 = (f32[4,8,128]{2,1,0:T(8,128)S(1)}, f32[4,8,128]{2,1,0:T(8,128)S(1)}, u32[]{:S(2)}, u32[]{:S(2)}) collective-permute-start(f32[4,8,128]{2,1,0:T(8,128)S(1)} %shard_map.119.own_ref), channel_id=1, source_target_pairs={{0,56},{8,16},{16,8},{24,32},{32,24},{40,48},{48,40},{56,0},{64,12... | collective-permute-start | bytes 49160 | tf_op jit(solution)/shard_map/ppermute | solution.py:373
  49.1 4.8 %collective-permute-start.11 = (f32[4,8,128]{2,1,0:T(8,128)S(1)}, f32[4,8,128]{2,1,0:T(8,128)S(1)}, u32[]{:S(2)}, u32[]{:S(2)}) collective-permute-start(f32[4,8,128]{2,1,0:T(8,128)S(1)} %shard_map.119.own_ref), channel_id=1, source_target_pairs={{0,48},{8,24},{16,0},{24,40},{32,16},{40,56},{48,32},{56,8},{64,11... | collective-permute-start | bytes 49160 | tf_op jit(solution)/shard_map/ppermute | solution.py:373
  53.9 7.6 %collective-permute-start.12 = (f32[4,8,128]{2,1,0:T(8,128)S(1)}, f32[4,8,128]{2,1,0:T(8,128)S(1)}, u32[]{:S(2)}, u32[]{:S(2)}) collective-permute-start(f32[4,8,128]{2,1,0:T(8,128)S(1)} %get-tuple-element.40), channel_id=1, source_target_pairs={{0,48},{8,24},{16,0},{24,40},{32,16},{40,56},{48,32},{56,8},{64,11... | collective-permute-start | bytes 49160 | tf_op jit(solution)/shard_map/ppermute | solution.py:373
  56.2 6.9 %collective-permute-start.13 = (f32[4,8,128]{2,1,0:T(8,128)S(1)}, f32[4,8,128]{2,1,0:T(8,128)S(1)}, u32[]{:S(2)}, u32[]{:S(2)}) collective-permute-start(f32[4,8,128]{2,1,0:T(8,128)S(1)} %get-tuple-element.39.own_ref), channel_id=1, source_target_pairs={{0,40},{8,32},{16,56},{24,48},{32,8},{40,0},{48,24},{56,16},{64,10... | collective-permute-start | bytes 49160 | tf_op jit(solution)/shard_map/ppermute | solution.py:373

commit v6 on v5

--- a/solution.py
+++ b/solution.py
@@ -48,31 +48,30 @@
     return ranks, beams, total
 
 
-def message_kernel(fin_ref, q_ref, kv_ref, msg_ref):
+def pack_kernel(
+    par_ref, fin_ref, cache_ref, w_ref, head_ref, q_ref, kv_ref, msg_ref, a_ref, wext_ref, sems, wsem
+):
+    me = lax.axis_index("dp")
+    half = lax.rem(me, 2)
+    start = (me - half) * BD + (1 - half) * BD
+    rows = w_ref.shape[0]
+    wcopy = pltpu.make_async_copy(w_ref, wext_ref.at[pl.ds(0, rows)], wsem)
+    wcopy.start()
+    _, beams, total = needed(locals_of(par_ref, start, half))
+    early = a_ref.shape[0]
+    for u in range(early):
+
+        @pl.when(u // 2 < total)
+        def _():
+            pltpu.make_async_copy(cache_ref.at[beams[u // 2], u % 2], a_ref.at[u], sems.at[u]).start()
+
+    wext_ref[pl.ds(rows, 16), :] = jnp.broadcast_to(head_ref[...].astype(F32), (16, HD)).astype(BF16)
     for s in range(BD):
         step = kv_ref[1, s].astype(F32)
         flag = jnp.full((1, HD), fin_ref[s], jnp.int32).astype(F32)
         msg_ref[s] = jnp.concatenate(
             [q_ref[1, s].astype(F32), step, flag, jnp.zeros((5, HD), F32)], axis=0
         ).astype(BF16)
-
-
-def pack_kernel(par_ref, cache_ref, w_ref, head_ref, after_ref, a_ref, wext_ref, sems, wsem):
-    me = lax.axis_index("dp")
-    half = lax.rem(me, 2)
-    start = (me - half) * BD + (1 - half) * BD
-    _, beams, total = needed(locals_of(par_ref, start, half))
-    early = a_ref.shape[0]
-    for u in range(early):
-
-        @pl.when(u // 2 < total)
-        def _():
-            pltpu.make_async_copy(cache_ref.at[beams[u // 2], u % 2], a_ref.at[u], sems.at[u]).start()
-
-    rows = w_ref.shape[0]
-    wcopy = pltpu.make_async_copy(w_ref, wext_ref.at[pl.ds(0, rows)], wsem)
-    wcopy.start()
-    wext_ref[pl.ds(rows, 16), :] = jnp.broadcast_to(head_ref[...].astype(F32), (16, HD)).astype(BF16)
     wcopy.wait()
     for u in range(early):
 
@@ -384,26 +383,24 @@
     depth = reward_in.shape[0]
     part_a = shape((EARLY, CACHE, HD), BF16)
     part_b = shape((2 * MOST - EARLY, CACHE, HD), BF16)
-    (msg,) = call(
-        message_kernel, [shape((BD, 16, HD), BF16)], [SM, VM, VM], [VM], limit=57, cost=100000
-    )(finished, queries, kv)
-    recv_msg = swap(msg)
-    early, wext = call(
+    msg, early, wext = call(
         pack_kernel,
-        [part_a, shape((depth + 16, HD), BF16)],
-        [SM, HB, HB, VM, pl.ANY],
-        [VM, VM],
+        [shape((BD, 16, HD), BF16), part_a, shape((depth + 16, HD), BF16)],
+        [SM, SM, HB, HB, VM, VM, VM],
+        [VM, VM, VM],
         [pltpu.SemaphoreType.DMA((EARLY,)), pltpu.SemaphoreType.DMA],
         limit=57,
-        cost=20000000,
-    )(parents, cache, reward_in, reward_head.reshape(1, HD), msg)
+        cost=1000000,
+    )(parents, finished, cache, reward_in, reward_head.reshape(1, HD), queries, kv)
+    recv_msg = swap(msg)
     (early,) = call(
         gate_kernel, [part_a], [pl.ANY, pl.ANY], [pl.ANY], aliases={0: 0}, limit=16, cost=1000
     )(early, recv_msg)
     recv_early = swap(early)
-    others = [
-        lax.ppermute(wext, "dp", [(i, (i + nz * k) % ndp) for i in range(ndp)]) for k in range(1, nx)
-    ]
+    near_w, far_w = (
+        lax.ppermute(wext, "dp", [(i, (i + nz * k) % ndp) for i in range(ndp)]) for k in (1, nx - 1)
+    )
+    others = [near_w, lax.ppermute(near_w, "dp", [(i, (i + nz) % ndp) for i in range(ndp)]), far_w]
     first_out, own_out, to_swap, rows, meta, pick, late, newc = call(
         attend_kernel,
         [

time: 64.2 us -> 63.2 us (0.984)
  waiting for transfers between devices: 13.6 us -> 14.7 us
  Pallas kernels: 12.8 us -> 11.8 us
  starting transfers between devices: 23.9 us -> 23.1 us
    ppermute x3 -> x2, starting transfers between devices: 4.51 us -> 2.03 us  [per_device(): lax.ppermute(wext, 'dp', [(i, (i + nz * k) % ndp) for i in range(ndp)])]
    ppermute x4, waiting for transfers between devices: 2.33 us -> 4.03 us  [swap(): lax.ppermute(array, 'dp', [(i, i ^ 1) for i in range(lax.axis_size('dp'))])]
    ppermute x0 -> x1, starting transfers between devices: none -> 1.55 us  [per_device(): lax.ppermute(near_w, 'dp', [(i, (i + nz) % ndp) for i in range(ndp)])]
    pallas_call x2 -> x1, Pallas kernels: 4.1 us -> 3.16 us  [per_device(): call(pack_kernel, [shape((BD, 16, HD), BF16), part_a, shape((depth + 16,...]
    ppermute x7, starting transfers between devices: 13.8 us -> 14.6 us  [away(): return lax.ppermute(array, 'dp', pairs)]
  transfers between devices with their start and end apart: 14 -> 14, of which waited for: 5 -> 7; matrix products, arithmetic and copies ran while one was open for 0% -> 0% of each run, Pallas kernels for 16% -> 12%
where the time goes in v6:
time: 63.2 us; the launch traced here: 63 us
  starting transfers between devices  23.1 us (37%)
  waiting for transfers between devices  14.7 us (23%)
  blocking collectives  12.5 us (20%)
  Pallas kernels  11.8 us (19%)
  between operations  0.79 us (1%)
    ppermute x7, starting transfers between devices, away(): return lax.ppermute(array, 'dp', pairs)  14.6 us
    all_to_all x1, blocking collectives, per_device(): partials = lax.all_to_all(partial, 'tensor', 0, 0, tiled=True)  12.5 us
    ppermute x7, waiting for transfers between devices, away(): return lax.ppermute(array, 'dp', pairs)  10.7 us
    ppermute x4, starting transfers between devices, swap(): lax.ppermute(array, 'dp', [(i, i ^ 1) for i in range(lax.axis_size('dp'))])  5.01 us
    pallas_call x1, Pallas kernels, per_device(): call(attend_kernel, [shape((BD, GH * HD), BF16), shape((BD, GH * HD), BF1...  4.58 us
    ppermute x4, waiting for transfers between devices, swap(): lax.ppermute(array, 'dp', [(i, i ^ 1) for i in range(lax.axis_size('dp'))])  4.03 us
    pallas_call x1, Pallas kernels, per_device(): call(pack_kernel, [shape((BD, 16, HD), BF16), part_a, shape((depth + 16,...  3.16 us
    pallas_call x2, Pallas kernels, place(): call(functools.partial(place_kernel, first), [shape(pick.shape, F32), sha...  2.36 us
  transfers between devices with their start and end apart: 14, of which 7 were waited for; matrix products, arithmetic and copies ran while one was open for 0% of the time, Pallas kernels for 12%

profile of v6, /device:TPU:2, one launch (start us, length us, event | category | flops | bytes accessed | tf_op | source)
XLA Modules:
  0.0 63.0 jit_solution(65185126199408176)
XLA Ops:
  0.7 3.2 %shard_map.111 = (bf16[8,16,128]{2,1,0:T(8,128)(2,1)}, bf16[1,1024,128]{2,1,0:T(8,128)(2,1)}, bf16[1040,128]{1,0:T(8,128)(2,1)}) custom-call(s32[256]{0:T(256)} %par_ref.3, s32[8]{0:T(128)} %fin_ref.3, bf16[8,2,1024,128]{3,2,1,0:T(8,128)(2,1)} %bitcast.6, bf16[1024,128]{1,0:T(8,128)(2,1)} %w_ref.1, bf16[1,128]{1,0:T(2,128)(2,1)} %bitcast.11, ...), custom_call_target="tpu_custom_call" | custom-call | flops 1000000 | bytes 1000000 | tf_op jit(solution)/shard_map/pallas_call | solution.py:386
  3.9 2.0 %collective-permute-start = (bf16[8,16,128]{2,1,0:T(8,128)(2,1)}, bf16[8,16,128]{2,1,0:T(8,128)(2,1)S(1)}, u32[]{:S(2)}, u32[]{:S(2)}) collective-permute-start(bf16[8,16,128]{2,1,0:T(8,128)(2,1)} %get-tuple-element.24), channel_id=1, source_target_pairs={{0,8},{8,0},{16,24},{24,16},{32,40},{40,32},{48,56},{56,48},{64,72... | collective-permute-start | bytes 98312 | tf_op jit(solution)/shard_map/ppermute | solution.py:351
  5.9 1.5 %collective-permute-start.3 = (bf16[1040,128]{1,0:T(8,128)(2,1)}, bf16[1040,128]{1,0:T(8,128)(2,1)S(1)}, u32[]{:S(2)}, u32[]{:S(2)}) collective-permute-start(bf16[1040,128]{1,0:T(8,128)(2,1)} %get-tuple-element.31.w0), channel_id=1, source_target_pairs={{0,64},{8,72},{16,80},{24,88},{32,96},{40,104},{48,112},{56,120},{... | collective-permute-start | bytes 798728 | tf_op jit(solution)/shard_map/ppermute | solution.py:401
  7.4 0.5 collective-permute-start.4
  8.1 1.9 %collective-permute-start.2 = (bf16[1,1024,128]{2,1,0:T(8,128)(2,1)}, bf16[1,1024,128]{2,1,0:T(8,128)(2,1)S(1)}, u32[]{:S(2)}, u32[]{:S(2)}) collective-permute-start(bf16[1,1024,128]{2,1,0:T(8,128)(2,1)} %shard_map.113), channel_id=1, source_target_pairs={{0,8},{8,0},{16,24},{24,16},{32,40},{40,32},{48,56},{56,48},{64,72... | collective-permute-start | bytes 786440 | tf_op jit(solution)/shard_map/ppermute | solution.py:351
  10.0 4.6 %shard_map.112 = (bf16[8,1024]{1,0:T(8,128)(2,1)}, bf16[8,1024]{1,0:T(8,128)(2,1)S(1)}, bf16[16,1024]{1,0:T(8,128)(2,1)S(1)}, bf16[8,1024]{1,0:T(8,128)(2,1)S(1)...) custom-call(s32[256]{0:T(256)S(1)} %copy-done.4, ...), custom_call_target="tpu_custom_call" | custom-call | flops 20000000 | bytes 20000000 | tf_op jit(solution)/shard_map/pallas_call | solution.py:404
  14.6 0.6 collective-permute-start.1
  15.2 3.4 %collective-permute-done.1.swap_ref = bf16[16,1024]{1,0:T(8,128)(2,1)S(1)} collective-permute-done((bf16[16,1024]{1,0:T(8,128)(2,1)S(1)}, bf16[16,1024]{1,0:T(8,128)(2,1)S(1)}, u32[]{:S(2)}, u32[]{:S(2)}) %collective-permute-start.1) | collective-permute-done | bytes 32800 | tf_op jit(solution)/shard_map/ppermute | solution.py:351
  18.6 0.6 shard_map.114
  19.8 1.6 %collective-permute-start.9 = (bf16[1040,128]{1,0:T(8,128)(2,1)S(1)}, bf16[1040,128]{1,0:T(8,128)(2,1)S(1)}, u32[]{:S(2)}, u32[]{:S(2)}) collective-permute-start(bf16[1040,128]{1,0:T(8,128)(2,1)S(1)} %collective-permute-done.3.refs_2_.w1), channel_id=1, source_target_pairs={{0,64},{8,72},{16,80},{24,88},{32,96},{40,104},{48,112},{56,120},{... | collective-permute-start | bytes 798728 | tf_op jit(solution)/shard_map/ppermute | solution.py:403
  21.3 5.4 %collective-permute-start.6 = (bf16[8,1024]{1,0:T(8,128)(2,1)S(1)}, bf16[8,1024]{1,0:T(8,128)(2,1)S(1)}, u32[]{:S(2)}, u32[]{:S(2)}) collective-permute-start(bf16[8,1024]{1,0:T(8,128)(2,1)S(1)} %get-tuple-element.40.own_ref), channel_id=1, source_target_pairs={{0,56},{8,16},{16,8},{24,32},{32,24},{40,48},{48,40},{56,0},{64,12... | collective-permute-start | bytes 49160 | tf_op jit(solution)/shard_map/ppermute | solution.py:372
  26.7 1.5 %collective-permute-start.7 = (bf16[8,1024]{1,0:T(8,128)(2,1)S(1)}, bf16[8,1024]{1,0:T(8,128)(2,1)S(1)}, u32[]{:S(2)}, u32[]{:S(2)}) collective-permute-start(bf16[8,1024]{1,0:T(8,128)(2,1)S(1)} %get-tuple-element.40.own_ref), channel_id=1, source_target_pairs={{0,48},{8,24},{16,0},{24,40},{32,16},{40,56},{48,32},{56,8},{64,11... | collective-permute-start | bytes 49160 | tf_op jit(solution)/shard_map/ppermute | solution.py:372
  28.2 0.9 %collective-permute-start.8 = (bf16[8,1024]{1,0:T(8,128)(2,1)S(1)}, bf16[8,1024]{1,0:T(8,128)(2,1)S(1)}, u32[]{:S(2)}, u32[]{:S(2)}) collective-permute-start(bf16[8,1024]{1,0:T(8,128)(2,1)S(1)} %get-tuple-element.40.own_ref), channel_id=1, source_target_pairs={{0,40},{8,32},{16,56},{24,48},{32,8},{40,0},{48,24},{56,16},{64,10... | collective-permute-start | bytes 49160 | tf_op jit(solution)/shard_map/ppermute | solution.py:372
  29.1 2.4 %collective-permute-done.7.r2 = bf16[8,1024]{1,0:T(8,128)(2,1)S(1)} collective-permute-done((bf16[8,1024]{1,0:T(8,128)(2,1)S(1)}, bf16[8,1024]{1,0:T(8,128)(2,1)S(1)}, u32[]{:S(2)}, u32[]{:S(2)}) %collective-permute-start.7) | collective-permute-done | bytes 16416 | tf_op jit(solution)/shard_map/ppermute | solution.py:372
  31.5 3.6 %collective-permute-done.8.r3 = bf16[8,1024]{1,0:T(8,128)(2,1)S(1)} collective-permute-done((bf16[8,1024]{1,0:T(8,128)(2,1)S(1)}, bf16[8,1024]{1,0:T(8,128)(2,1)S(1)}, u32[]{:S(2)}, u32[]{:S(2)}) %collective-permute-start.8) | collective-permute-done | bytes 16416 | tf_op jit(solution)/shard_map/ppermute | solution.py:372
  35.3 12.5 %all_to_all.5.hid_ref = bf16[8,32,640]{2,1,0:T(8,128)(2,1)S(1)} all-to-all(bf16[8,32,640]{2,1,0:T(8,128)(2,1)S(1)} %shard_map.117), channel_id=1, replica_groups=mesh['dp'=32,'tensor'=8] {'tensor'}, dimensions={0} | all-to-all | bytes 655360 | tf_op jit(solution)/shard_map/all_to_all | solution.py:446
  48.1 1.5 %collective-permute-start.11 = (f32[4,8,128]{2,1,0:T(8,128)S(1)}, f32[4,8,128]{2,1,0:T(8,128)S(1)}, u32[]{:S(2)}, u32[]{:S(2)}) collective-permute-start(f32[4,8,128]{2,1,0:T(8,128)S(1)} %shard_map.118.own_ref), channel_id=1, source_target_pairs={{0,48},{8,24},{16,0},{24,40},{32,16},{40,56},{48,32},{56,8},{64,11... | collective-permute-start | bytes 49160 | tf_op jit(solution)/shard_map/ppermute | solution.py:372
  49.6 3.6 %collective-permute-done.10.near_ref = f32[4,8,128]{2,1,0:T(8,128)S(1)} collective-permute-done((f32[4,8,128]{2,1,0:T(8,128)S(1)}, f32[4,8,128]{2,1,0:T(8,128)S(1)}, u32[]{:S(2)}, u32[]{:S(2)}) %collective-permute-start.10) | collective-permute-done | bytes 16416 | tf_op jit(solution)/shard_map/ppermute | solution.py:372
  53.2 2.3 %collective-permute-start.12 = (f32[4,8,128]{2,1,0:T(8,128)S(1)}, f32[4,8,128]{2,1,0:T(8,128)S(1)}, u32[]{:S(2)}, u32[]{:S(2)}) collective-permute-start(f32[4,8,128]{2,1,0:T(8,128)S(1)} %get-tuple-element.42), channel_id=1, source_target_pairs={{0,48},{8,24},{16,0},{24,40},{32,16},{40,56},{48,32},{56,8},{64,11... | collective-permute-start | bytes 49160 | tf_op jit(solution)/shard_map/ppermute | solution.py:372
  55.5 2.9 %collective-permute-start.13 = (f32[4,8,128]{2,1,0:T(8,128)S(1)}, f32[4,8,128]{2,1,0:T(8,128)S(1)}, u32[]{:S(2)}, u32[]{:S(2)}) collective-permute-start(f32[4,8,128]{2,1,0:T(8,128)S(1)} %get-tuple-element.41.own_ref), channel_id=1, source_target_pairs={{0,40},{8,32},{16,56},{24,48},{32,8},{40,0},{48,24},{56,16},{64,10... | collective-permute-start | bytes 49160 | tf_op jit(solution)/shard_map/ppermute | solution.py:372
  58.5 0.9 %shard_map.115 = (f32[8,128]{1,0:T(8,128)S(1)}, bf16[8,2,1024,128]{3,2,1,0:T(8,128)(2,1)}) custom-call(s32[8,128]{1,0:T(8,128)S(1)} %get-tuple-element.33.meta_ref, bf16[1,1024,128]{2,1,0:T(8,128)(2,1)S(1)} %collective-permute-done.2.refs_1_.recv_ref, f32[8,128]{1,0:T(8,128)S(1)} %get-tuple-element.35.pick_ref, ...), custom_call_target="tpu_custom_call", output_to_operand_aliasing={{1}: (3, {})} | custom-call | flops 1000000 | bytes 1000000 | tf_op jit(solution)/shard_map/pallas_call | solution.py:355
  59.8 1.4 %shard_map.116 = (f32[8,128]{1,0:T(8,128)S(1)}, bf16[8,2,1024,128]{3,2,1,0:T(8,128)(2,1)}) custom-call(s32[8,128]{1,0:T(8,128)S(1)} %get-tuple-element.33.meta_ref, bf16[7,1024,128]{2,1,0:T(8,128)(2,1)S(1)} %collective-permute-done.5.recv_ref, f32[8,128]{1,0:T(8,128)S(1)} %get-tuple-element.37.pick_ref, ...), custom_call_target="tpu_custom_call", output_to_operand_aliasing={{1}: (3, {})} | custom-call | flops 1000000 | bytes 1000000 | tf_op jit(solution)/shard_map/pallas_call | solution.py:355
  61.3 1.1 %collective-permute-done.13.three_ref = f32[4,8,128]{2,1,0:T(8,128)S(1)} collective-permute-done((f32[4,8,128]{2,1,0:T(8,128)S(1)}, f32[4,8,128]{2,1,0:T(8,128)S(1)}, u32[]{:S(2)}, u32[]{:S(2)}) %collective-permute-start.13) | collective-permute-done | bytes 16416 | tf_op jit(solution)/shard_map/ppermute | solution.py:372
  62.4 0.6 %shard_map.120 = f32[8]{0:T(128)} custom-call(f32[8,128]{1,0:T(8,128)S(1)} %get-tuple-element.39.pick_ref, f32[4,8,128]{2,1,0:T(8,128)S(1)} %get-tuple-element.41.own_ref, f32[4,8,128]{2,1,0:T(8,128)S(1)} %collective-permute-done.12.two_ref, f32[4,8,128]{2,1,0:T(8,128)S(1)} %collective-permute-done.13.three_ref), custom_call_target="tpu_custom_call" | custom-call | flops 1000000 | bytes 1000000 | tf_op jit(solution)/shard_map/pallas_call | solution.py:455
  (29 shorter events, 1.7 us)
Async XLA Ops:
  0.6 9.4 %copy-start = (bf16[8,2,1024,1,128]{4,2,3,1,0:T(8,128)(2,1)S(1)}, bf16[8,2,1024,1,128]{4,2,3,1,0:T(8,128)(2,1)}, u32[]{:S(2)}) copy-start(bf16[8,2,1024,1,128]{4,2,3,1,0:T(8,128)(2,1)} %param.8) | copy-start | bytes 12582916
  0.6 9.4 %copy-start.3 = (bf16[2,8,2,1,128]{4,2,3,1,0:T(2,128)(2,1)S(1)}, bf16[2,8,2,1,128]{4,2,3,1,0:T(2,128)(2,1)}, u32[]{:S(2)}) copy-start(bf16[2,8,2,1,128]{4,2,3,1,0:T(2,128)(2,1)} %param.10) | copy-start | bytes 24580
  0.7 9.4 %copy-start.2 = (bf16[2,8,8,128]{3,2,1,0:T(8,128)(2,1)S(1)}, bf16[2,8,8,128]{3,2,1,0:T(8,128)(2,1)}, u32[]{:S(2)}) copy-start(bf16[2,8,8,128]{3,2,1,0:T(8,128)(2,1)} %q_ref.3) | copy-start | bytes 98308
  0.7 9.4 %copy-start.4 = (s32[256]{0:T(256)S(1)}, s32[256]{0:T(256)}, u32[]{:S(2)}) copy-start(s32[256]{0:T(256)} %par_ref.3) | copy-start | bytes 3076
  0.7 9.3 %copy-start.5 = (s32[8]{0:T(128)S(1)}, s32[8]{0:T(128)}, u32[]{:S(2)}) copy-start(s32[8]{0:T(128)} %fin_ref.3) | copy-start | bytes 100
  0.7 9.3 %copy-start.6 = (s32[256]{0:T(256)S(1)}, s32[256]{0:T(256)}, u32[]{:S(2)}) copy-start(s32[256]{0:T(256)} %len_ref.1) | copy-start | bytes 3076
  3.9 31.2 %copy-start.1 = (bf16[1040,128]{1,0:T(8,128)(2,1)S(1)}, bf16[1040,128]{1,0:T(8,128)(2,1)}, u32[]{:S(2)}) copy-start(bf16[1040,128]{1,0:T(8,128)(2,1)} %get-tuple-element.31.w0) | copy-start | bytes 798724
  3.9 4.2 %collective-permute-start = (bf16[8,16,128]{2,1,0:T(8,128)(2,1)}, bf16[8,16,128]{2,1,0:T(8,128)(2,1)S(1)}, u32[]{:S(2)}, u32[]{:S(2)}) collective-permute-start(bf16[8,16,128]{2,1,0:T(8,128)(2,1)} %get-tuple-element.24), channel_id=1, source_target_pairs={{0,8},{8,0},{16,24},{24,16},{32,40},{40,32},{48,56},{56,48},{64,72... | collective-permute-start | bytes 98312 | tf_op jit(solution)/shard_map/ppermute | solution.py:351
  5.9 12.8 %collective-permute-start.3 = (bf16[1040,128]{1,0:T(8,128)(2,1)}, bf16[1040,128]{1,0:T(8,128)(2,1)S(1)}, u32[]{:S(2)}, u32[]{:S(2)}) collective-permute-start(bf16[1040,128]{1,0:T(8,128)(2,1)} %get-tuple-element.31.w0), channel_id=1, source_target_pairs={{0,64},{8,72},{16,80},{24,88},{32,96},{40,104},{48,112},{56,120},{... | collective-permute-start | bytes 798728 | tf_op jit(solution)/shard_map/ppermute | solution.py:401
  7.4 11.3 %collective-permute-start.4 = (bf16[1040,128]{1,0:T(8,128)(2,1)}, bf16[1040,128]{1,0:T(8,128)(2,1)S(1)}, u32[]{:S(2)}, u32[]{:S(2)}) collective-permute-start(bf16[1040,128]{1,0:T(8,128)(2,1)} %get-tuple-element.31.w0), channel_id=1, source_target_pairs={{0,192},{8,200},{16,208},{24,216},{32,224},{40,232},{48,240},{56,2... | collective-permute-start | bytes 798728 | tf_op jit(solution)/shard_map/ppermute | solution.py:401
  8.1 10.5 %collective-permute-start.2 = (bf16[1,1024,128]{2,1,0:T(8,128)(2,1)}, bf16[1,1024,128]{2,1,0:T(8,128)(2,1)S(1)}, u32[]{:S(2)}, u32[]{:S(2)}) collective-permute-start(bf16[1,1024,128]{2,1,0:T(8,128)(2,1)} %shard_map.113), channel_id=1, source_target_pairs={{0,8},{8,0},{16,24},{24,16},{32,40},{40,32},{48,56},{56,48},{64,72... | collective-permute-start | bytes 786440 | tf_op jit(solution)/shard_map/ppermute | solution.py:351
  14.6 4.0 %collective-permute-start.1 = (bf16[16,1024]{1,0:T(8,128)(2,1)S(1)}, bf16[16,1024]{1,0:T(8,128)(2,1)S(1)}, u32[]{:S(2)}, u32[]{:S(2)}) collective-permute-start(bf16[16,1024]{1,0:T(8,128)(2,1)S(1)} %get-tuple-element.28), channel_id=1, source_target_pairs={{0,8},{8,0},{16,24},{24,16},{32,40},{40,32},{48,56},{56,48},{64,72... | collective-permute-start | bytes 98312 | tf_op jit(solution)/shard_map/ppermute | solution.py:351
  19.2 40.6 %collective-permute-start.5 = (bf16[7,1024,128]{2,1,0:T(8,128)(2,1)S(1)}, bf16[7,1024,128]{2,1,0:T(8,128)(2,1)S(1)}, u32[]{:S(2)}, u32[]{:S(2)}) collective-permute-start(bf16[7,1024,128]{2,1,0:T(8,128)(2,1)S(1)} %get-tuple-element.34), channel_id=1, source_target_pairs={{0,8},{8,0},{16,24},{24,16},{32,40},{40,32},{48,56},{56,48},{64,72... | collective-permute-start | bytes 5505032 | tf_op jit(solution)/shard_map/ppermute | solution.py:351
  19.8 15.3 %collective-permute-start.9 = (bf16[1040,128]{1,0:T(8,128)(2,1)S(1)}, bf16[1040,128]{1,0:T(8,128)(2,1)S(1)}, u32[]{:S(2)}, u32[]{:S(2)}) collective-permute-start(bf16[1040,128]{1,0:T(8,128)(2,1)S(1)} %collective-permute-done.3.refs_2_.w1), channel_id=1, source_target_pairs={{0,64},{8,72},{16,80},{24,88},{32,96},{40,104},{48,112},{56,120},{... | collective-permute-start | bytes 798728 | tf_op jit(solution)/shard_map/ppermute | solution.py:403
  21.3 7.8 %collective-permute-start.6 = (bf16[8,1024]{1,0:T(8,128)(2,1)S(1)}, bf16[8,1024]{1,0:T(8,128)(2,1)S(1)}, u32[]{:S(2)}, u32[]{:S(2)}) collective-permute-start(bf16[8,1024]{1,0:T(8,128)(2,1)S(1)} %get-tuple-element.40.own_ref), channel_id=1, source_target_pairs={{0,56},{8,16},{16,8},{24,32},{32,24},{40,48},{48,40},{56,0},{64,12... | collective-permute-start | bytes 49160 | tf_op jit(solution)/shard_map/ppermute | solution.py:372
  26.7 4.7 %collective-permute-start.7 = (bf16[8,1024]{1,0:T(8,128)(2,1)S(1)}, bf16[8,1024]{1,0:T(8,128)(2,1)S(1)}, u32[]{:S(2)}, u32[]{:S(2)}) collective-permute-start(bf16[8,1024]{1,0:T(8,128)(2,1)S(1)} %get-tuple-element.40.own_ref), channel_id=1, source_target_pairs={{0,48},{8,24},{16,0},{24,40},{32,16},{40,56},{48,32},{56,8},{64,11... | collective-permute-start | bytes 49160 | tf_op jit(solution)/shard_map/ppermute | solution.py:372
  28.2 6.9 %collective-permute-start.8 = (bf16[8,1024]{1,0:T(8,128)(2,1)S(1)}, bf16[8,1024]{1,0:T(8,128)(2,1)S(1)}, u32[]{:S(2)}, u32[]{:S(2)}) collective-permute-start(bf16[8,1024]{1,0:T(8,128)(2,1)S(1)} %get-tuple-element.40.own_ref), channel_id=1, source_target_pairs={{0,40},{8,32},{16,56},{24,48},{32,8},{40,0},{48,24},{56,16},{64,10... | collective-permute-start | bytes 49160 | tf_op jit(solution)/shard_map/ppermute | solution.py:372
  48.0 5.2 %collective-permute-start.10 = (f32[4,8,128]{2,1,0:T(8,128)S(1)}, f32[4,8,128]{2,1,0:T(8,128)S(1)}, u32[]{:S(2)}, u32[]{:S(2)}) collective-permute-start(f32[4,8,128]{2,1,0:T(8,128)S(1)} %shard_map.118.own_ref), channel_id=1, source_target_pairs={{0,56},{8,16},{16,8},{24,32},{32,24},{40,48},{48,40},{56,0},{64,12... | collective-permute-start | bytes 49160 | tf_op jit(solution)/shard_map/ppermute | solution.py:372
  48.1 5.1 %collective-permute-start.11 = (f32[4,8,128]{2,1,0:T(8,128)S(1)}, f32[4,8,128]{2,1,0:T(8,128)S(1)}, u32[]{:S(2)}, u32[]{:S(2)}) collective-permute-start(f32[4,8,128]{2,1,0:T(8,128)S(1)} %shard_map.118.own_ref), channel_id=1, source_target_pairs={{0,48},{8,24},{16,0},{24,40},{32,16},{40,56},{48,32},{56,8},{64,11... | collective-permute-start | bytes 49160 | tf_op jit(solution)/shard_map/ppermute | solution.py:372
  53.2 8.1 %collective-permute-start.12 = (f32[4,8,128]{2,1,0:T(8,128)S(1)}, f32[4,8,128]{2,1,0:T(8,128)S(1)}, u32[]{:S(2)}, u32[]{:S(2)}) collective-permute-start(f32[4,8,128]{2,1,0:T(8,128)S(1)} %get-tuple-element.42), channel_id=1, source_target_pairs={{0,48},{8,24},{16,0},{24,40},{32,16},{40,56},{48,32},{56,8},{64,11... | collective-permute-start | bytes 49160 | tf_op jit(solution)/shard_map/ppermute | solution.py:372
  55.5 6.9 %collective-permute-start.13 = (f32[4,8,128]{2,1,0:T(8,128)S(1)}, f32[4,8,128]{2,1,0:T(8,128)S(1)}, u32[]{:S(2)}, u32[]{:S(2)}) collective-permute-start(f32[4,8,128]{2,1,0:T(8,128)S(1)} %get-tuple-element.41.own_ref), channel_id=1, source_target_pairs={{0,40},{8,32},{16,56},{24,48},{32,8},{40,0},{48,24},{56,16},{64,10... | collective-permute-start | bytes 49160 | tf_op jit(solution)/shard_map/ppermute | solution.py:372

commit v7 on v6

--- a/solution.py
+++ b/solution.py
@@ -10,6 +10,7 @@
 
 D_GEN = 8192
 MOST = 4
+PARTS = 4
 BD = 8
 CACHE = 1024
 HD = 128
@@ -49,7 +50,7 @@
 
 
 def pack_kernel(
-    par_ref, fin_ref, cache_ref, w_ref, head_ref, q_ref, kv_ref, msg_ref, a_ref, wext_ref, sems, wsem
+    par_ref, fin_ref, cache_ref, w_ref, head_ref, q_ref, kv_ref, msg_ref, a_ref, wext_ref, sem, wsem
 ):
     me = lax.axis_index("dp")
     half = lax.rem(me, 2)
@@ -59,11 +60,10 @@
     wcopy.start()
     _, beams, total = needed(locals_of(par_ref, start, half))
     early = a_ref.shape[0]
-    for u in range(early):
-
-        @pl.when(u // 2 < total)
-        def _():
-            pltpu.make_async_copy(cache_ref.at[beams[u // 2], u % 2], a_ref.at[u], sems.at[u]).start()
+
+    @pl.when(total > 0)
+    def _():
+        pltpu.make_async_copy(cache_ref.at[beams[0], pl.ds(0, early)], a_ref, sem).start()
 
     wext_ref[pl.ds(rows, 16), :] = jnp.broadcast_to(head_ref[...].astype(F32), (16, HD)).astype(BF16)
     for s in range(BD):
@@ -73,11 +73,10 @@
             [q_ref[1, s].astype(F32), step, flag, jnp.zeros((5, HD), F32)], axis=0
         ).astype(BF16)
     wcopy.wait()
-    for u in range(early):
-
-        @pl.when(u // 2 < total)
-        def _():
-            pltpu.make_async_copy(cache_ref.at[0, 0], a_ref.at[u], sems.at[u]).wait()
+
+    @pl.when(total > 0)
+    def _():
+        pltpu.make_async_copy(cache_ref.at[0, pl.ds(0, early)], a_ref, sem).wait()
 
 
 OWN = BD * GH
@@ -98,14 +97,21 @@
     scaling = math.log2(math.e) / math.sqrt(HD)
     their_local = locals_of(par_ref, theirs, half)
     _, beams, send_total = needed(their_local)
-    skip = 2 * MOST - late_ref.shape[0]
-    for u in range(skip, 2 * MOST):
-
-        @pl.when(u // 2 < send_total)
-        def _():
-            pltpu.make_async_copy(
-                cache_ref.at[beams[u // 2], u % 2], late_ref.at[u - skip], sendsem.at[u]
-            ).start()
+    skip = MOST * PARTS - late_ref.shape[0]
+
+    def late_copy(r):
+        low = skip if r == 0 else 0
+        return pltpu.make_async_copy(
+            cache_ref.at[beams[r], pl.ds(low, PARTS - low)],
+            late_ref.at[pl.ds(r * PARTS + low - skip, PARTS - low)],
+            sendsem.at[r],
+        )
+
+    for r in range(MOST):
+
+        @pl.when(r < send_total)
+        def _():
+            late_copy(r).start()
 
     own_local = locals_of(par_ref, mine, half)
     for s in range(BD):
@@ -154,7 +160,10 @@
     def match(b):
         q = jnp.concatenate([q2, q1s[b]], axis=0)
         return q, lax.dot_general(
-            q, cache_ref[b, 0], (((1,), (1,)), ((), ())), preferred_element_type=F32
+            q,
+            cache_ref[b, 0 : PARTS // 2].reshape(CACHE, HD),
+            (((1,), (1,)), ((), ())),
+            preferred_element_type=F32,
         )
 
     def weigh(b, q, logits):
@@ -171,7 +180,11 @@
         return p, p0, p1, inv, step
 
     def mix(b, p, p0, p1, inv, step):
-        mixed = jnp.dot((p * inv).astype(BF16), cache_ref[b, 1], preferred_element_type=F32)
+        mixed = jnp.dot(
+            (p * inv).astype(BF16),
+            cache_ref[b, PARTS // 2 : PARTS].reshape(CACHE, HD),
+            preferred_element_type=F32,
+        )
         mixed = mixed + (p0 * inv).astype(BF16).astype(F32) * step[1:2]
         mixed = mixed + (p1 * inv).astype(BF16).astype(F32) * v1s[...]
         fscr[b * GH : (b + 1) * GH, :] = mixed[ALL : ALL + GH]
@@ -225,11 +238,11 @@
         for b in range(BD):
             slot = jnp.where(cross_local[s] == b, ranks[b], slot)
         meta_ref[s : s + 1, :] = jnp.full((1, HD), slot, jnp.int32)
-    for u in range(skip, 2 * MOST):
-
-        @pl.when(u // 2 < send_total)
-        def _():
-            pltpu.make_async_copy(cache_ref.at[0, 0], late_ref.at[0], sendsem.at[u]).wait()
+    for r in range(MOST):
+
+        @pl.when(r < send_total)
+        def _():
+            late_copy(r).wait()
 
     for s in range(BD):
 
@@ -242,26 +255,27 @@
     token_ref, newc_ref, sems = refs[-3:]
     token_ref[...] = pick_ref[...]
     count = recv_ref.shape[0]
-    waits = []
-    for s in range(BD):
-        slot = meta_ref[s : s + 1, :][0, 0]
-        for half in range(2):
-            unit = 2 * slot + half - first
-            fits = (slot >= 0) & (unit >= 0) & (unit < count)
-            waits.append(fits)
-
-            @pl.when(fits)
-            def _():
-                pltpu.make_async_copy(
-                    recv_ref.at[jnp.clip(unit, 0, count - 1)], newc_ref.at[s, half], sems.at[s, half]
-                ).start()
-
-    for s in range(BD):
-        for half in range(2):
-
-            @pl.when(waits[2 * s + half])
-            def _():
-                pltpu.make_async_copy(recv_ref.at[0], newc_ref.at[s, half], sems.at[s, half]).wait()
+    copies = []
+    for s in range(BD):
+        rank = meta_ref[s : s + 1, :][0, 0]
+        part = min(count, PARTS - first)
+        copies.append(
+            (rank == 0, recv_ref.at[pl.ds(0, part)], newc_ref.at[s, pl.ds(first, part)], sems.at[s])
+        )
+        if count > PARTS:
+            at = jnp.clip(rank * PARTS - first, 0, count - PARTS)
+            copies.append((rank > 0, recv_ref.at[pl.ds(at, PARTS)], newc_ref.at[s], sems.at[s]))
+    for fits, source, target, sem in copies:
+
+        @pl.when(fits)
+        def _():
+            pltpu.make_async_copy(source, target, sem).start()
+
+    for fits, source, target, sem in copies:
+
+        @pl.when(fits)
+        def _():
+            pltpu.make_async_copy(source, target, sem).wait()
 
 
 def gate_kernel(*refs):
@@ -269,7 +283,7 @@
 
 
 def join_kernel(own_ref, rows_ref, swap_ref, *refs):
-    second_ref, full_ref = refs[-3:-1]
+    second_ref, full_ref = refs
     second_ref[...] = own_ref[...] + swap_ref[0:BD, :]
     full_ref[...] = rows_ref[...] + swap_ref[BD : 2 * BD, :]
 
@@ -357,7 +371,7 @@
         [shape(pick.shape, F32), shape(newc.shape, BF16)],
         [VM, VM, VM, HB],
         [VM, HB],
-        [pltpu.SemaphoreType.DMA((BD, 2))],
+        [pltpu.SemaphoreType.DMA((BD,))],
         aliases={3: 1},
         limit=16,
     )(meta, recv, pick, newc)
@@ -372,23 +386,23 @@
     return lax.ppermute(array, "dp", pairs)
 
 
-EARLY = 1
+EARLY = 2
 
 
 def per_device(nx, nz, cache_kv, lengths, step_kv, queries, parents, finished, reward_in, reward_head):
     ndp = nx * nz
     nt = lax.axis_size("tensor")
-    cache = cache_kv.reshape(BD, 2, CACHE, HD)
+    cache = cache_kv.reshape(BD, PARTS, 2 * CACHE // PARTS, HD)
     kv = step_kv.reshape(2, BD, 2, HD)
     depth = reward_in.shape[0]
-    part_a = shape((EARLY, CACHE, HD), BF16)
-    part_b = shape((2 * MOST - EARLY, CACHE, HD), BF16)
+    part_a = shape((EARLY,) + cache.shape[2:], BF16)
+    part_b = shape((MOST * PARTS - EARLY,) + cache.shape[2:], BF16)
     msg, early, wext = call(
         pack_kernel,
         [shape((BD, 16, HD), BF16), part_a, shape((depth + 16, HD), BF16)],
         [SM, SM, HB, HB, VM, VM, VM],
         [VM, VM, VM],
-        [pltpu.SemaphoreType.DMA((EARLY,)), pltpu.SemaphoreType.DMA],
+        [pltpu.SemaphoreType.DMA, pltpu.SemaphoreType.DMA],
         limit=57,
         cost=1000000,
     )(parents, finished, cache, reward_in, reward_head.reshape(1, HD), queries, kv)
@@ -411,7 +425,7 @@
             shape((BD, HD), jnp.int32),
             shape((BD, HD), F32),
             part_b,
-            shape((BD, 2, CACHE, HD), BF16),
+            shape(cache.shape, BF16),
         ],
         [SM, SM, SM, VM, VM, VM, VM],
         [VM] * 7 + [HB],
@@ -426,19 +440,22 @@
             VM((2 * BD, GH * HD), F32),
             VM((BD, GH * HD), F32),
             pltpu.SemaphoreType.DMA((BD,)),
-            pltpu.SemaphoreType.DMA((2 * MOST,)),
+            pltpu.SemaphoreType.DMA((MOST,)),
         ],
         cost=20000000,
         limit=32,
     )(parents, lengths, finished, cache, queries, kv, recv_msg)
-    second_out, rows, late = call(
+    recv_swap = swap(to_swap)
+    (late,) = call(
+        gate_kernel, [part_b], [pl.ANY] * 5, [pl.ANY], aliases={0: 0}, limit=16, cost=1000
+    )(late, recv_swap, recv_early, others[0], others[2])
+    second_out, rows = call(
         join_kernel,
-        [shape(own_out.shape, BF16), shape(rows.shape, BF16), part_b],
-        [VM] * 3 + [pl.ANY] * 4,
-        [VM, VM, pl.ANY],
-        aliases={3: 2},
+        [shape(own_out.shape, BF16), shape(rows.shape, BF16)],
+        [VM] * 3,
+        [VM, VM],
         limit=16,
-    )(own_out, rows, swap(to_swap), late, recv_early, others[0], others[2])
+    )(own_out, rows, recv_swap)
     recv_late = swap(late)
     (partial,) = call(
         hidden_kernel, [shape((nt, nz // 2 * BD, 5 * HD), BF16)], [VM] * 8, [VM], limit=16

time: 63.2 us -> 63.3 us (level)
    ppermute x7, waiting for transfers between devices: 10.7 us -> 11.4 us  [away(): return lax.ppermute(array, 'dp', pairs)]
  transfers between devices with their start and end apart: 14 -> 14, of which waited for: 7 -> 6; matrix products, arithmetic and copies ran while one was open for 0% -> 0% of each run, Pallas kernels for 12% -> 12%
where the time goes in v7:
time: 63.3 us; the launch traced here: 63.1 us
  starting transfers between devices  23 us (36%)
  waiting for transfers between devices  15.1 us (24%)
  blocking collectives  12.6 us (20%)
  Pallas kernels  11.6 us (18%)
  between operations  0.8 us (1%)
    ppermute x7, starting transfers between devices, away(): return lax.ppermute(array, 'dp', pairs)  14.4 us
    all_to_all x1, blocking collectives, per_device(): partials = lax.all_to_all(partial, 'tensor', 0, 0, tiled=True)  12.6 us
    ppermute x7, waiting for transfers between devices, away(): return lax.ppermute(array, 'dp', pairs)  11.4 us
    ppermute x4, starting transfers between devices, swap(): lax.ppermute(array, 'dp', [(i, i ^ 1) for i in range(lax.axis_size('dp'))])  5.06 us
    pallas_call x1, Pallas kernels, per_device(): call(attend_kernel, [shape((BD, GH * HD), BF16), shape((BD, GH * HD), BF1...  4.54 us
    ppermute x4, waiting for transfers between devices, swap(): lax.ppermute(array, 'dp', [(i, i ^ 1) for i in range(lax.axis_size('dp'))])  3.64 us
    pallas_call x1, Pallas kernels, per_device(): call(pack_kernel, [shape((BD, 16, HD), BF16), part_a, shape((depth + 16,...  3.16 us
    pallas_call x2, Pallas kernels, place(): call(functools.partial(place_kernel, first), [shape(pick.shape, F32), sha...  2.17 us
  transfers between devices with their start and end apart: 14, of which 6 were waited for; matrix products, arithmetic and copies ran while one was open for 0% of the time, Pallas kernels for 12%

profile of v7, /device:TPU:2, one launch (start us, length us, event | category | flops | bytes accessed | tf_op | source)
XLA Modules:
  0.0 63.1 jit_solution(8682840975469797517)
XLA Ops:
  0.7 3.2 %shard_map.111 = (bf16[8,16,128]{2,1,0:T(8,128)(2,1)}, bf16[2,512,128]{2,1,0:T(8,128)(2,1)}, bf16[1040,128]{1,0:T(8,128)(2,1)}) custom-call(s32[256]{0:T(256)} %par_ref.3, s32[8]{0:T(128)} %fin_ref.3, bf16[8,4,512,128]{3,2,1,0:T(8,128)(2,1)} %bitcast.6, bf16[1024,128]{1,0:T(8,128)(2,1)} %w_ref.1, bf16[1,128]{1,0:T(2,128)(2,1)} %bitcast.11, ...), custom_call_target="tpu_custom_call" | custom-call | flops 1000000 | bytes 1000000 | tf_op jit(solution)/shard_map/pallas_call | solution.py:400
  3.9 2.0 %collective-permute-start = (bf16[8,16,128]{2,1,0:T(8,128)(2,1)}, bf16[8,16,128]{2,1,0:T(8,128)(2,1)S(1)}, u32[]{:S(2)}, u32[]{:S(2)}) collective-permute-start(bf16[8,16,128]{2,1,0:T(8,128)(2,1)} %get-tuple-element.23), channel_id=1, source_target_pairs={{0,8},{8,0},{16,24},{24,16},{32,40},{40,32},{48,56},{56,48},{64,72... | collective-permute-start | bytes 98312 | tf_op jit(solution)/shard_map/ppermute | solution.py:365
  5.9 1.4 %collective-permute-start.3 = (bf16[1040,128]{1,0:T(8,128)(2,1)}, bf16[1040,128]{1,0:T(8,128)(2,1)S(1)}, u32[]{:S(2)}, u32[]{:S(2)}) collective-permute-start(bf16[1040,128]{1,0:T(8,128)(2,1)} %get-tuple-element.32.w0), channel_id=1, source_target_pairs={{0,64},{8,72},{16,80},{24,88},{32,96},{40,104},{48,112},{56,120},{... | collective-permute-start | bytes 798728 | tf_op jit(solution)/shard_map/ppermute | solution.py:415
  7.3 0.6 collective-permute-start.4
  8.1 1.9 %collective-permute-start.2 = (bf16[2,512,128]{2,1,0:T(8,128)(2,1)}, bf16[2,512,128]{2,1,0:T(8,128)(2,1)S(1)}, u32[]{:S(2)}, u32[]{:S(2)}) collective-permute-start(bf16[2,512,128]{2,1,0:T(8,128)(2,1)} %shard_map.114), channel_id=1, source_target_pairs={{0,8},{8,0},{16,24},{24,16},{32,40},{40,32},{48,56},{56,48},{64,72... | collective-permute-start | bytes 786440 | tf_op jit(solution)/shard_map/ppermute | solution.py:365
  10.0 4.5 %shard_map.112 = (bf16[8,1024]{1,0:T(8,128)(2,1)}, bf16[8,1024]{1,0:T(8,128)(2,1)S(1)}, bf16[16,1024]{1,0:T(8,128)(2,1)S(1)}, bf16[8,1024]{1,0:T(8,128)(2,1)S(1)...) custom-call(s32[256]{0:T(256)S(1)} %copy-done.4, ...), custom_call_target="tpu_custom_call" | custom-call | flops 20000000 | bytes 20000000 | tf_op jit(solution)/shard_map/pallas_call | solution.py:418
  14.6 0.6 collective-permute-start.1
  15.2 3.5 %collective-permute-done.1.swap_ref.refs_1_ = bf16[16,1024]{1,0:T(8,128)(2,1)S(1)} collective-permute-done((bf16[16,1024]{1,0:T(8,128)(2,1)S(1)}, bf16[16,1024]{1,0:T(8,128)(2,1)S(1)}, u32[]{:S(2)}, u32[]{:S(2)}) %collective-permute-start.1) | collective-permute-done | bytes 32800 | tf_op jit(solution)/shard_map/ppermute | solution.py:365
  19.2 1.5 %collective-permute-start.9 = (bf16[1040,128]{1,0:T(8,128)(2,1)S(1)}, bf16[1040,128]{1,0:T(8,128)(2,1)S(1)}, u32[]{:S(2)}, u32[]{:S(2)}) collective-permute-start(bf16[1040,128]{1,0:T(8,128)(2,1)S(1)} %collective-permute-done.3.refs_3_.w1), channel_id=1, source_target_pairs={{0,64},{8,72},{16,80},{24,88},{32,96},{40,104},{48,112},{56,120},{... | collective-permute-start | bytes 798728 | tf_op jit(solution)/shard_map/ppermute | solution.py:417
  20.7 0.6 shard_map.113
  21.3 5.5 %collective-permute-start.6 = (bf16[8,1024]{1,0:T(8,128)(2,1)S(1)}, bf16[8,1024]{1,0:T(8,128)(2,1)S(1)}, u32[]{:S(2)}, u32[]{:S(2)}) collective-permute-start(bf16[8,1024]{1,0:T(8,128)(2,1)S(1)} %get-tuple-element.38.own_ref), channel_id=1, source_target_pairs={{0,56},{8,16},{16,8},{24,32},{32,24},{40,48},{48,40},{56,0},{64,12... | collective-permute-start | bytes 49160 | tf_op jit(solution)/shard_map/ppermute | solution.py:386
  26.8 1.7 %collective-permute-start.7 = (bf16[8,1024]{1,0:T(8,128)(2,1)S(1)}, bf16[8,1024]{1,0:T(8,128)(2,1)S(1)}, u32[]{:S(2)}, u32[]{:S(2)}) collective-permute-start(bf16[8,1024]{1,0:T(8,128)(2,1)S(1)} %get-tuple-element.38.own_ref), channel_id=1, source_target_pairs={{0,48},{8,24},{16,0},{24,40},{32,16},{40,56},{48,32},{56,8},{64,11... | collective-permute-start | bytes 49160 | tf_op jit(solution)/shard_map/ppermute | solution.py:386
  28.5 0.7 %collective-permute-start.8 = (bf16[8,1024]{1,0:T(8,128)(2,1)S(1)}, bf16[8,1024]{1,0:T(8,128)(2,1)S(1)}, u32[]{:S(2)}, u32[]{:S(2)}) collective-permute-start(bf16[8,1024]{1,0:T(8,128)(2,1)S(1)} %get-tuple-element.38.own_ref), channel_id=1, source_target_pairs={{0,40},{8,32},{16,56},{24,48},{32,8},{40,0},{48,24},{56,16},{64,10... | collective-permute-start | bytes 49160 | tf_op jit(solution)/shard_map/ppermute | solution.py:386
  29.2 2.4 %collective-permute-done.7.r2 = bf16[8,1024]{1,0:T(8,128)(2,1)S(1)} collective-permute-done((bf16[8,1024]{1,0:T(8,128)(2,1)S(1)}, bf16[8,1024]{1,0:T(8,128)(2,1)S(1)}, u32[]{:S(2)}, u32[]{:S(2)}) %collective-permute-start.7) | collective-permute-done | bytes 16416 | tf_op jit(solution)/shard_map/ppermute | solution.py:386
  31.6 3.8 %collective-permute-done.8.r3 = bf16[8,1024]{1,0:T(8,128)(2,1)S(1)} collective-permute-done((bf16[8,1024]{1,0:T(8,128)(2,1)S(1)}, bf16[8,1024]{1,0:T(8,128)(2,1)S(1)}, u32[]{:S(2)}, u32[]{:S(2)}) %collective-permute-start.8) | collective-permute-done | bytes 16416 | tf_op jit(solution)/shard_map/ppermute | solution.py:386
  35.7 12.6 %all_to_all.5.hid_ref = bf16[8,32,640]{2,1,0:T(8,128)(2,1)S(1)} all-to-all(bf16[8,32,640]{2,1,0:T(8,128)(2,1)S(1)} %shard_map.118), channel_id=1, replica_groups=mesh['dp'=32,'tensor'=8] {'tensor'}, dimensions={0} | all-to-all | bytes 655360 | tf_op jit(solution)/shard_map/all_to_all | solution.py:463
  48.6 1.0 %collective-permute-start.11 = (f32[4,8,128]{2,1,0:T(8,128)S(1)}, f32[4,8,128]{2,1,0:T(8,128)S(1)}, u32[]{:S(2)}, u32[]{:S(2)}) collective-permute-start(f32[4,8,128]{2,1,0:T(8,128)S(1)} %shard_map.119.own_ref), channel_id=1, source_target_pairs={{0,48},{8,24},{16,0},{24,40},{32,16},{40,56},{48,32},{56,8},{64,11... | collective-permute-start | bytes 49160 | tf_op jit(solution)/shard_map/ppermute | solution.py:386
  49.6 3.9 %collective-permute-done.10.near_ref = f32[4,8,128]{2,1,0:T(8,128)S(1)} collective-permute-done((f32[4,8,128]{2,1,0:T(8,128)S(1)}, f32[4,8,128]{2,1,0:T(8,128)S(1)}, u32[]{:S(2)}, u32[]{:S(2)}) %collective-permute-start.10) | collective-permute-done | bytes 16416 | tf_op jit(solution)/shard_map/ppermute | solution.py:386
  53.6 2.0 %collective-permute-start.12 = (f32[4,8,128]{2,1,0:T(8,128)S(1)}, f32[4,8,128]{2,1,0:T(8,128)S(1)}, u32[]{:S(2)}, u32[]{:S(2)}) collective-permute-start(f32[4,8,128]{2,1,0:T(8,128)S(1)} %get-tuple-element.40), channel_id=1, source_target_pairs={{0,48},{8,24},{16,0},{24,40},{32,16},{40,56},{48,32},{56,8},{64,11... | collective-permute-start | bytes 49160 | tf_op jit(solution)/shard_map/ppermute | solution.py:386
  55.6 3.4 %collective-permute-start.13 = (f32[4,8,128]{2,1,0:T(8,128)S(1)}, f32[4,8,128]{2,1,0:T(8,128)S(1)}, u32[]{:S(2)}, u32[]{:S(2)}) collective-permute-start(f32[4,8,128]{2,1,0:T(8,128)S(1)} %get-tuple-element.39.own_ref), channel_id=1, source_target_pairs={{0,40},{8,32},{16,56},{24,48},{32,8},{40,0},{48,24},{56,16},{64,10... | collective-permute-start | bytes 49160 | tf_op jit(solution)/shard_map/ppermute | solution.py:386
  59.0 0.8 %shard_map.116 = (f32[8,128]{1,0:T(8,128)S(1)}, bf16[8,4,512,128]{3,2,1,0:T(8,128)(2,1)}) custom-call(s32[8,128]{1,0:T(8,128)S(1)} %get-tuple-element.29.meta_ref, bf16[2,512,128]{2,1,0:T(8,128)(2,1)S(1)} %collective-permute-done.2.refs_2_.recv_ref, f32[8,128]{1,0:T(8,128)S(1)} %get-tuple-element.33.pick_ref, ...), custom_call_target="tpu_custom_call", output_to_operand_aliasing={{1}: (3, {})} | custom-call | flops 1000000 | bytes 1000000 | tf_op jit(solution)/shard_map/pallas_call | solution.py:369
  59.8 1.4 %shard_map.117 = (f32[8,128]{1,0:T(8,128)S(1)}, bf16[8,4,512,128]{3,2,1,0:T(8,128)(2,1)}) custom-call(s32[8,128]{1,0:T(8,128)S(1)} %get-tuple-element.29.meta_ref, bf16[14,512,128]{2,1,0:T(8,128)(2,1)S(1)} %collective-permute-done.5.recv_ref, f32[8,128]{1,0:T(8,128)S(1)} %get-tuple-element.35.pick_ref, ...), custom_call_target="tpu_custom_call", output_to_operand_aliasing={{1}: (3, {})} | custom-call | flops 1000000 | bytes 1000000 | tf_op jit(solution)/shard_map/pallas_call | solution.py:369
  61.2 1.3 %collective-permute-done.13.three_ref = f32[4,8,128]{2,1,0:T(8,128)S(1)} collective-permute-done((f32[4,8,128]{2,1,0:T(8,128)S(1)}, f32[4,8,128]{2,1,0:T(8,128)S(1)}, u32[]{:S(2)}, u32[]{:S(2)}) %collective-permute-start.13) | collective-permute-done | bytes 16416 | tf_op jit(solution)/shard_map/ppermute | solution.py:386
  62.4 0.6 %shard_map.121 = f32[8]{0:T(128)} custom-call(f32[8,128]{1,0:T(8,128)S(1)} %get-tuple-element.37.pick_ref, f32[4,8,128]{2,1,0:T(8,128)S(1)} %get-tuple-element.39.own_ref, f32[4,8,128]{2,1,0:T(8,128)S(1)} %collective-permute-done.12.two_ref, f32[4,8,128]{2,1,0:T(8,128)S(1)} %collective-permute-done.13.three_ref), custom_call_target="tpu_custom_call" | custom-call | flops 1000000 | bytes 1000000 | tf_op jit(solution)/shard_map/pallas_call | solution.py:472
  (30 shorter events, 1.4 us)
Async XLA Ops:
  0.6 9.4 %copy-start = (bf16[8,2,1024,1,128]{4,2,3,1,0:T(8,128)(2,1)S(1)}, bf16[8,2,1024,1,128]{4,2,3,1,0:T(8,128)(2,1)}, u32[]{:S(2)}) copy-start(bf16[8,2,1024,1,128]{4,2,3,1,0:T(8,128)(2,1)} %param.8) | copy-start | bytes 12582916
  0.6 9.4 %copy-start.3 = (bf16[2,8,2,1,128]{4,2,3,1,0:T(2,128)(2,1)S(1)}, bf16[2,8,2,1,128]{4,2,3,1,0:T(2,128)(2,1)}, u32[]{:S(2)}) copy-start(bf16[2,8,2,1,128]{4,2,3,1,0:T(2,128)(2,1)} %param.10) | copy-start | bytes 24580
  0.7 9.3 %copy-start.2 = (bf16[2,8,8,128]{3,2,1,0:T(8,128)(2,1)S(1)}, bf16[2,8,8,128]{3,2,1,0:T(8,128)(2,1)}, u32[]{:S(2)}) copy-start(bf16[2,8,8,128]{3,2,1,0:T(8,128)(2,1)} %q_ref.3) | copy-start | bytes 98308
  0.7 9.3 %copy-start.4 = (s32[256]{0:T(256)S(1)}, s32[256]{0:T(256)}, u32[]{:S(2)}) copy-start(s32[256]{0:T(256)} %par_ref.3) | copy-start | bytes 3076
  0.7 9.3 %copy-start.5 = (s32[8]{0:T(128)S(1)}, s32[8]{0:T(128)}, u32[]{:S(2)}) copy-start(s32[8]{0:T(128)} %fin_ref.3) | copy-start | bytes 100
  0.7 9.3 %copy-start.6 = (s32[256]{0:T(256)S(1)}, s32[256]{0:T(256)}, u32[]{:S(2)}) copy-start(s32[256]{0:T(256)} %len_ref.1) | copy-start | bytes 3076
  3.9 4.2 %collective-permute-start = (bf16[8,16,128]{2,1,0:T(8,128)(2,1)}, bf16[8,16,128]{2,1,0:T(8,128)(2,1)S(1)}, u32[]{:S(2)}, u32[]{:S(2)}) collective-permute-start(bf16[8,16,128]{2,1,0:T(8,128)(2,1)} %get-tuple-element.23), channel_id=1, source_target_pairs={{0,8},{8,0},{16,24},{24,16},{32,40},{40,32},{48,56},{56,48},{64,72... | collective-permute-start | bytes 98312 | tf_op jit(solution)/shard_map/ppermute | solution.py:365
  5.9 12.8 %collective-permute-start.3 = (bf16[1040,128]{1,0:T(8,128)(2,1)}, bf16[1040,128]{1,0:T(8,128)(2,1)S(1)}, u32[]{:S(2)}, u32[]{:S(2)}) collective-permute-start(bf16[1040,128]{1,0:T(8,128)(2,1)} %get-tuple-element.32.w0), channel_id=1, source_target_pairs={{0,64},{8,72},{16,80},{24,88},{32,96},{40,104},{48,112},{56,120},{... | collective-permute-start | bytes 798728 | tf_op jit(solution)/shard_map/ppermute | solution.py:415
  7.3 11.3 %collective-permute-start.4 = (bf16[1040,128]{1,0:T(8,128)(2,1)}, bf16[1040,128]{1,0:T(8,128)(2,1)S(1)}, u32[]{:S(2)}, u32[]{:S(2)}) collective-permute-start(bf16[1040,128]{1,0:T(8,128)(2,1)} %get-tuple-element.32.w0), channel_id=1, source_target_pairs={{0,192},{8,200},{16,208},{24,216},{32,224},{40,232},{48,240},{56,2... | collective-permute-start | bytes 798728 | tf_op jit(solution)/shard_map/ppermute | solution.py:415
  8.1 27.3 %copy-start.1 = (bf16[1040,128]{1,0:T(8,128)(2,1)S(1)}, bf16[1040,128]{1,0:T(8,128)(2,1)}, u32[]{:S(2)}) copy-start(bf16[1040,128]{1,0:T(8,128)(2,1)} %get-tuple-element.32.w0) | copy-start | bytes 798724
  8.1 10.6 %collective-permute-start.2 = (bf16[2,512,128]{2,1,0:T(8,128)(2,1)}, bf16[2,512,128]{2,1,0:T(8,128)(2,1)S(1)}, u32[]{:S(2)}, u32[]{:S(2)}) collective-permute-start(bf16[2,512,128]{2,1,0:T(8,128)(2,1)} %shard_map.114), channel_id=1, source_target_pairs={{0,8},{8,0},{16,24},{24,16},{32,40},{40,32},{48,56},{56,48},{64,72... | collective-permute-start | bytes 786440 | tf_op jit(solution)/shard_map/ppermute | solution.py:365
  14.6 4.0 %collective-permute-start.1 = (bf16[16,1024]{1,0:T(8,128)(2,1)S(1)}, bf16[16,1024]{1,0:T(8,128)(2,1)S(1)}, u32[]{:S(2)}, u32[]{:S(2)}) collective-permute-start(bf16[16,1024]{1,0:T(8,128)(2,1)S(1)} %get-tuple-element.27), channel_id=1, source_target_pairs={{0,8},{8,0},{16,24},{24,16},{32,40},{40,32},{48,56},{56,48},{64,72... | collective-permute-start | bytes 98312 | tf_op jit(solution)/shard_map/ppermute | solution.py:365
  18.6 41.1 %collective-permute-start.5 = (bf16[14,512,128]{2,1,0:T(8,128)(2,1)S(1)}, bf16[14,512,128]{2,1,0:T(8,128)(2,1)S(1)}, u32[]{:S(2)}, u32[]{:S(2)}) collective-permute-start(bf16[14,512,128]{2,1,0:T(8,128)(2,1)S(1)} %shard_map.115), channel_id=1, source_target_pairs={{0,8},{8,0},{16,24},{24,16},{32,40},{40,32},{48,56},{56,48},{64,72... | collective-permute-start | bytes 5505032 | tf_op jit(solution)/shard_map/ppermute | solution.py:365
  19.2 16.2 %collective-permute-start.9 = (bf16[1040,128]{1,0:T(8,128)(2,1)S(1)}, bf16[1040,128]{1,0:T(8,128)(2,1)S(1)}, u32[]{:S(2)}, u32[]{:S(2)}) collective-permute-start(bf16[1040,128]{1,0:T(8,128)(2,1)S(1)} %collective-permute-done.3.refs_3_.w1), channel_id=1, source_target_pairs={{0,64},{8,72},{16,80},{24,88},{32,96},{40,104},{48,112},{56,120},{... | collective-permute-start | bytes 798728 | tf_op jit(solution)/shard_map/ppermute | solution.py:417
  21.3 7.9 %collective-permute-start.6 = (bf16[8,1024]{1,0:T(8,128)(2,1)S(1)}, bf16[8,1024]{1,0:T(8,128)(2,1)S(1)}, u32[]{:S(2)}, u32[]{:S(2)}) collective-permute-start(bf16[8,1024]{1,0:T(8,128)(2,1)S(1)} %get-tuple-element.38.own_ref), channel_id=1, source_target_pairs={{0,56},{8,16},{16,8},{24,32},{32,24},{40,48},{48,40},{56,0},{64,12... | collective-permute-start | bytes 49160 | tf_op jit(solution)/shard_map/ppermute | solution.py:386
  26.8 4.7 %collective-permute-start.7 = (bf16[8,1024]{1,0:T(8,128)(2,1)S(1)}, bf16[8,1024]{1,0:T(8,128)(2,1)S(1)}, u32[]{:S(2)}, u32[]{:S(2)}) collective-permute-start(bf16[8,1024]{1,0:T(8,128)(2,1)S(1)} %get-tuple-element.38.own_ref), channel_id=1, source_target_pairs={{0,48},{8,24},{16,0},{24,40},{32,16},{40,56},{48,32},{56,8},{64,11... | collective-permute-start | bytes 49160 | tf_op jit(solution)/shard_map/ppermute | solution.py:386
  28.5 6.9 %collective-permute-start.8 = (bf16[8,1024]{1,0:T(8,128)(2,1)S(1)}, bf16[8,1024]{1,0:T(8,128)(2,1)S(1)}, u32[]{:S(2)}, u32[]{:S(2)}) collective-permute-start(bf16[8,1024]{1,0:T(8,128)(2,1)S(1)} %get-tuple-element.38.own_ref), channel_id=1, source_target_pairs={{0,40},{8,32},{16,56},{24,48},{32,8},{40,0},{48,24},{56,16},{64,10... | collective-permute-start | bytes 49160 | tf_op jit(solution)/shard_map/ppermute | solution.py:386
  48.5 5.0 %collective-permute-start.10 = (f32[4,8,128]{2,1,0:T(8,128)S(1)}, f32[4,8,128]{2,1,0:T(8,128)S(1)}, u32[]{:S(2)}, u32[]{:S(2)}) collective-permute-start(f32[4,8,128]{2,1,0:T(8,128)S(1)} %shard_map.119.own_ref), channel_id=1, source_target_pairs={{0,56},{8,16},{16,8},{24,32},{32,24},{40,48},{48,40},{56,0},{64,12... | collective-permute-start | bytes 49160 | tf_op jit(solution)/shard_map/ppermute | solution.py:386
  48.6 4.9 %collective-permute-start.11 = (f32[4,8,128]{2,1,0:T(8,128)S(1)}, f32[4,8,128]{2,1,0:T(8,128)S(1)}, u32[]{:S(2)}, u32[]{:S(2)}) collective-permute-start(f32[4,8,128]{2,1,0:T(8,128)S(1)} %shard_map.119.own_ref), channel_id=1, source_target_pairs={{0,48},{8,24},{16,0},{24,40},{32,16},{40,56},{48,32},{56,8},{64,11... | collective-permute-start | bytes 49160 | tf_op jit(solution)/shard_map/ppermute | solution.py:386
  53.6 7.6 %collective-permute-start.12 = (f32[4,8,128]{2,1,0:T(8,128)S(1)}, f32[4,8,128]{2,1,0:T(8,128)S(1)}, u32[]{:S(2)}, u32[]{:S(2)}) collective-permute-start(f32[4,8,128]{2,1,0:T(8,128)S(1)} %get-tuple-element.40), channel_id=1, source_target_pairs={{0,48},{8,24},{16,0},{24,40},{32,16},{40,56},{48,32},{56,8},{64,11... | collective-permute-start | bytes 49160 | tf_op jit(solution)/shard_map/ppermute | solution.py:386
  55.6 6.9 %collective-permute-start.13 = (f32[4,8,128]{2,1,0:T(8,128)S(1)}, f32[4,8,128]{2,1,0:T(8,128)S(1)}, u32[]{:S(2)}, u32[]{:S(2)}) collective-permute-start(f32[4,8,128]{2,1,0:T(8,128)S(1)} %get-tuple-element.39.own_ref), channel_id=1, source_target_pairs={{0,40},{8,32},{16,56},{24,48},{32,8},{40,0},{48,24},{56,16},{64,10... | collective-permute-start | bytes 49160 | tf_op jit(solution)/shard_map/ppermute | solution.py:386
